TPU v7x, 512 devices: a whole 4x8x8 slice. The times are simulated.
512 devices in a mesh: row: 32 (over x, z), col: 16 (over y, core).
Axes of the slice: x: 4, y: 8, z: 8, core: 2. Of those that a mesh axis runs over, the one named last changes fastest.
Arguments:
- source_points: bfloat16 [32768, 1024], P(('row', 'col')), as said below
- target_points: bfloat16 [16384, 1024], P(('col', 'row')), may hold values from -0.3125 to 0.3125
- source_logmass: float32 [32768], P('row'), may hold values from -5 to 5
- target_logmass: float32 [16384], P('col'), may hold values from -5 to 5
Outputs:
- source_potential: float32 [32768], P('row')
- target_potential: float32 [16384], P('col')
Inputs may be any that keep to these rules, and one draw needn't show every extreme that they name: `source_points`: normally distributed features of scale about 1024 ** -0.5 per entry; rows may differ in scale.
All inputs are finite; a program needn't handle non-finite values.
Results may differ from a plain program's by a relative error of at most 0.0003.
Values may be sent and summed in bfloat16 or wider, within the bound.
No kernel may reach another device: no remote copies, remote signals or barrier semaphores. Data moves between devices by JAX's collectives and lax.ppermute only.
A program may use at most 64 MiB of HBM per device.

v0:
```python
import jax
import jax.numpy as jnp
from jax import lax
from jax.sharding import PartitionSpec as P

ITERS = 3


epsilon = 0.05


def local(source_points, target_points, source_logmass, target_logmass):
    source_full = lax.all_gather(source_points, "col", axis=0, tiled=True)
    source_sq = jnp.sum(jnp.square(source_full.astype(jnp.float32)), axis=1)
    rows = source_full.shape[0]
    columns = target_logmass.shape[0]
    target_full = lax.all_gather(target_points, "row", axis=0, tiled=True)
    target_sq = jnp.sum(jnp.square(target_full.astype(jnp.float32)), axis=1)
    target_potential = jnp.zeros((columns,), jnp.float32)
    source_potential = jnp.zeros((rows,), jnp.float32)
    for step in range(ITERS):
        products = lax.dot_general(
            source_full, target_full, (((1,), (1,)), ((), ())), preferred_element_type=jnp.float32
        )
        cost_tile = source_sq[:, None] + target_sq[None, :] - 2.0 * products
        scores = target_logmass[None, :] + (target_potential[None, :] - cost_tile) / epsilon
        highest = lax.pmax(jnp.max(scores, axis=1), "col")
        totals = lax.psum(jnp.sum(jnp.exp(scores - highest[:, None]), axis=1), "col")
        source_potential = -epsilon * (highest + jnp.log(totals))
        weights = source_logmass[:, None] + (source_potential[:, None] - cost_tile) / epsilon
        largest = lax.pmax(jnp.max(weights, axis=0), "row")
        sums = lax.psum(jnp.sum(jnp.exp(weights - largest[None, :]), axis=0), "row")
        target_potential = -epsilon * (largest + jnp.log(sums))
    return (source_potential, target_potential)


def solution(mesh):
    in_specs = (P(("row", "col"), None), P(("col", "row"), None), P("row"), P("col"))
    out_specs = (P("row"), P("col"))
    return jax.shard_map(local, mesh=mesh, in_specs=in_specs, out_specs=out_specs, check_vma=False)
```

profile of v0, /device:TPU:64, one launch (start us, length us, event | category | flops | bytes accessed | tf_op | source)
XLA Modules:
  0.0 757.5 jit_solution(3312934306368715039)
XLA Ops:
  7.2 0.0 copy-start.2
  7.2 0.0 all-gather.3.cloned.1.call-start
  7.2 0.7 all-gather.3.cloned.1.call-update
  7.9 0.0 all-gather.5.cloned.1.call-start
  8.0 0.7 all-gather.5.cloned.1.call-update
  8.7 47.3 %all-gather.3.cloned.1.call-done = bf16[1024,1024]{1,0:T(8,128)(2,1)} async-done(((bf16[64,1024]{1,0:T(8,128)(2,1)}), bf16[1024,1024]{1,0:T(8,128)(2,1)}) %all-gather.3.cloned.1.call-update) | async-done | bytes 2097168 | tf_op jit(solution)/shard_map/all_gather | solution.py:13
  56.0 0.0 copy-start
  56.0 2.2 multiply_reduce_fusion.1
  58.2 82.8 %all-gather.5.cloned.1.call-done = bf16[1024,1024]{1,0:T(8,128)(2,1)} async-done(((bf16[32,1024]{1,0:T(8,128)(2,1)}), bf16[1024,1024]{1,0:T(8,128)(2,1)}) %all-gather.5.cloned.1.call-update) | async-done | bytes 2097168 | tf_op jit(solution)/shard_map/all_gather | solution.py:17
  141.0 2.1 multiply_reduce_fusion
  143.1 0.0 copy-done.2
  143.1 0.0 copy-done
  143.1 6.1 fusion
  149.2 0.0 copy-start.1
  149.2 23.5 %pmax.42 = f32[1024]{0:T(1024)S(1)} all-reduce(f32[1024]{0:T(1024)S(1)} %get-tuple-element.2), channel_id=1, replica_groups=mesh['row'=32,'col'=16] {'col'}, use_global_device_ids=true, to_apply=%region_3.0 | all-reduce | flops 1024 | bytes 8192 | tf_op jit(solution)/shard_map/pmax | solution.py:27
  172.8 3.3 exponential_reduce_fusion.5
  176.0 23.6 %psum.42 = f32[1024]{0:T(1024)S(1)} all-reduce(f32[1024]{0:T(1024)S(1)} %exponential_reduce_fusion.5), channel_id=1, replica_groups=mesh['row'=32,'col'=16] {'col'}, use_global_device_ids=true, to_apply=%region_5.0 | all-reduce | flops 1024 | bytes 8192 | tf_op jit(solution)/shard_map/psum | solution.py:28
  199.6 0.0 copy-done.1
  199.6 2.8 fusion.1
  202.4 71.1 %pmax.43 = f32[1024]{0:T(1024)S(1)} all-reduce(f32[1024]{0:T(1024)S(1)} %fusion.1), channel_id=1, replica_groups=mesh['row'=32,'col'=16] {'row'}, use_global_device_ids=true, to_apply=%region_7.0 | all-reduce | flops 1024 | bytes 8192 | tf_op jit(solution)/shard_map/pmax | solution.py:31
  273.5 3.2 exponential_reduce_fusion.4
  276.7 72.1 %psum.43 = f32[1024]{0:T(1024)S(1)} all-reduce(f32[1024]{0:T(1024)S(1)} %exponential_reduce_fusion.4), channel_id=1, replica_groups=mesh['row'=32,'col'=16] {'row'}, use_global_device_ids=true, to_apply=%region_9.0 | all-reduce | flops 1024 | bytes 8192 | tf_op jit(solution)/shard_map/psum | solution.py:32
  348.8 2.8 fusion.2
  351.7 23.6 %pmax.44 = f32[1024]{0:T(1024)S(1)} all-reduce(f32[1024]{0:T(1024)S(1)} %fusion.2), channel_id=1, replica_groups=mesh['row'=32,'col'=16] {'col'}, use_global_device_ids=true, to_apply=%region_11.0 | all-reduce | flops 1024 | bytes 8192 | tf_op jit(solution)/shard_map/pmax | solution.py:27
  375.2 3.3 exponential_reduce_fusion.3
  378.5 23.6 %psum.44 = f32[1024]{0:T(1024)S(1)} all-reduce(f32[1024]{0:T(1024)S(1)} %exponential_reduce_fusion.3), channel_id=1, replica_groups=mesh['row'=32,'col'=16] {'col'}, use_global_device_ids=true, to_apply=%region_13.0 | all-reduce | flops 1024 | bytes 8192 | tf_op jit(solution)/shard_map/psum | solution.py:28
  402.1 2.8 fusion.3
  404.9 69.7 %pmax.45 = f32[1024]{0:T(1024)S(1)} all-reduce(f32[1024]{0:T(1024)S(1)} %fusion.3), channel_id=1, replica_groups=mesh['row'=32,'col'=16] {'row'}, use_global_device_ids=true, to_apply=%region_15.0 | all-reduce | flops 1024 | bytes 8192 | tf_op jit(solution)/shard_map/pmax | solution.py:31
  474.5 3.2 exponential_reduce_fusion.2
  477.8 71.6 %psum.45 = f32[1024]{0:T(1024)S(1)} all-reduce(f32[1024]{0:T(1024)S(1)} %exponential_reduce_fusion.2), channel_id=1, replica_groups=mesh['row'=32,'col'=16] {'row'}, use_global_device_ids=true, to_apply=%region_17.0 | all-reduce | flops 1024 | bytes 8192 | tf_op jit(solution)/shard_map/psum | solution.py:32
  549.4 2.8 fusion.4
  552.2 23.7 %pmax.46 = f32[1024]{0:T(1024)S(1)} all-reduce(f32[1024]{0:T(1024)S(1)} %fusion.4), channel_id=1, replica_groups=mesh['row'=32,'col'=16] {'col'}, use_global_device_ids=true, to_apply=%region_19.0 | all-reduce | flops 1024 | bytes 8192 | tf_op jit(solution)/shard_map/pmax | solution.py:27
  575.9 3.3 exponential_reduce_fusion.1
  579.2 23.6 %psum.46 = f32[1024]{0:T(1024)S(1)} all-reduce(f32[1024]{0:T(1024)S(1)} %exponential_reduce_fusion.1), channel_id=1, replica_groups=mesh['row'=32,'col'=16] {'col'}, use_global_device_ids=true, to_apply=%region_21.0 | all-reduce | flops 1024 | bytes 8192 | tf_op jit(solution)/shard_map/psum | solution.py:28
  602.7 0.0 copy-start.3
  602.8 2.8 fusion.5
  605.6 69.7 %pmax.47 = f32[1024]{0:T(1024)S(1)} all-reduce(f32[1024]{0:T(1024)S(1)} %fusion.5), channel_id=1, replica_groups=mesh['row'=32,'col'=16] {'row'}, use_global_device_ids=true, to_apply=%region_23.0 | all-reduce | flops 1024 | bytes 8192 | tf_op jit(solution)/shard_map/pmax | solution.py:31
  675.2 3.2 exponential_reduce_fusion
  678.5 0.0 copy-done.3
  678.5 71.6 %psum.47 = f32[1024]{0:T(1024)S(1)} all-reduce(f32[1024]{0:T(1024)S(1)} %exponential_reduce_fusion), channel_id=1, replica_groups=mesh['row'=32,'col'=16] {'row'}, use_global_device_ids=true, to_apply=%region_25.0 | all-reduce | flops 1024 | bytes 8192 | tf_op jit(solution)/shard_map/psum | solution.py:32
  750.1 0.6 add_multiply_fusion
  (5 shorter events, 0.0 us)
Async XLA Ops:
  7.2 135.9 %copy-start.2 = (f32[1024]{0:T(1024)S(1)}, f32[1024]{0:T(1024)}, u32[]{:S(2)}) copy-start(f32[1024]{0:T(1024)} %param.7) | copy-start | bytes 12292
  7.2 48.8 %all-gather.3.cloned.1.call-start = ((), (), s32[]{:S(2)}) async-start(), calls=%async_computation | async-start | bytes 2228224 | tf_op jit(solution)/shard_map/all_gather | solution.py:13
  7.9 133.1 %all-gather.5.cloned.1.call-start = ((), (), s32[]{:S(2)}) async-start(), calls=%async_computation.1 | async-start | bytes 2162688 | tf_op jit(solution)/shard_map/all_gather | solution.py:17
  56.0 87.1 %copy-start = (bf16[1024,1024]{1,0:T(8,128)(2,1)S(1)}, bf16[1024,1024]{1,0:T(8,128)(2,1)}, u32[]{:S(2)}) copy-start(bf16[1024,1024]{1,0:T(8,128)(2,1)} %all-gather.3.cloned.1.call-done) | copy-start | bytes 6291460
  149.2 50.4 %copy-start.1 = (f32[1024]{0:T(1024)S(1)}, f32[1024]{0:T(1024)}, u32[]{:S(2)}) copy-start(f32[1024]{0:T(1024)} %param.6) | copy-start | bytes 12292
  602.7 75.7 %copy-start.3 = (f32[1024]{0:T(1024)}, f32[1024]{0:T(1024)S(1)}, u32[]{:S(2)}) copy-start(f32[1024]{0:T(1024)S(1)} %add_multiply_fusion.1) | copy-start | bytes 12292
Sparse Core Ops, SparseCore 0:
  10.1 45.8 all-gather.2
  59.2 81.7 all-gather.4
where the time goes:
time: 758 us
  blocking collectives  567 us (75%)
  waiting for transfers between devices  132 us (17%)
  other arithmetic  38.5 us (5%)
  between operations  14.1 us (2%)
    psum x3, blocking collectives, local(): sums = lax.psum(jnp.sum(jnp.exp(weights - largest[None, :]), axis=0), 'row')  215 us
    pmax x3, blocking collectives, local(): largest = lax.pmax(jnp.max(weights, axis=0), 'row')  210 us
    all_gather x1, waiting for transfers between devices, local(): target_full = lax.all_gather(target_points, 'row', axis=0, tiled=True)  82.8 us
    pmax x3, blocking collectives, local(): highest = lax.pmax(jnp.max(scores, axis=1), 'col')  70.8 us
    psum x3, blocking collectives, local(): lax.psum(jnp.sum(jnp.exp(scores - highest[:, None]), axis=1), 'col')  70.7 us
    all_gather x1, waiting for transfers between devices, local(): source_full = lax.all_gather(source_points, 'col', axis=0, tiled=True)  47.3 us
  transfers between devices with their start and end apart: 2, of which 2 were waited for; matrix products, arithmetic and copies ran while one was open for 0% of the time, Pallas kernels for 0%

commit v1 on v0

v1 whole, which is shorter than its diff:
```python
import math

import jax
import jax.numpy as jnp
from jax import lax
from jax.experimental import pallas as pl
from jax.experimental.pallas import tpu as pltpu
from jax.sharding import PartitionSpec as P

ITERS = 3
EPSILON = 0.05
LOG2E = math.log2(math.e)
SCALE = 2.0 / EPSILON * LOG2E
BACK = EPSILON / LOG2E
NX, NZ = 4, 8
N = 1024
LANES = 128
GROUPS = N // LANES
PER_X = GROUPS // NX
F32 = jnp.float32
SMALL = (GROUPS, LANES)


def move_x(values, step):
    pairs = [(x * NZ + z, (x + step) % NX * NZ + z) for x in range(NX) for z in range(NZ)]
    return lax.ppermute(values, "row", pairs)


def gather_targets(points):
    copies = jnp.broadcast_to(points[None], (NZ,) + points.shape)
    lines = [[x * NZ + z for z in range(NZ)] for x in range(NX)]
    mine = lax.all_to_all(copies, "row", 0, 0, axis_index_groups=lines)
    mine = mine.reshape(-1, points.shape[1])
    half = mine.shape[0] // 2
    before, after = move_x(mine, 1), move_x(mine, -1)
    far = jnp.concatenate([move_x(after[:half], -1), move_x(before[half:], 1)], axis=0)
    return mine, after, far, before


def turned(values, back=False):
    x = lax.axis_index("row") // NZ
    out = values
    for s in range(1, NX):
        cut = (NX - s if back else s) * PER_X
        out = jnp.where(x == s, jnp.concatenate([values[cut:], values[:cut]], axis=0), out)
    return out


def merge_all(parts):
    top = jnp.max(parts, axis=0)
    return top + jnp.log2(jnp.sum(jnp.exp2(parts - top[None]), axis=0))


def over_targets(values, tiles, part, flat):
    for r in range(GROUPS):
        flat[:, pl.ds(r * LANES, LANES)] = jnp.broadcast_to(values[r : r + 1], SMALL)
    rows = []
    for r in range(GROUPS):
        tile = jnp.concatenate([ref[pl.ds(r * LANES, LANES), :] for ref in tiles], axis=1)
        tile = tile + flat[0:1, :]
        top = jnp.max(tile, axis=1, keepdims=True)
        log = top + jnp.log2(jnp.sum(jnp.exp2(tile - top), axis=1, keepdims=True))
        rows.append(jnp.broadcast_to(log, (LANES, LANES)).T[0:1])
    part[...] = jnp.broadcast_to(jnp.concatenate(rows, axis=0)[None], part.shape)


def first_kernel(mass, squares, *refs):
    tiles, (part, flat) = refs[:NX], refs[NX:]
    values = turned(mass[...] * LOG2E) - squares[...] * (1.0 / BACK)
    over_targets(values, tiles, part, flat)


def source_kernel(parts, mass, *refs):
    tiles, (part, flat) = refs[:NX], refs[NX:]
    over_targets(turned(mass[...] * LOG2E - merge_all(parts[...])), tiles, part, flat)


def target_kernel(parts, mass, squares, *refs):
    tiles, (part, potential, side) = refs[:NX], refs[NX:]
    log = merge_all(parts[...])
    potential[...] = squares[...] - BACK * log
    values = mass[...] * LOG2E - log
    for r in range(GROUPS):
        block = jnp.broadcast_to(values[r : r + 1], (LANES, LANES)).T
        side[pl.ds(r * LANES, LANES), :] = block
    rows = []
    for r in range(GROUPS):
        at = pl.ds(r % PER_X * LANES, LANES)
        tile = tiles[r // PER_X][:, at] + side[...]
        top = jnp.max(tile, axis=0, keepdims=True)
        rows.append(top + jnp.log2(jnp.sum(jnp.exp2(tile - top), axis=0, keepdims=True)))
    whole = turned(jnp.concatenate(rows, axis=0), back=True)
    part[...] = jnp.broadcast_to(whole[None], part.shape)


def last_kernel(parts, squares, potential):
    potential[...] = turned(squares[...], back=True) - BACK * merge_all(parts[...])


VMEM = pl.BlockSpec(memory_space=pltpu.VMEM)
WIDE = pltpu.VMEM((GROUPS, N), F32)
TALL = pltpu.VMEM((N, LANES), F32)


def call(kernel, shapes, scratch, *args):
    return pl.pallas_call(
        kernel,
        out_shape=[jax.ShapeDtypeStruct(shape, F32) for shape in shapes],
        in_specs=[VMEM] * len(args),
        out_specs=[VMEM] * len(shapes),
        scratch_shapes=scratch,
        compiler_params=pltpu.CompilerParams(vmem_limit_bytes=16 * 2**20),
        cost_estimate=pl.CostEstimate(
            flops=6 * N * N, bytes_accessed=4 * N * N, transcendentals=N * N
        ),
        name=kernel.__name__,
    )(*args)


def products(a, b):
    return SCALE * lax.dot_general(a, b, (((1,), (1,)), ((), ())), preferred_element_type=F32)


def squares(points):
    return jnp.sum(jnp.square(points.astype(F32)), axis=1).reshape(-1, LANES)


def local(source_points, target_points, source_logmass, target_logmass):
    rows, cols = lax.axis_size("row"), lax.axis_size("col")
    source_mass = source_logmass.reshape(SMALL)
    target_mass = target_logmass.reshape(SMALL)
    source = lax.all_gather(source_points, "col", axis=0, tiled=True)
    targets = gather_targets(target_points)
    target_sq = jnp.concatenate([squares(block) for block in targets], axis=0)
    tiles = [products(source, block) for block in targets]
    (part,) = call(first_kernel, [(cols,) + SMALL], [WIDE], target_mass, target_sq, *tiles)
    source_sq = squares(source)
    for step in range(ITERS):
        parts = lax.all_to_all(part, "col", 0, 0)
        part, source_potential = call(
            target_kernel, [(rows,) + SMALL, SMALL], [TALL], parts, source_mass, source_sq, *tiles
        )
        parts = lax.all_to_all(part, "row", 0, 0)
        if step < ITERS - 1:
            (part,) = call(source_kernel, [(cols,) + SMALL], [WIDE], parts, target_mass, *tiles)
    (target_potential,) = call(last_kernel, [SMALL], [], parts, target_sq)
    return source_potential.reshape(-1), target_potential.reshape(-1)


def solution(mesh):
    in_specs = (P(("row", "col"), None), P(("col", "row"), None), P("row"), P("col"))
    out_specs = (P("row"), P("col"))
    return jax.shard_map(local, mesh=mesh, in_specs=in_specs, out_specs=out_specs, check_vma=False)
```

time: 758 us -> 169 us (0.22)
  the two profiles are of different devices: /device:TPU:64 before, /device:TPU:1 now
where the time goes in v1:
time: 169 us; the launch traced here: 168 us
  blocking collectives  88.4 us (52%)
  starting transfers between devices  25.6 us (15%)
  waiting for transfers between devices  19 us (11%)
  between operations  14.2 us (8%)
  Pallas kernels  9.71 us (6%)
  matrix products  4.73 us (3%)
  local copies, waits for them, and re-layouts  3.83 us (2%)
  other arithmetic  2.81 us (2%)
    all_to_all x3, blocking collectives, local(): parts = lax.all_to_all(part, 'row', 0, 0)  37.1 us
    all_to_all x1, blocking collectives, gather_targets(): mine = lax.all_to_all(copies, 'row', 0, 0, axis_index_groups=lines)  26.7 us
    all_to_all x2, blocking collectives, local(): parts = lax.all_to_all(part, 'col', 0, 0)  24.7 us
    ppermute x4, starting transfers between devices, move_x(): return lax.ppermute(values, 'row', pairs)  13.6 us
    ppermute x4, waiting for transfers between devices, move_x(): return lax.ppermute(values, 'row', pairs)  12.6 us
    all_to_all x1, starting transfers between devices, local(): parts = lax.all_to_all(part, 'col', 0, 0)  11.9 us
    pallas_call x7, Pallas kernels, call(): pl.pallas_call(kernel, out_shape=[jax.ShapeDtypeStruct(shape, F32) for sh...  9.71 us
    all_to_all x1, waiting for transfers between devices, local(): parts = lax.all_to_all(part, 'col', 0, 0)  5.74 us
  transfers between devices with their start and end apart: 6, of which 4 were waited for; matrix products, arithmetic and copies ran while one was open for 2% of the time, Pallas kernels for 0%

profile of v1, /device:TPU:1, one launch (start us, length us, event | category | flops | bytes accessed | tf_op | source)
XLA Modules:
  0.0 168.3 jit_solution(3638416718685519556)
XLA Ops:
  7.2 0.0 all-gather.2.cloned.1.call-start
  7.2 0.7 all-gather.2.cloned.1.call-update
  7.9 0.9 broadcast_in_dim.2
  8.8 26.7 %all_to_all.35 = bf16[8,32,1024]{2,1,0:T(8,128)(2,1)S(1)} all-to-all(bf16[8,32,1024]{2,1,0:T(8,128)(2,1)S(1)} %broadcast_in_dim.2), channel_id=1, replica_groups={{0,16,32,48,64,80,96,112},{128,144,160,176,192,208,224,240},{256,272,28..., dimensions={0} | all-to-all | bytes 1048576 | tf_op jit(solution)/shard_map/all_to_all | solution.py:32
  35.5 4.4 %collective-permute-start = (bf16[256,1024]{1,0:T(8,128)(2,1)S(1)}, bf16[256,1024]{1,0:T(8,128)(2,1)S(1)}, u32[]{:S(2)}, u32[]{:S(2)}) collective-permute-start(bf16[256,1024]{1,0:T(8,128)(2,1)S(1)} %bitcast.28), channel_id=1, source_target_pairs={{0,384},{16,400},{32,416},{48,432},{64,448},{80,464},{96,480},{112... | collective-permute-start | bytes 1572872 | tf_op jit(solution)/shard_map/ppermute | solution.py:26
  39.8 1.9 %collective-permute-start.2 = (bf16[256,1024]{1,0:T(8,128)(2,1)S(1)}, bf16[256,1024]{1,0:T(8,128)(2,1)S(1)}, u32[]{:S(2)}, u32[]{:S(2)}) collective-permute-start(bf16[256,1024]{1,0:T(8,128)(2,1)S(1)} %bitcast.29), channel_id=1, source_target_pairs={{0,128},{16,144},{32,160},{48,176},{64,192},{80,208},{96,224},{112... | collective-permute-start | bytes 1572872 | tf_op jit(solution)/shard_map/ppermute | solution.py:26
  41.8 0.2 multiply_reduce_fusion.4
  41.9 0.1 reshape.38
  42.0 6.5 %collective-permute-done = bf16[256,1024]{1,0:T(8,128)(2,1)S(1)} collective-permute-done((bf16[256,1024]{1,0:T(8,128)(2,1)S(1)}, bf16[256,1024]{1,0:T(8,128)(2,1)S(1)}, u32[]{:S(2)}, u32[]{:S(2)}) %collective-permute-start) | collective-permute-done | bytes 524320 | tf_op jit(solution)/shard_map/ppermute | solution.py:26
  48.6 5.4 %collective-permute-start.1 = (bf16[128,1024]{1,0:T(8,128)(2,1)S(1)}, bf16[128,1024]{1,0:T(8,128)(2,1)S(1)}, u32[]{:S(2)}, u32[]{:S(2)}) collective-permute-start(bf16[128,1024]{1,0:T(8,128)(2,1)S(1)} %slice.8), channel_id=1, source_target_pairs={{0,384},{16,400},{32,416},{48,432},{64,448},{80,464},{96,480},{112... | collective-permute-start | bytes 786440 | tf_op jit(solution)/shard_map/ppermute | solution.py:26
  54.0 0.0 collective-permute-done.2
  54.1 1.9 %collective-permute-start.3 = (bf16[128,1024]{1,0:T(8,128)(2,1)S(1)}, bf16[128,1024]{1,0:T(8,128)(2,1)S(1)}, u32[]{:S(2)}, u32[]{:S(2)}) collective-permute-start(bf16[128,1024]{1,0:T(8,128)(2,1)S(1)} %slice.9), channel_id=1, source_target_pairs={{0,128},{16,144},{32,160},{48,176},{64,192},{80,208},{96,224},{112... | collective-permute-start | bytes 786440 | tf_op jit(solution)/shard_map/ppermute | solution.py:26
  56.0 0.2 multiply_reduce_fusion.3
  56.2 0.2 multiply_reduce_fusion.1
  56.4 1.0 collective-permute-done.1
  57.3 5.0 %collective-permute-done.3 = bf16[128,1024]{1,0:T(8,128)(2,1)S(1)} collective-permute-done((bf16[128,1024]{1,0:T(8,128)(2,1)S(1)}, bf16[128,1024]{1,0:T(8,128)(2,1)S(1)}, u32[]{:S(2)}, u32[]{:S(2)}) %collective-permute-start.3) | collective-permute-done | bytes 262176 | tf_op jit(solution)/shard_map/ppermute | solution.py:26
  62.4 0.2 multiply_reduce_fusion.2
  62.6 0.0 copy-done.6
  62.6 0.0 copy-done.8
  62.6 0.0 all-gather.2.cloned.1.call-done
  62.7 0.0 copy-start.5
  62.7 2.5 %fusion.refs_2_ = f32[1024,256]{1,0:T(8,128)S(1)} fusion(bf16[256,1024]{1,0:T(8,128)(2,1)S(1)} %constant_dynamic-update-slice_fusion, bf16[1024,1024]{1,0:T(8,128)(2,1)} %all-gather.2.cloned.1.call-done), kind=kOutput, calls=%fused_computation.3 | convolution fusion | flops 537133056 | bytes 3670016 | tf_op jit(solution)/shard_map/dot_general | solution.py:121
  65.2 0.0 copy-done.5
  65.2 0.0 copy-start.9
  65.2 0.8 convolution_multiply_fusion.refs_3_
  66.0 0.3 copy-done.9
  66.2 0.7 convolution_multiply_fusion.2.refs_1_
  67.0 0.3 copy-done.7
  67.3 0.7 convolution_multiply_fusion.3.refs_0_
  68.0 0.0 copy-done.3
  68.0 1.8 %first_kernel.1 = f32[16,8,128]{2,1,0:T(8,128)} custom-call(f32[8,128]{1,0:T(8,128)S(1)} %bitcast.22, f32[8,128]{1,0:T(8,128)S(1)} %pad_maximum_fusion.squares, f32[1024,256]{1,0:T(8,128)S(1)} %convolution_multiply_fusion.3.refs_0_, f32[1024,256]{1,0:T(8,128)S(1)} %convolution_multiply_fusion.2.refs_1_, f32[1024,256]{1,0:T(8,128)S(1)} %fusion.refs_2_, ...), custom_call_target="tpu_custom_call" | custom-call | flops 6291456 | bytes 4194304 | tf_op jit(solution)/shard_map/first_kernel/pallas_call | solution.py:106
  69.9 1.0 copy-done
  70.8 11.9 %all-to-all-start.1 = ((f32[16,8,128]{2,1,0:T(8,128)}), f32[16,8,128]{2,1,0:T(8,128)S(1)}, u32[]{:S(2)}, u32[]{:S(2)}) async-start(f32[16,8,128]{2,1,0:T(8,128)} %first_kernel.1), calls=%async_computation.1 | async-start | bytes 131072 | tf_op jit(solution)/shard_map/all_to_all | solution.py:139
  82.8 2.1 %multiply_reduce_fusion = f32[1024]{0:T(1024)S(1)} fusion(bf16[1024,1024]{1,0:T(8,128)(2,1)} %all-gather.2.cloned.1.call-done), kind=kLoop, calls=%fused_computation | loop fusion | flops 3144704 | bytes 2101248 | tf_op jit(solution)/shard_map/reduce_sum | solution.py:125
  84.9 5.7 %all-to-all-done.1.parts = f32[16,8,128]{2,1,0:T(8,128)S(1)} async-done(((f32[16,8,128]{2,1,0:T(8,128)}), f32[16,8,128]{2,1,0:T(8,128)S(1)}, u32[]{:S(2)}, u32[]{:S(2)}) %all-to-all-start.1) | async-done | bytes 65568 | tf_op jit(solution)/shard_map/all_to_all | solution.py:139
  90.6 1.2 copy-done.1
  91.8 1.6 target_kernel.3
  93.4 12.3 %all_to_all.36.parts = f32[32,8,128]{2,1,0:T(8,128)S(1)} all-to-all(f32[32,8,128]{2,1,0:T(8,128)S(1)} %get-tuple-element.6), channel_id=1, replica_groups=mesh['row'=32,'col'=16] {'row'}, dimensions={0} | all-to-all | bytes 262144 | tf_op jit(solution)/shard_map/all_to_all | solution.py:143
  105.7 0.0 copy-done.2
  105.7 1.2 source_kernel.2
  106.9 12.3 %all_to_all.37.parts = f32[16,8,128]{2,1,0:T(8,128)S(1)} all-to-all(f32[16,8,128]{2,1,0:T(8,128)S(1)} %source_kernel.2), channel_id=1, replica_groups=mesh['row'=32,'col'=16] {'col'}, dimensions={0} | all-to-all | bytes 131072 | tf_op jit(solution)/shard_map/all_to_all | solution.py:139
  119.3 1.6 target_kernel.4
  120.9 12.4 %all_to_all.38.parts = f32[32,8,128]{2,1,0:T(8,128)S(1)} all-to-all(f32[32,8,128]{2,1,0:T(8,128)S(1)} %get-tuple-element.7), channel_id=1, replica_groups=mesh['row'=32,'col'=16] {'row'}, dimensions={0} | all-to-all | bytes 262144 | tf_op jit(solution)/shard_map/all_to_all | solution.py:143
  133.3 1.2 source_kernel.3
  134.5 12.3 %all_to_all.39.parts = f32[16,8,128]{2,1,0:T(8,128)S(1)} all-to-all(f32[16,8,128]{2,1,0:T(8,128)S(1)} %source_kernel.3), channel_id=1, replica_groups=mesh['row'=32,'col'=16] {'col'}, dimensions={0} | all-to-all | bytes 131072 | tf_op jit(solution)/shard_map/all_to_all | solution.py:139
  146.8 1.6 target_kernel.5
  148.4 12.4 %all_to_all.40.parts = f32[32,8,128]{2,1,0:T(8,128)S(1)} all-to-all(f32[32,8,128]{2,1,0:T(8,128)S(1)} %get-tuple-element.9), channel_id=1, replica_groups=mesh['row'=32,'col'=16] {'row'}, dimensions={0} | all-to-all | bytes 262144 | tf_op jit(solution)/shard_map/all_to_all | solution.py:143
  160.9 0.7 last_kernel.1
  (14 shorter events, 0.1 us)
Async XLA Ops:
  7.2 55.5 %all-gather.2.cloned.1.call-start = ((), (), s32[]{:S(2)}) async-start(), calls=%async_computation.7 | async-start | bytes 2228224 | tf_op jit(solution)/shard_map/all_gather | solution.py:132
  35.5 27.1 %copy-start.6 = (bf16[8,32,1024]{2,1,0:T(8,128)(2,1)}, bf16[8,32,1024]{2,1,0:T(8,128)(2,1)S(1)}, u32[]{:S(2)}) copy-start(bf16[8,32,1024]{2,1,0:T(8,128)(2,1)S(1)} %all_to_all.35) | copy-start | bytes 1572868
  35.5 13.1 %collective-permute-start = (bf16[256,1024]{1,0:T(8,128)(2,1)S(1)}, bf16[256,1024]{1,0:T(8,128)(2,1)S(1)}, u32[]{:S(2)}, u32[]{:S(2)}) collective-permute-start(bf16[256,1024]{1,0:T(8,128)(2,1)S(1)} %bitcast.28), channel_id=1, source_target_pairs={{0,384},{16,400},{32,416},{48,432},{64,448},{80,464},{96,480},{112... | collective-permute-start | bytes 1572872 | tf_op jit(solution)/shard_map/ppermute | solution.py:26
  39.8 14.2 %collective-permute-start.2 = (bf16[256,1024]{1,0:T(8,128)(2,1)S(1)}, bf16[256,1024]{1,0:T(8,128)(2,1)S(1)}, u32[]{:S(2)}, u32[]{:S(2)}) collective-permute-start(bf16[256,1024]{1,0:T(8,128)(2,1)S(1)} %bitcast.29), channel_id=1, source_target_pairs={{0,128},{16,144},{32,160},{48,176},{64,192},{80,208},{96,224},{112... | collective-permute-start | bytes 1572872 | tf_op jit(solution)/shard_map/ppermute | solution.py:26
  48.6 14.1 %copy-start.8 = (bf16[256,1024]{1,0:T(8,128)(2,1)}, bf16[256,1024]{1,0:T(8,128)(2,1)S(1)}, u32[]{:S(2)}) copy-start(bf16[256,1024]{1,0:T(8,128)(2,1)S(1)} %collective-permute-done) | copy-start | bytes 1572868
  48.6 8.7 %collective-permute-start.1 = (bf16[128,1024]{1,0:T(8,128)(2,1)S(1)}, bf16[128,1024]{1,0:T(8,128)(2,1)S(1)}, u32[]{:S(2)}, u32[]{:S(2)}) collective-permute-start(bf16[128,1024]{1,0:T(8,128)(2,1)S(1)} %slice.8), channel_id=1, source_target_pairs={{0,384},{16,400},{32,416},{48,432},{64,448},{80,464},{96,480},{112... | collective-permute-start | bytes 786440 | tf_op jit(solution)/shard_map/ppermute | solution.py:26
  54.1 8.3 %collective-permute-start.3 = (bf16[128,1024]{1,0:T(8,128)(2,1)S(1)}, bf16[128,1024]{1,0:T(8,128)(2,1)S(1)}, u32[]{:S(2)}, u32[]{:S(2)}) collective-permute-start(bf16[128,1024]{1,0:T(8,128)(2,1)S(1)} %slice.9), channel_id=1, source_target_pairs={{0,128},{16,144},{32,160},{48,176},{64,192},{80,208},{96,224},{112... | collective-permute-start | bytes 786440 | tf_op jit(solution)/shard_map/ppermute | solution.py:26
  62.7 2.5 %copy-start.5 = (bf16[1024,1024]{1,0:T(8,128)(2,1)S(1)}, bf16[1024,1024]{1,0:T(8,128)(2,1)}, u32[]{:S(2)}) copy-start(bf16[1024,1024]{1,0:T(8,128)(2,1)} %all-gather.2.cloned.1.call-done) | copy-start | bytes 6291460
  65.2 1.0 copy-start.9
  66.2 1.0 copy-start.7
  67.3 0.8 copy-start.3
  69.9 1.0 copy-start
  70.8 19.8 %copy-start.4 = (f32[1024]{0:T(1024)S(1)}, f32[1024]{0:T(1024)}, u32[]{:S(2)}) copy-start(f32[1024]{0:T(1024)} %param.6) | copy-start | bytes 12292
  70.8 19.8 %all-to-all-start.1 = ((f32[16,8,128]{2,1,0:T(8,128)}), f32[16,8,128]{2,1,0:T(8,128)S(1)}, u32[]{:S(2)}, u32[]{:S(2)}) async-start(f32[16,8,128]{2,1,0:T(8,128)} %first_kernel.1), calls=%async_computation.1 | async-start | bytes 131072 | tf_op jit(solution)/shard_map/all_to_all | solution.py:139
  90.6 1.2 copy-start.1
  91.8 13.9 %copy-start.2 = (f32[1024,256]{1,0:T(8,128)S(1)}, f32[1024,256]{1,0:T(8,128)}, u32[]{:S(2)}) copy-start(f32[1024,256]{1,0:T(8,128)} %copy-done) | copy-start | bytes 3145732
Sparse Core Ops, SparseCore 0:
  10.1 47.7 all-gather.1

commit v2 on v1

v2 whole, which is shorter than its diff:
```python
import math

import jax
import jax.numpy as jnp
from jax import lax
from jax.experimental import pallas as pl
from jax.experimental.pallas import tpu as pltpu
from jax.sharding import PartitionSpec as P

ITERS = 3
EPSILON = 0.05
LOG2E = math.log2(math.e)
SCALE = 2.0 / EPSILON * LOG2E
BACK = EPSILON / LOG2E
NX, NZ, NY, NC = 4, 8, 8, 2
RING = (0, -1, 1, -2, 2, -3, 3, 4)
N = 1024
LANES = 128
GROUPS = N // LANES
F32 = jnp.float32
SMALL = (GROUPS, LANES)


def move_col(values, place):
    pairs = []
    for y in range(NY):
        for core in range(NC):
            to_y, to_core = place(y, core)
            pairs.append((y * NC + core, to_y % NY * NC + to_core))
    return lax.ppermute(values, "col", pairs)


def ring_step(ahead, back):
    return (
        move_col(ahead, lambda y, core: (y + 1, core)),
        move_col(back, lambda y, core: (y - 1, core)),
    )


def spread(values, count, lines):
    copies = jnp.broadcast_to(values[None], (count,) + values.shape)
    out = lax.all_to_all(copies, "row", 0, 0, axis_index_groups=lines)
    return out.reshape((-1,) + values.shape[1:])


def gather_points(source_points, target_points, masses):
    along_z = [[x * NZ + z for z in range(NZ)] for x in range(NX)]
    along_x = [[x * NZ + z for x in range(NX)] for z in range(NZ)]
    line = spread(target_points, NZ, along_z)
    held = {0: source_points}
    held[-1], held[1] = ring_step(source_points, source_points)
    held[-2], held[2] = ring_step(held[-1], held[1])
    held[-2], held[2], line, masses = lax.optimization_barrier((held[-2], held[2], line, masses))
    target = spread(line, NX, along_x)
    held[-3], held[3] = ring_step(held[-2], held[2])
    held[4] = move_col(held[3], lambda y, core: (y - 1, core))
    mine = assemble([held[place] for place in RING])
    other = move_col(mine, lambda y, core: (y, 1 - core))
    return mine, other, target, masses


def assemble_kernel(*refs):
    pieces = refs[: len(RING)]
    out, sems = refs[len(RING) :]
    y = lax.axis_index("col") // NC
    made = []
    for k, ref in enumerate(pieces):
        rows = ref.shape[0]
        start = pl.multiple_of((y + RING[k] + NY) % NY * rows, rows)
        made.append(pltpu.make_async_copy(ref, out.at[pl.ds(start, rows)], sems.at[k]))
        made[-1].start()
    for copy in made:
        copy.wait()


def place_kernel(points, out, squares, sems):
    made = []
    for r in range(GROUPS):
        rows = pl.ds(r * LANES, LANES)
        made.append(pltpu.make_async_copy(points.at[rows], out.at[rows], sems.at[r]))
        made[-1].start()
    sums = []
    for r in range(GROUPS):
        made[r].wait()
        square = jnp.square(out[pl.ds(r * LANES, LANES), :].astype(F32))
        total = jnp.sum(square, axis=1, keepdims=True)
        sums.append(jnp.broadcast_to(total, (LANES, LANES)).T[0:1])
    squares[...] = jnp.concatenate(sums, axis=0)


def columns(values, side):
    for r in range(GROUPS):
        side[pl.ds(r * LANES, LANES), :] = jnp.broadcast_to(values[r : r + 1], (LANES, LANES)).T


def by_core(values):
    swapped = jnp.concatenate([values[GROUPS // 2 :], values[: GROUPS // 2]], axis=0)
    core = lax.axis_index("col") % NC
    return jnp.where(core == 1, swapped, values)


def merge_all(parts):
    top = jnp.max(parts, axis=0)
    return top + jnp.log2(jnp.sum(jnp.exp2(parts - top[None]), axis=0))


def over_targets(values, mine, other, part, flat):
    for r in range(GROUPS):
        flat[:, pl.ds(r * LANES, LANES)] = jnp.broadcast_to(values[r : r + 1], SMALL)
    rows = []
    for scaled in (mine, other):
        for r in range(GROUPS // NC):
            tile = scaled[pl.ds(r * LANES, LANES), :] + flat[0:1, :]
            top = jnp.max(tile, axis=1, keepdims=True)
            log = top + jnp.log2(jnp.sum(jnp.exp2(tile - top), axis=1, keepdims=True))
            rows.append(jnp.broadcast_to(log, (LANES, LANES)).T[0:1])
    part[...] = jnp.broadcast_to(by_core(jnp.concatenate(rows, axis=0))[None], part.shape)


def first_kernel(mass, squares, mine, other, part, flat):
    over_targets(mass[...] - squares[...] * (1.0 / BACK), mine, other, part, flat)


def source_kernel(parts, mass, mine, other, part, flat):
    over_targets(mass[...] - merge_all(parts[...]), mine, other, part, flat)


def target_kernel(parts, mass, squares, mine, other, part, potential, side):
    log = merge_all(parts[...])
    potential[...] = by_core(squares[...]) - BACK * log
    columns(by_core(mass[...] - log), side)
    rows = []
    for r in range(GROUPS):
        at = pl.ds(r * LANES, LANES)
        tile = jnp.concatenate([mine[:, at], other[:, at]], axis=0) + side[...]
        top = jnp.max(tile, axis=0, keepdims=True)
        rows.append(top + jnp.log2(jnp.sum(jnp.exp2(tile - top), axis=0, keepdims=True)))
    part[...] = jnp.broadcast_to(jnp.concatenate(rows, axis=0)[None], part.shape)


def last_kernel(parts, squares, potential):
    potential[...] = squares[...] - BACK * merge_all(parts[...])


VMEM = pl.BlockSpec(memory_space=pltpu.VMEM)
HBM = pl.BlockSpec(memory_space=pltpu.HBM)
PARAMS = pltpu.CompilerParams(vmem_limit_bytes=16 * 2**20)
COST = pl.CostEstimate(flops=6 * N * N, bytes_accessed=4 * N * N, transcendentals=N * N)


def assemble(pieces):
    rows, depth = pieces[0].shape
    return pl.pallas_call(
        assemble_kernel,
        out_shape=jax.ShapeDtypeStruct((NY * rows, depth), jnp.bfloat16),
        in_specs=[HBM] * len(RING),
        out_specs=VMEM,
        scratch_shapes=[pltpu.SemaphoreType.DMA((len(RING),))],
        compiler_params=PARAMS,
        cost_estimate=pl.CostEstimate(flops=0, bytes_accessed=2**22, transcendentals=0),
        name="assemble",
    )(*pieces)


WIDE = pltpu.VMEM((GROUPS, N), F32)
TALL = pltpu.VMEM((N, LANES), F32)


def place(points):
    return pl.pallas_call(
        place_kernel,
        out_shape=(
            jax.ShapeDtypeStruct(points.shape, jnp.bfloat16),
            jax.ShapeDtypeStruct(SMALL, F32),
        ),
        in_specs=[HBM],
        out_specs=(VMEM, VMEM),
        scratch_shapes=[pltpu.SemaphoreType.DMA((GROUPS,))],
        compiler_params=PARAMS,
        cost_estimate=COST,
        name="place",
    )(points)


def call(kernel, shapes, scratch, *args):
    return pl.pallas_call(
        kernel,
        out_shape=[jax.ShapeDtypeStruct(shape, F32) for shape in shapes],
        in_specs=[VMEM] * len(args),
        out_specs=[VMEM] * len(shapes),
        scratch_shapes=scratch,
        compiler_params=PARAMS,
        cost_estimate=COST,
        name=kernel.__name__,
    )(*args)


def products(a, b):
    return SCALE * lax.dot_general(a, b, (((1,), (1,)), ((), ())), preferred_element_type=F32)


def squares(points):
    return jnp.sum(jnp.square(points.astype(F32)), axis=1).reshape(-1, LANES)


def core_first(values):
    return values.reshape(NY, NC, -1).transpose(1, 0, 2).reshape(SMALL)


def y_first(values):
    return values.reshape(NC, NY, -1).transpose(1, 0, 2).reshape(-1)


def local(source_points, target_points, source_logmass, target_logmass):
    rows, cols = lax.axis_size("row"), lax.axis_size("col")
    masses = core_first(source_logmass * LOG2E), (target_logmass * LOG2E).reshape(SMALL)
    mine, other, target, masses = gather_points(source_points, target_points, masses)
    source_mass, target_mass = masses
    target, target_sq = place(target)
    tiles = products(mine, target), products(other, target)
    (part,) = call(first_kernel, [(cols,) + SMALL], [WIDE], target_mass, target_sq, *tiles)
    source_sq = jnp.concatenate([squares(mine), squares(other)], axis=0)
    for step in range(ITERS):
        parts = lax.all_to_all(part, "col", 0, 0)
        part, source_potential = call(
            target_kernel, [(rows,) + SMALL, SMALL], [TALL], parts, source_mass, source_sq, *tiles
        )
        parts = lax.all_to_all(part, "row", 0, 0)
        if step < ITERS - 1:
            (part,) = call(source_kernel, [(cols,) + SMALL], [WIDE], parts, target_mass, *tiles)
    (target_potential,) = call(last_kernel, [SMALL], [], parts, target_sq)
    return y_first(source_potential), target_potential.reshape(-1)


def solution(mesh):
    in_specs = (P(("row", "col"), None), P(("col", "row"), None), P("row"), P("col"))
    out_specs = (P("row"), P("col"))
    return jax.shard_map(local, mesh=mesh, in_specs=in_specs, out_specs=out_specs, check_vma=False)
```

time: 169 us -> 164 us (0.970)
  blocking collectives: 88.4 us -> 52.9 us
  starting transfers between devices: 25.6 us -> 59.7 us
  between operations: 14.2 us -> 0.79 us
  local copies, waits for them, and re-layouts: 3.83 us -> 8.95 us
  Pallas kernels: 9.71 us -> 12.6 us
  waiting for transfers between devices: 19 us -> 21 us
    all_to_all x1 -> x0, blocking collectives: 26.7 us -> none  [gather_targets(): mine = lax.all_to_all(copies, 'row', 0, 0, axis_index_groups=lines)]
    all_to_all x0 -> x3, starting transfers between devices: none -> 18.9 us  [the longest x2 15 us: spread(): out = lax.all_to_all(copies, 'row', 0, 0, axis_index_groups=lines)]
    ppermute x4 -> x8, starting transfers between devices: 13.6 us -> 31.2 us  [move_col(): return lax.ppermute(values, 'col', pairs)]
    all_to_all x0 -> x3, waiting for transfers between devices: none -> 11.2 us  [the longest x1 8.39 us: local(): parts = lax.all_to_all(part, 'row', 0, 0)]
    ppermute x4 -> x8, waiting for transfers between devices: 12.6 us -> 3.48 us  [move_col(): return lax.ppermute(values, 'col', pairs)]
    all_to_all x3 -> x2, blocking collectives: 37.1 us -> 28.2 us  [local(): parts = lax.all_to_all(part, 'row', 0, 0)]
    pallas_call x0 -> x2, Pallas kernels: none -> 2.98 us  [the longest x1 1.54 us: place(): pl.pallas_call(place_kernel, out_shape=(jax.ShapeDtypeStruct(points.shape...]
    broadcast_in_dim x1 -> x2, local copies, waits for them, and re-layouts: 0.89 us -> 3.3 us  [spread(): copies = jnp.broadcast_to(values[None], (count,) + values.shape)]
  transfers between devices with their start and end apart: 6 -> 12, of which waited for: 4 -> 7; matrix products, arithmetic and copies ran while one was open for 2% -> 3% of each run, Pallas kernels for 0% -> 2%
where the time goes in v2:
time: 164 us; the launch traced here: 163 us
  starting transfers between devices  59.7 us (36%)
  blocking collectives  52.9 us (32%)
  waiting for transfers between devices  21 us (13%)
  Pallas kernels  12.6 us (8%)
  local copies, waits for them, and re-layouts  8.95 us (5%)
  matrix products  3.81 us (2%)
  other arithmetic  3.18 us (2%)
    ppermute x8, starting transfers between devices, move_col(): return lax.ppermute(values, 'col', pairs)  31.2 us
    all_to_all x2, blocking collectives, local(): parts = lax.all_to_all(part, 'row', 0, 0)  28.2 us
    all_to_all x2, blocking collectives, local(): parts = lax.all_to_all(part, 'col', 0, 0)  24.7 us
    all_to_all x2, starting transfers between devices, spread(): out = lax.all_to_all(copies, 'row', 0, 0, axis_index_groups=lines)  15 us
    all_to_all x1, starting transfers between devices, local(): parts = lax.all_to_all(part, 'col', 0, 0)  9.68 us
    pallas_call x7, Pallas kernels, call(): pl.pallas_call(kernel, out_shape=[jax.ShapeDtypeStruct(shape, F32) for sh...  9.57 us
    all_to_all x1, waiting for transfers between devices, local(): parts = lax.all_to_all(part, 'row', 0, 0)  8.39 us
    all_to_all x1, waiting for transfers between devices, local(): parts = lax.all_to_all(part, 'col', 0, 0)  6.29 us
  transfers between devices with their start and end apart: 12, of which 7 were waited for; matrix products, arithmetic and copies ran while one was open for 3% of the time, Pallas kernels for 2%

profile of v2, /device:TPU:1, one launch (start us, length us, event | category | flops | bytes accessed | tf_op | source)
XLA Modules:
  0.0 162.9 jit_solution(5973746635709602944)
XLA Ops:
  0.6 1.7 %broadcast_in_dim.4 = bf16[8,32,1024]{2,1,0:T(8,128)(2,1)} broadcast(bf16[32,1024]{1,0:T(8,128)(2,1)} %param.5), dimensions={1,2} | broadcast | bytes 589824 | tf_op jit(solution)/shard_map/broadcast_in_dim | solution.py:41
  2.3 10.9 %all-to-all-start = ((bf16[8,32,1024]{2,1,0:T(8,128)(2,1)}), bf16[8,32,1024]{2,1,0:T(8,128)(2,1)S(1)}, u32[]{:S(2)}, u32[]{:S(2)}) async-start(bf16[8,32,1024]{2,1,0:T(8,128)(2,1)} %broadcast_in_dim.4), calls=%async_computation | async-start | bytes 1048576 | tf_op jit(solution)/shard_map/all_to_all | solution.py:42
  13.2 3.2 %collective-permute-start = (bf16[64,1024]{1,0:T(8,128)(2,1)}, bf16[64,1024]{1,0:T(8,128)(2,1)S(1)}, u32[]{:S(2)}, u32[]{:S(2)}) collective-permute-start(bf16[64,1024]{1,0:T(8,128)(2,1)} %refs_0_.1), channel_id=1, source_target_pairs={{0,2},{1,3},{2,4},{3,5},{4,6},{5,7},{6,8},{7,9},{8,10},{9,11},{10,... | collective-permute-start | bytes 393224 | tf_op jit(solution)/shard_map/ppermute | solution.py:30
  16.4 3.8 %collective-permute-start.2 = (bf16[64,1024]{1,0:T(8,128)(2,1)}, bf16[64,1024]{1,0:T(8,128)(2,1)S(1)}, u32[]{:S(2)}, u32[]{:S(2)}) collective-permute-start(bf16[64,1024]{1,0:T(8,128)(2,1)} %refs_0_.1), channel_id=1, source_target_pairs={{0,14},{1,15},{2,0},{3,1},{4,2},{5,3},{6,4},{7,5},{8,6},{9,7},{10,... | collective-permute-start | bytes 393224 | tf_op jit(solution)/shard_map/ppermute | solution.py:30
  20.2 0.7 broadcast_multiply_fusion
  20.9 0.1 reshape.37
  21.0 0.1 reshape.38.mass
  21.1 0.3 collective-permute-done.refs_1_
  21.4 1.9 %collective-permute-start.1 = (bf16[64,1024]{1,0:T(8,128)(2,1)S(1)}, bf16[64,1024]{1,0:T(8,128)(2,1)S(1)}, u32[]{:S(2)}, u32[]{:S(2)}) collective-permute-start(bf16[64,1024]{1,0:T(8,128)(2,1)S(1)} %collective-permute-done.refs_1_), channel_id=1, source_target_pairs={{0,2},{1,3},{2,4},{3,5},{4,6},{5,7},{6,8},{7,9},{8,10},{9,11},{10,... | collective-permute-start | bytes 393224 | tf_op jit(solution)/shard_map/ppermute | solution.py:30
  23.3 4.6 %collective-permute-start.3 = (bf16[64,1024]{1,0:T(8,128)(2,1)S(1)}, bf16[64,1024]{1,0:T(8,128)(2,1)S(1)}, u32[]{:S(2)}, u32[]{:S(2)}) collective-permute-start(bf16[64,1024]{1,0:T(8,128)(2,1)S(1)} %collective-permute-done.2.refs_2_), channel_id=1, source_target_pairs={{0,14},{1,15},{2,0},{3,1},{4,2},{5,3},{6,4},{7,5},{8,6},{9,7},{10,... | collective-permute-start | bytes 393224 | tf_op jit(solution)/shard_map/ppermute | solution.py:30
  27.9 0.7 multiply_bitcast_fusion.mass
  28.6 1.2 collective-permute-done.3.refs_4_
  29.8 1.3 all-to-all-done
  31.2 1.6 broadcast_in_dim.5
  32.8 4.1 %all-to-all-start.1 = ((bf16[4,256,1024]{2,1,0:T(8,128)(2,1)}), bf16[4,256,1024]{2,1,0:T(8,128)(2,1)S(1)}, u32[]{:S(2)}, u32[]{:S(2)}) async-start(bf16[4,256,1024]{2,1,0:T(8,128)(2,1)} %broadcast_in_dim.5), calls=%async_computation.1 | async-start | bytes 4194304 | tf_op jit(solution)/shard_map/all_to_all | solution.py:42
  36.9 5.1 %collective-permute-start.5 = (bf16[64,1024]{1,0:T(8,128)(2,1)S(1)}, bf16[64,1024]{1,0:T(8,128)(2,1)S(1)}, u32[]{:S(2)}, u32[]{:S(2)}) collective-permute-start(bf16[64,1024]{1,0:T(8,128)(2,1)S(1)} %collective-permute-done.3.refs_4_), channel_id=1, source_target_pairs={{0,14},{1,15},{2,0},{3,1},{4,2},{5,3},{6,4},{7,5},{8,6},{9,7},{10,... | collective-permute-start | bytes 393224 | tf_op jit(solution)/shard_map/ppermute | solution.py:30
  42.0 1.9 %collective-permute-start.4 = (bf16[64,1024]{1,0:T(8,128)(2,1)S(1)}, bf16[64,1024]{1,0:T(8,128)(2,1)S(1)}, u32[]{:S(2)}, u32[]{:S(2)}) collective-permute-start(bf16[64,1024]{1,0:T(8,128)(2,1)S(1)} %collective-permute-done.1.refs_3_), channel_id=1, source_target_pairs={{0,2},{1,3},{2,4},{3,5},{4,6},{5,7},{6,8},{7,9},{8,10},{9,11},{10,... | collective-permute-start | bytes 393224 | tf_op jit(solution)/shard_map/ppermute | solution.py:30
  43.9 5.2 %collective-permute-start.6 = (bf16[64,1024]{1,0:T(8,128)(2,1)S(1)}, bf16[64,1024]{1,0:T(8,128)(2,1)S(1)}, u32[]{:S(2)}, u32[]{:S(2)}) collective-permute-start(bf16[64,1024]{1,0:T(8,128)(2,1)S(1)} %collective-permute-done.5.refs_6_), channel_id=1, source_target_pairs={{0,14},{1,15},{2,0},{3,1},{4,2},{5,3},{6,4},{7,5},{8,6},{9,7},{10,... | collective-permute-start | bytes 393224 | tf_op jit(solution)/shard_map/ppermute | solution.py:30
  49.2 1.9 %collective-permute-done.6.refs_7_ = bf16[64,1024]{1,0:T(8,128)(2,1)S(1)} collective-permute-done((bf16[64,1024]{1,0:T(8,128)(2,1)S(1)}, bf16[64,1024]{1,0:T(8,128)(2,1)S(1)}, u32[]{:S(2)}, u32[]{:S(2)}) %collective-permute-start.6) | collective-permute-done | bytes 131104 | tf_op jit(solution)/shard_map/ppermute | solution.py:30
  51.1 0.9 copy-done.5
  52.0 0.9 copy-done.7
  52.9 1.4 assemble.1
  54.4 5.4 %collective-permute-start.7 = (bf16[512,1024]{1,0:T(8,128)(2,1)S(1)}, bf16[512,1024]{1,0:T(8,128)(2,1)}, u32[]{:S(2)}, u32[]{:S(2)}) collective-permute-start(bf16[512,1024]{1,0:T(8,128)(2,1)S(1)} %assemble.1), channel_id=1, source_target_pairs={{0,1},{1,0},{2,3},{3,2},{4,5},{5,4},{6,7},{7,6},{8,9},{9,8},{10,11... | collective-permute-start | bytes 3145736 | tf_op jit(solution)/shard_map/ppermute | solution.py:30
  59.8 0.3 multiply_reduce_fusion.1
  60.1 1.5 all-to-all-done.1
  61.6 1.5 place.1
  63.2 1.3 convolution_multiply_fusion.1.mine
  64.5 2.5 %convolution_multiply_fusion.other = f32[512,1024]{1,0:T(8,128)S(1)} fusion(bf16[512,1024]{1,0:T(8,128)(2,1)} %collective-permute-done.7, bf16[1024,1024]{1,0:T(8,128)(2,1)S(1)} %get-tuple-element.18), kind=kOutput, calls=%fused_computation.2 | convolution fusion | flops 1074266112 | bytes 5242880 | tf_op jit(solution)/shard_map/dot_general | solution.py:199
  67.0 1.8 %first_kernel.1 = f32[16,8,128]{2,1,0:T(8,128)} custom-call(f32[8,128]{1,0:T(8,128)S(1)} %multiply_bitcast_fusion.mass, f32[8,128]{1,0:T(8,128)S(1)} %get-tuple-element.15.squares, f32[512,1024]{1,0:T(8,128)S(1)} %convolution_multiply_fusion.1.mine, f32[512,1024]{1,0:T(8,128)S(1)} %convolution_multiply_fusion.other), custom_call_target="tpu_custom_call" | custom-call | flops 6291456 | bytes 4194304 | tf_op jit(solution)/shard_map/first_kernel/pallas_call | solution.py:186
  68.8 1.3 copy-done
  70.1 9.7 %all-to-all-start.2 = ((f32[16,8,128]{2,1,0:T(8,128)}), f32[16,8,128]{2,1,0:T(8,128)S(1)}, u32[]{:S(2)}, u32[]{:S(2)}) async-start(f32[16,8,128]{2,1,0:T(8,128)} %first_kernel.1), calls=%async_computation.2 | async-start | bytes 131072 | tf_op jit(solution)/shard_map/all_to_all | solution.py:224
  79.8 1.5 multiply_reduce_fusion
  81.3 6.3 %all-to-all-done.2.parts = f32[16,8,128]{2,1,0:T(8,128)S(1)} async-done(((f32[16,8,128]{2,1,0:T(8,128)}), f32[16,8,128]{2,1,0:T(8,128)S(1)}, u32[]{:S(2)}, u32[]{:S(2)}) %all-to-all-start.2) | async-done | bytes 65568 | tf_op jit(solution)/shard_map/all_to_all | solution.py:224
  87.6 1.6 copy-done.1
  89.2 1.5 target_kernel.3
  90.7 15.7 %all_to_all.40.parts = f32[32,8,128]{2,1,0:T(8,128)S(1)} all-to-all(f32[32,8,128]{2,1,0:T(8,128)S(1)} %get-tuple-element.20), channel_id=1, replica_groups=mesh['row'=32,'col'=16] {'row'}, dimensions={0} | all-to-all | bytes 262144 | tf_op jit(solution)/shard_map/all_to_all | solution.py:228
  106.5 1.2 source_kernel.2
  107.7 12.3 %all_to_all.41.parts = f32[16,8,128]{2,1,0:T(8,128)S(1)} all-to-all(f32[16,8,128]{2,1,0:T(8,128)S(1)} %source_kernel.2), channel_id=1, replica_groups=mesh['row'=32,'col'=16] {'col'}, dimensions={0} | all-to-all | bytes 131072 | tf_op jit(solution)/shard_map/all_to_all | solution.py:224
  120.0 1.6 target_kernel.4
  121.6 12.4 %all_to_all.42.parts = f32[32,8,128]{2,1,0:T(8,128)S(1)} all-to-all(f32[32,8,128]{2,1,0:T(8,128)S(1)} %get-tuple-element.21), channel_id=1, replica_groups=mesh['row'=32,'col'=16] {'row'}, dimensions={0} | all-to-all | bytes 262144 | tf_op jit(solution)/shard_map/all_to_all | solution.py:228
  134.0 1.2 source_kernel.3
  135.2 12.3 %all_to_all.43.parts = f32[16,8,128]{2,1,0:T(8,128)S(1)} all-to-all(f32[16,8,128]{2,1,0:T(8,128)S(1)} %source_kernel.3), channel_id=1, replica_groups=mesh['row'=32,'col'=16] {'col'}, dimensions={0} | all-to-all | bytes 131072 | tf_op jit(solution)/shard_map/all_to_all | solution.py:224
  147.5 1.7 %target_kernel.5 = (f32[32,8,128]{2,1,0:T(8,128)}, f32[8,128]{1,0:T(8,128)S(1)}) custom-call(f32[16,8,128]{2,1,0:T(8,128)S(1)} %all_to_all.43.parts, f32[8,128]{1,0:T(8,128)S(1)} %reshape.38.mass, f32[8,128]{1,0:T(8,128)S(1)} %pad_maximum_fusion.squares, f32[512,1024]{1,0:T(8,128)S(1)} %convolution_multiply_fusion.1.mine, f32[512,1024]{1,0:T(8,128)S(1)} %copy-done.2), custom_call_target="tpu_custom_call" | custom-call | flops 6291456 | bytes 4194304 | tf_op jit(solution)/shard_map/target_kernel/pallas_call | solution.py:186
  149.2 3.8 %all-to-all-start.7 = ((f32[32,8,128]{2,1,0:T(8,128)}), f32[32,8,128]{2,1,0:T(8,128)S(1)}, u32[]{:S(2)}, u32[]{:S(2)}) async-start(f32[32,8,128]{2,1,0:T(8,128)} %get-tuple-element.23), calls=%async_computation.7 | async-start | bytes 262144 | tf_op jit(solution)/shard_map/all_to_all | solution.py:228
  153.1 0.1 reshape.43
  153.1 0.7 reshape.44
  153.8 8.4 %all-to-all-done.7.parts = f32[32,8,128]{2,1,0:T(8,128)S(1)} async-done(((f32[32,8,128]{2,1,0:T(8,128)}), f32[32,8,128]{2,1,0:T(8,128)S(1)}, u32[]{:S(2)}, u32[]{:S(2)}) %all-to-all-start.7) | async-done | bytes 131104 | tf_op jit(solution)/shard_map/all_to_all | solution.py:228
  162.2 0.7 last_kernel.1
  (20 shorter events, 0.1 us)
Async XLA Ops:
  2.3 28.8 %all-to-all-start = ((bf16[8,32,1024]{2,1,0:T(8,128)(2,1)}), bf16[8,32,1024]{2,1,0:T(8,128)(2,1)S(1)}, u32[]{:S(2)}, u32[]{:S(2)}) async-start(bf16[8,32,1024]{2,1,0:T(8,128)(2,1)} %broadcast_in_dim.4), calls=%async_computation | async-start | bytes 1048576 | tf_op jit(solution)/shard_map/all_to_all | solution.py:42
  13.2 8.2 %collective-permute-start = (bf16[64,1024]{1,0:T(8,128)(2,1)}, bf16[64,1024]{1,0:T(8,128)(2,1)S(1)}, u32[]{:S(2)}, u32[]{:S(2)}) collective-permute-start(bf16[64,1024]{1,0:T(8,128)(2,1)} %refs_0_.1), channel_id=1, source_target_pairs={{0,2},{1,3},{2,4},{3,5},{4,6},{5,7},{6,8},{7,9},{8,10},{9,11},{10,... | collective-permute-start | bytes 393224 | tf_op jit(solution)/shard_map/ppermute | solution.py:30
  16.4 6.9 %collective-permute-start.2 = (bf16[64,1024]{1,0:T(8,128)(2,1)}, bf16[64,1024]{1,0:T(8,128)(2,1)S(1)}, u32[]{:S(2)}, u32[]{:S(2)}) collective-permute-start(bf16[64,1024]{1,0:T(8,128)(2,1)} %refs_0_.1), channel_id=1, source_target_pairs={{0,14},{1,15},{2,0},{3,1},{4,2},{5,3},{6,4},{7,5},{8,6},{9,7},{10,... | collective-permute-start | bytes 393224 | tf_op jit(solution)/shard_map/ppermute | solution.py:30
  21.4 7.2 %collective-permute-start.1 = (bf16[64,1024]{1,0:T(8,128)(2,1)S(1)}, bf16[64,1024]{1,0:T(8,128)(2,1)S(1)}, u32[]{:S(2)}, u32[]{:S(2)}) collective-permute-start(bf16[64,1024]{1,0:T(8,128)(2,1)S(1)} %collective-permute-done.refs_1_), channel_id=1, source_target_pairs={{0,2},{1,3},{2,4},{3,5},{4,6},{5,7},{6,8},{7,9},{8,10},{9,11},{10,... | collective-permute-start | bytes 393224 | tf_op jit(solution)/shard_map/ppermute | solution.py:30
  23.3 6.5 %collective-permute-start.3 = (bf16[64,1024]{1,0:T(8,128)(2,1)S(1)}, bf16[64,1024]{1,0:T(8,128)(2,1)S(1)}, u32[]{:S(2)}, u32[]{:S(2)}) collective-permute-start(bf16[64,1024]{1,0:T(8,128)(2,1)S(1)} %collective-permute-done.2.refs_2_), channel_id=1, source_target_pairs={{0,14},{1,15},{2,0},{3,1},{4,2},{5,3},{6,4},{7,5},{8,6},{9,7},{10,... | collective-permute-start | bytes 393224 | tf_op jit(solution)/shard_map/ppermute | solution.py:30
  28.6 13.4 %copy-start.4 = (bf16[64,1024]{1,0:T(8,128)(2,1)}, bf16[64,1024]{1,0:T(8,128)(2,1)S(1)}, u32[]{:S(2)}) copy-start(bf16[64,1024]{1,0:T(8,128)(2,1)S(1)} %collective-permute-done.1.refs_3_) | copy-start | bytes 393220
  29.8 7.1 %copy-start.6 = (bf16[64,1024]{1,0:T(8,128)(2,1)}, bf16[64,1024]{1,0:T(8,128)(2,1)S(1)}, u32[]{:S(2)}) copy-start(bf16[64,1024]{1,0:T(8,128)(2,1)S(1)} %collective-permute-done.3.refs_4_) | copy-start | bytes 393220
  32.8 18.4 %copy-start.3 = (bf16[64,1024]{1,0:T(8,128)(2,1)S(1)}, bf16[64,1024]{1,0:T(8,128)(2,1)}, u32[]{:S(2)}) copy-start(bf16[64,1024]{1,0:T(8,128)(2,1)} %refs_0_.1) | copy-start | bytes 393220
  32.8 28.9 %all-to-all-start.1 = ((bf16[4,256,1024]{2,1,0:T(8,128)(2,1)}), bf16[4,256,1024]{2,1,0:T(8,128)(2,1)S(1)}, u32[]{:S(2)}, u32[]{:S(2)}) async-start(bf16[4,256,1024]{2,1,0:T(8,128)(2,1)} %broadcast_in_dim.5), calls=%async_computation.1 | async-start | bytes 4194304 | tf_op jit(solution)/shard_map/all_to_all | solution.py:42
  36.9 7.0 %collective-permute-start.5 = (bf16[64,1024]{1,0:T(8,128)(2,1)S(1)}, bf16[64,1024]{1,0:T(8,128)(2,1)S(1)}, u32[]{:S(2)}, u32[]{:S(2)}) collective-permute-start(bf16[64,1024]{1,0:T(8,128)(2,1)S(1)} %collective-permute-done.3.refs_4_), channel_id=1, source_target_pairs={{0,14},{1,15},{2,0},{3,1},{4,2},{5,3},{6,4},{7,5},{8,6},{9,7},{10,... | collective-permute-start | bytes 393224 | tf_op jit(solution)/shard_map/ppermute | solution.py:30
  42.0 7.2 %collective-permute-start.4 = (bf16[64,1024]{1,0:T(8,128)(2,1)S(1)}, bf16[64,1024]{1,0:T(8,128)(2,1)S(1)}, u32[]{:S(2)}, u32[]{:S(2)}) collective-permute-start(bf16[64,1024]{1,0:T(8,128)(2,1)S(1)} %collective-permute-done.1.refs_3_), channel_id=1, source_target_pairs={{0,2},{1,3},{2,4},{3,5},{4,6},{5,7},{6,8},{7,9},{8,10},{9,11},{10,... | collective-permute-start | bytes 393224 | tf_op jit(solution)/shard_map/ppermute | solution.py:30
  43.9 7.2 %collective-permute-start.6 = (bf16[64,1024]{1,0:T(8,128)(2,1)S(1)}, bf16[64,1024]{1,0:T(8,128)(2,1)S(1)}, u32[]{:S(2)}, u32[]{:S(2)}) collective-permute-start(bf16[64,1024]{1,0:T(8,128)(2,1)S(1)} %collective-permute-done.5.refs_6_), channel_id=1, source_target_pairs={{0,14},{1,15},{2,0},{3,1},{4,2},{5,3},{6,4},{7,5},{8,6},{9,7},{10,... | collective-permute-start | bytes 393224 | tf_op jit(solution)/shard_map/ppermute | solution.py:30
  51.1 0.9 copy-start.5
  52.0 0.9 copy-start.7
  54.4 10.1 %collective-permute-start.7 = (bf16[512,1024]{1,0:T(8,128)(2,1)S(1)}, bf16[512,1024]{1,0:T(8,128)(2,1)}, u32[]{:S(2)}, u32[]{:S(2)}) collective-permute-start(bf16[512,1024]{1,0:T(8,128)(2,1)S(1)} %assemble.1), channel_id=1, source_target_pairs={{0,1},{1,0},{2,3},{3,2},{4,5},{5,4},{6,7},{7,6},{8,9},{9,8},{10,11... | collective-permute-start | bytes 3145736 | tf_op jit(solution)/shard_map/ppermute | solution.py:30
  68.8 1.3 copy-start
  70.1 17.5 %all-to-all-start.2 = ((f32[16,8,128]{2,1,0:T(8,128)}), f32[16,8,128]{2,1,0:T(8,128)S(1)}, u32[]{:S(2)}, u32[]{:S(2)}) async-start(f32[16,8,128]{2,1,0:T(8,128)} %first_kernel.1), calls=%async_computation.2 | async-start | bytes 131072 | tf_op jit(solution)/shard_map/all_to_all | solution.py:224
  87.6 1.6 copy-start.1
  89.2 17.3 %copy-start.2 = (f32[512,1024]{1,0:T(8,128)S(1)}, f32[512,1024]{1,0:T(8,128)}, u32[]{:S(2)}) copy-start(f32[512,1024]{1,0:T(8,128)} %copy-done) | copy-start | bytes 6291460
  149.2 13.0 %all-to-all-start.7 = ((f32[32,8,128]{2,1,0:T(8,128)}), f32[32,8,128]{2,1,0:T(8,128)S(1)}, u32[]{:S(2)}, u32[]{:S(2)}) async-start(f32[32,8,128]{2,1,0:T(8,128)} %get-tuple-element.23), calls=%async_computation.7 | async-start | bytes 262144 | tf_op jit(solution)/shard_map/all_to_all | solution.py:228

commit v3 on v2

--- a/solution.py
+++ b/solution.py
@@ -38,7 +38,16 @@
 
 
 def spread(values, count, lines):
-    copies = jnp.broadcast_to(values[None], (count,) + values.shape)
+    copies = pl.pallas_call(
+        copies_kernel,
+        out_shape=jax.ShapeDtypeStruct((count,) + values.shape, values.dtype),
+        in_specs=[ANY],
+        out_specs=ANY,
+        scratch_shapes=[pltpu.SemaphoreType.DMA((count,))],
+        compiler_params=PARAMS,
+        cost_estimate=pl.CostEstimate(flops=0, bytes_accessed=2**22, transcendentals=0),
+        name="copies",
+    )(values)
     out = lax.all_to_all(copies, "row", 0, 0, axis_index_groups=lines)
     return out.reshape((-1,) + values.shape[1:])
 
@@ -73,19 +82,14 @@
         copy.wait()
 
 
-def place_kernel(points, out, squares, sems):
-    made = []
-    for r in range(GROUPS):
-        rows = pl.ds(r * LANES, LANES)
-        made.append(pltpu.make_async_copy(points.at[rows], out.at[rows], sems.at[r]))
-        made[-1].start()
-    sums = []
-    for r in range(GROUPS):
-        made[r].wait()
-        square = jnp.square(out[pl.ds(r * LANES, LANES), :].astype(F32))
-        total = jnp.sum(square, axis=1, keepdims=True)
-        sums.append(jnp.broadcast_to(total, (LANES, LANES)).T[0:1])
-    squares[...] = jnp.concatenate(sums, axis=0)
+def copies_kernel(values, out, sems):
+    made = [
+        pltpu.make_async_copy(values, out.at[k], sems.at[k]) for k in range(out.shape[0])
+    ]
+    for copy in made:
+        copy.start()
+    for copy in made:
+        copy.wait()
 
 
 def columns(values, side):
@@ -144,7 +148,8 @@
 
 VMEM = pl.BlockSpec(memory_space=pltpu.VMEM)
 HBM = pl.BlockSpec(memory_space=pltpu.HBM)
-PARAMS = pltpu.CompilerParams(vmem_limit_bytes=16 * 2**20)
+ANY = pl.BlockSpec(memory_space=pl.ANY)
+PARAMS = pltpu.CompilerParams(vmem_limit_bytes=4 * 2**20)
 COST = pl.CostEstimate(flops=6 * N * N, bytes_accessed=4 * N * N, transcendentals=N * N)
 
 
@@ -166,22 +171,6 @@
 TALL = pltpu.VMEM((N, LANES), F32)
 
 
-def place(points):
-    return pl.pallas_call(
-        place_kernel,
-        out_shape=(
-            jax.ShapeDtypeStruct(points.shape, jnp.bfloat16),
-            jax.ShapeDtypeStruct(SMALL, F32),
-        ),
-        in_specs=[HBM],
-        out_specs=(VMEM, VMEM),
-        scratch_shapes=[pltpu.SemaphoreType.DMA((GROUPS,))],
-        compiler_params=PARAMS,
-        cost_estimate=COST,
-        name="place",
-    )(points)
-
-
 def call(kernel, shapes, scratch, *args):
     return pl.pallas_call(
         kernel,
@@ -216,7 +205,7 @@
     masses = core_first(source_logmass * LOG2E), (target_logmass * LOG2E).reshape(SMALL)
     mine, other, target, masses = gather_points(source_points, target_points, masses)
     source_mass, target_mass = masses
-    target, target_sq = place(target)
+    target_sq = squares(target)
     tiles = products(mine, target), products(other, target)
     (part,) = call(first_kernel, [(cols,) + SMALL], [WIDE], target_mass, target_sq, *tiles)
     source_sq = jnp.concatenate([squares(mine), squares(other)], axis=0)

time: 164 us -> 166 us (1.012)
  local copies, waits for them, and re-layouts: 8.95 us -> 4.69 us
  waiting for transfers between devices: 21 us -> 23.4 us
  matrix products: 3.81 us -> 6.08 us
  other arithmetic: 3.18 us -> 5.25 us
    broadcast_in_dim x2 -> x0, local copies, waits for them, and re-layouts: 3.3 us -> none  [spread(): copies = jnp.broadcast_to(values[None], (count,) + values.shape)]
    all_to_all x2, waiting for transfers between devices: 2.83 us -> 5.24 us  [spread(): out = lax.all_to_all(copies, 'row', 0, 0, axis_index_groups=lines)]
    dot_general x2, matrix products: 3.81 us -> 6.08 us  [products(): lax.dot_general(a, b, (((1,), (1,)), ((), ())), preferred_element_type=F32)]
    reduce_sum x2 -> x3, other arithmetic: 1.78 us -> 3.85 us  [squares(): return jnp.sum(jnp.square(points.astype(F32)), axis=1).reshape(-1, LANES)]
    unnamed x16 -> x10, local copies, waits for them, and re-layouts: 4.74 us -> 3.77 us
  transfers between devices with their start and end apart: 12 -> 12, of which waited for: 7 -> 7; matrix products, arithmetic and copies ran while one was open for 3% -> 5% of each run, Pallas kernels for 2% -> 1%
where the time goes in v3:
time: 166 us; the launch traced here: 165 us
  starting transfers between devices  59.6 us (36%)
  blocking collectives  52.3 us (32%)
  waiting for transfers between devices  23.4 us (14%)
  Pallas kernels  13.2 us (8%)
  matrix products  6.08 us (4%)
  other arithmetic  5.25 us (3%)
  local copies, waits for them, and re-layouts  4.69 us (3%)
    ppermute x8, starting transfers between devices, move_col(): return lax.ppermute(values, 'col', pairs)  30.9 us
    all_to_all x2, blocking collectives, local(): parts = lax.all_to_all(part, 'row', 0, 0)  27.6 us
    all_to_all x2, blocking collectives, local(): parts = lax.all_to_all(part, 'col', 0, 0)  24.7 us
    all_to_all x2, starting transfers between devices, spread(): out = lax.all_to_all(copies, 'row', 0, 0, axis_index_groups=lines)  15.5 us
    pallas_call x7, Pallas kernels, call(): pl.pallas_call(kernel, out_shape=[jax.ShapeDtypeStruct(shape, F32) for sh...  9.58 us
    all_to_all x1, starting transfers between devices, local(): parts = lax.all_to_all(part, 'col', 0, 0)  9.4 us
    all_to_all x1, waiting for transfers between devices, local(): parts = lax.all_to_all(part, 'row', 0, 0)  8.39 us
    all_to_all x1, waiting for transfers between devices, local(): parts = lax.all_to_all(part, 'col', 0, 0)  6.29 us
  transfers between devices with their start and end apart: 12, of which 7 were waited for; matrix products, arithmetic and copies ran while one was open for 5% of the time, Pallas kernels for 1%

profile of v3, /device:TPU:1, one launch (start us, length us, event | category | flops | bytes accessed | tf_op | source)
XLA Modules:
  0.0 165.4 jit_solution(17562746815226354989)
XLA Ops:
  0.6 0.8 copy-done.4
  1.5 0.9 copies.2
  2.3 10.9 %all-to-all-start = ((bf16[8,32,1024]{2,1,0:T(8,128)(2,1)}), bf16[8,32,1024]{2,1,0:T(8,128)(2,1)S(1)}, u32[]{:S(2)}, u32[]{:S(2)}) async-start(bf16[8,32,1024]{2,1,0:T(8,128)(2,1)} %copies.2), calls=%async_computation | async-start | bytes 1048576 | tf_op jit(solution)/shard_map/all_to_all | solution.py:51
  13.2 3.2 %collective-permute-start = (bf16[64,1024]{1,0:T(8,128)(2,1)}, bf16[64,1024]{1,0:T(8,128)(2,1)S(1)}, u32[]{:S(2)}, u32[]{:S(2)}) collective-permute-start(bf16[64,1024]{1,0:T(8,128)(2,1)} %refs_0_.1), channel_id=1, source_target_pairs={{0,2},{1,3},{2,4},{3,5},{4,6},{5,7},{6,8},{7,9},{8,10},{9,11},{10,... | collective-permute-start | bytes 393224 | tf_op jit(solution)/shard_map/ppermute | solution.py:30
  16.4 3.8 %collective-permute-start.2 = (bf16[64,1024]{1,0:T(8,128)(2,1)}, bf16[64,1024]{1,0:T(8,128)(2,1)S(1)}, u32[]{:S(2)}, u32[]{:S(2)}) collective-permute-start(bf16[64,1024]{1,0:T(8,128)(2,1)} %refs_0_.1), channel_id=1, source_target_pairs={{0,14},{1,15},{2,0},{3,1},{4,2},{5,3},{6,4},{7,5},{8,6},{9,7},{10,... | collective-permute-start | bytes 393224 | tf_op jit(solution)/shard_map/ppermute | solution.py:30
  20.2 0.7 broadcast_multiply_fusion
  20.9 0.1 reshape.40
  21.0 0.1 reshape.41.mass
  21.1 0.3 collective-permute-done.refs_1_
  21.4 1.9 %collective-permute-start.1 = (bf16[64,1024]{1,0:T(8,128)(2,1)S(1)}, bf16[64,1024]{1,0:T(8,128)(2,1)S(1)}, u32[]{:S(2)}, u32[]{:S(2)}) collective-permute-start(bf16[64,1024]{1,0:T(8,128)(2,1)S(1)} %collective-permute-done.refs_1_), channel_id=1, source_target_pairs={{0,2},{1,3},{2,4},{3,5},{4,6},{5,7},{6,8},{7,9},{8,10},{9,11},{10,... | collective-permute-start | bytes 393224 | tf_op jit(solution)/shard_map/ppermute | solution.py:30
  23.3 4.6 %collective-permute-start.3 = (bf16[64,1024]{1,0:T(8,128)(2,1)S(1)}, bf16[64,1024]{1,0:T(8,128)(2,1)S(1)}, u32[]{:S(2)}, u32[]{:S(2)}) collective-permute-start(bf16[64,1024]{1,0:T(8,128)(2,1)S(1)} %collective-permute-done.2.refs_2_), channel_id=1, source_target_pairs={{0,14},{1,15},{2,0},{3,1},{4,2},{5,3},{6,4},{7,5},{8,6},{9,7},{10,... | collective-permute-start | bytes 393224 | tf_op jit(solution)/shard_map/ppermute | solution.py:30
  27.9 0.7 multiply_bitcast_fusion.mass
  28.6 1.2 collective-permute-done.3.refs_4_
  29.8 1.3 all-to-all-done
  31.2 1.4 copies.3
  32.5 4.6 %all-to-all-start.1 = ((bf16[4,256,1024]{2,1,0:T(8,128)(2,1)}), bf16[4,256,1024]{2,1,0:T(8,128)(2,1)}, u32[]{:S(2)}, u32[]{:S(2)}) async-start(bf16[4,256,1024]{2,1,0:T(8,128)(2,1)} %copies.3), calls=%async_computation.1 | async-start | bytes 4194304 | tf_op jit(solution)/shard_map/all_to_all | solution.py:51
  37.1 5.1 %collective-permute-start.5 = (bf16[64,1024]{1,0:T(8,128)(2,1)S(1)}, bf16[64,1024]{1,0:T(8,128)(2,1)S(1)}, u32[]{:S(2)}, u32[]{:S(2)}) collective-permute-start(bf16[64,1024]{1,0:T(8,128)(2,1)S(1)} %collective-permute-done.3.refs_4_), channel_id=1, source_target_pairs={{0,14},{1,15},{2,0},{3,1},{4,2},{5,3},{6,4},{7,5},{8,6},{9,7},{10,... | collective-permute-start | bytes 393224 | tf_op jit(solution)/shard_map/ppermute | solution.py:30
  42.2 1.9 %collective-permute-start.4 = (bf16[64,1024]{1,0:T(8,128)(2,1)S(1)}, bf16[64,1024]{1,0:T(8,128)(2,1)S(1)}, u32[]{:S(2)}, u32[]{:S(2)}) collective-permute-start(bf16[64,1024]{1,0:T(8,128)(2,1)S(1)} %collective-permute-done.1.refs_3_), channel_id=1, source_target_pairs={{0,2},{1,3},{2,4},{3,5},{4,6},{5,7},{6,8},{7,9},{8,10},{9,11},{10,... | collective-permute-start | bytes 393224 | tf_op jit(solution)/shard_map/ppermute | solution.py:30
  44.2 5.4 %collective-permute-start.6 = (bf16[64,1024]{1,0:T(8,128)(2,1)S(1)}, bf16[64,1024]{1,0:T(8,128)(2,1)S(1)}, u32[]{:S(2)}, u32[]{:S(2)}) collective-permute-start(bf16[64,1024]{1,0:T(8,128)(2,1)S(1)} %collective-permute-done.5.refs_6_), channel_id=1, source_target_pairs={{0,14},{1,15},{2,0},{3,1},{4,2},{5,3},{6,4},{7,5},{8,6},{9,7},{10,... | collective-permute-start | bytes 393224 | tf_op jit(solution)/shard_map/ppermute | solution.py:30
  49.6 0.0 collective-permute-done.4.refs_5_
  49.6 1.9 %collective-permute-done.6.refs_7_ = bf16[64,1024]{1,0:T(8,128)(2,1)S(1)} collective-permute-done((bf16[64,1024]{1,0:T(8,128)(2,1)S(1)}, bf16[64,1024]{1,0:T(8,128)(2,1)S(1)}, u32[]{:S(2)}, u32[]{:S(2)}) %collective-permute-start.6) | collective-permute-done | bytes 131104 | tf_op jit(solution)/shard_map/ppermute | solution.py:30
  51.5 1.4 assemble.1
  52.9 5.1 %collective-permute-start.7 = (bf16[512,1024]{1,0:T(8,128)(2,1)S(1)}, bf16[512,1024]{1,0:T(8,128)(2,1)}, u32[]{:S(2)}, u32[]{:S(2)}) collective-permute-start(bf16[512,1024]{1,0:T(8,128)(2,1)S(1)} %assemble.1), channel_id=1, source_target_pairs={{0,1},{1,0},{2,3},{3,2},{4,5},{5,4},{6,7},{7,6},{8,9},{9,8},{10,11... | collective-permute-start | bytes 3145736 | tf_op jit(solution)/shard_map/ppermute | solution.py:30
  58.0 0.3 multiply_reduce_fusion.2
  58.3 3.9 %all-to-all-done.1 = bf16[4,256,1024]{2,1,0:T(8,128)(2,1)} async-done(((bf16[4,256,1024]{2,1,0:T(8,128)(2,1)}), bf16[4,256,1024]{2,1,0:T(8,128)(2,1)}, u32[]{:S(2)}, u32[]{:S(2)}) %all-to-all-start.1) | async-done | bytes 2097184 | tf_op jit(solution)/shard_map/all_to_all | solution.py:51
  62.2 2.1 %multiply_reduce_fusion = f32[4,256]{1,0:T(4,128)S(1)} fusion(bf16[4,256,1024]{2,1,0:T(8,128)(2,1)} %all-to-all-done.1), kind=kLoop, calls=%fused_computation | loop fusion | flops 3144704 | bytes 2101248 | tf_op jit(solution)/shard_map/reduce_sum | solution.py:192
  64.3 2.9 %convolution_multiply_fusion.1.mine = f32[512,1024]{1,0:T(8,128)S(1)} fusion(bf16[512,1024]{1,0:T(8,128)(2,1)S(1)} %assemble.1, bf16[1024,1024]{1,0:T(8,128)(2,1)} %bitcast.3), kind=kOutput, calls=%fused_computation.4 | convolution fusion | flops 1074266112 | bytes 5242880 | tf_op jit(solution)/shard_map/dot_general | solution.py:188
  67.2 3.2 %convolution_multiply_fusion.other = f32[512,1024]{1,0:T(8,128)S(1)} fusion(bf16[512,1024]{1,0:T(8,128)(2,1)} %collective-permute-done.7, bf16[1024,1024]{1,0:T(8,128)(2,1)} %bitcast.3), kind=kOutput, calls=%fused_computation.3 | convolution fusion | flops 1074266112 | bytes 5242880 | tf_op jit(solution)/shard_map/dot_general | solution.py:188
  70.4 1.8 %first_kernel.1 = f32[16,8,128]{2,1,0:T(8,128)} custom-call(f32[8,128]{1,0:T(8,128)S(1)} %multiply_bitcast_fusion.mass, f32[8,128]{1,0:T(8,128)S(1)} %reshape.43.squares, f32[512,1024]{1,0:T(8,128)S(1)} %convolution_multiply_fusion.1.mine, f32[512,1024]{1,0:T(8,128)S(1)} %convolution_multiply_fusion.other), custom_call_target="tpu_custom_call" | custom-call | flops 6291456 | bytes 4194304 | tf_op jit(solution)/shard_map/first_kernel/pallas_call | solution.py:175
  72.2 1.3 copy-done
  73.5 9.4 %all-to-all-start.2 = ((f32[16,8,128]{2,1,0:T(8,128)}), f32[16,8,128]{2,1,0:T(8,128)S(1)}, u32[]{:S(2)}, u32[]{:S(2)}) async-start(f32[16,8,128]{2,1,0:T(8,128)} %first_kernel.1), calls=%async_computation.2 | async-start | bytes 131072 | tf_op jit(solution)/shard_map/all_to_all | solution.py:213
  82.9 1.5 multiply_reduce_fusion.1
  84.4 6.3 %all-to-all-done.2.parts = f32[16,8,128]{2,1,0:T(8,128)S(1)} async-done(((f32[16,8,128]{2,1,0:T(8,128)}), f32[16,8,128]{2,1,0:T(8,128)S(1)}, u32[]{:S(2)}, u32[]{:S(2)}) %all-to-all-start.2) | async-done | bytes 65568 | tf_op jit(solution)/shard_map/all_to_all | solution.py:213
  90.7 1.6 copy-done.1
  92.3 1.5 target_kernel.3
  93.8 15.2 %all_to_all.40.parts = f32[32,8,128]{2,1,0:T(8,128)S(1)} all-to-all(f32[32,8,128]{2,1,0:T(8,128)S(1)} %get-tuple-element.16), channel_id=1, replica_groups=mesh['row'=32,'col'=16] {'row'}, dimensions={0} | all-to-all | bytes 262144 | tf_op jit(solution)/shard_map/all_to_all | solution.py:217
  109.0 1.2 source_kernel.2
  110.2 12.3 %all_to_all.41.parts = f32[16,8,128]{2,1,0:T(8,128)S(1)} all-to-all(f32[16,8,128]{2,1,0:T(8,128)S(1)} %source_kernel.2), channel_id=1, replica_groups=mesh['row'=32,'col'=16] {'col'}, dimensions={0} | all-to-all | bytes 131072 | tf_op jit(solution)/shard_map/all_to_all | solution.py:213
  122.5 1.6 target_kernel.4
  124.1 12.4 %all_to_all.42.parts = f32[32,8,128]{2,1,0:T(8,128)S(1)} all-to-all(f32[32,8,128]{2,1,0:T(8,128)S(1)} %get-tuple-element.17), channel_id=1, replica_groups=mesh['row'=32,'col'=16] {'row'}, dimensions={0} | all-to-all | bytes 262144 | tf_op jit(solution)/shard_map/all_to_all | solution.py:217
  136.5 1.2 source_kernel.3
  137.7 12.3 %all_to_all.43.parts = f32[16,8,128]{2,1,0:T(8,128)S(1)} all-to-all(f32[16,8,128]{2,1,0:T(8,128)S(1)} %source_kernel.3), channel_id=1, replica_groups=mesh['row'=32,'col'=16] {'col'}, dimensions={0} | all-to-all | bytes 131072 | tf_op jit(solution)/shard_map/all_to_all | solution.py:213
  150.0 1.7 %target_kernel.5 = (f32[32,8,128]{2,1,0:T(8,128)}, f32[8,128]{1,0:T(8,128)S(1)}) custom-call(f32[16,8,128]{2,1,0:T(8,128)S(1)} %all_to_all.43.parts, f32[8,128]{1,0:T(8,128)S(1)} %reshape.41.mass, f32[8,128]{1,0:T(8,128)S(1)} %pad_maximum_fusion.squares, f32[512,1024]{1,0:T(8,128)S(1)} %convolution_multiply_fusion.1.mine, f32[512,1024]{1,0:T(8,128)S(1)} %copy-done.2), custom_call_target="tpu_custom_call" | custom-call | flops 6291456 | bytes 4194304 | tf_op jit(solution)/shard_map/target_kernel/pallas_call | solution.py:175
  151.7 3.8 %all-to-all-start.7 = ((f32[32,8,128]{2,1,0:T(8,128)}), f32[32,8,128]{2,1,0:T(8,128)S(1)}, u32[]{:S(2)}, u32[]{:S(2)}) async-start(f32[32,8,128]{2,1,0:T(8,128)} %get-tuple-element.19), calls=%async_computation.7 | async-start | bytes 262144 | tf_op jit(solution)/shard_map/all_to_all | solution.py:217
  155.6 0.1 reshape.47
  155.7 0.7 reshape.48
  156.3 8.4 %all-to-all-done.7.parts = f32[32,8,128]{2,1,0:T(8,128)S(1)} async-done(((f32[32,8,128]{2,1,0:T(8,128)}), f32[32,8,128]{2,1,0:T(8,128)S(1)}, u32[]{:S(2)}, u32[]{:S(2)}) %all-to-all-start.7) | async-done | bytes 131104 | tf_op jit(solution)/shard_map/all_to_all | solution.py:217
  164.7 0.7 last_kernel.1
  (15 shorter events, 0.1 us)
Async XLA Ops:
  0.6 0.8 copy-start.4
  2.3 28.8 %all-to-all-start = ((bf16[8,32,1024]{2,1,0:T(8,128)(2,1)}), bf16[8,32,1024]{2,1,0:T(8,128)(2,1)S(1)}, u32[]{:S(2)}, u32[]{:S(2)}) async-start(bf16[8,32,1024]{2,1,0:T(8,128)(2,1)} %copies.2), calls=%async_computation | async-start | bytes 1048576 | tf_op jit(solution)/shard_map/all_to_all | solution.py:51
  13.2 8.2 %collective-permute-start = (bf16[64,1024]{1,0:T(8,128)(2,1)}, bf16[64,1024]{1,0:T(8,128)(2,1)S(1)}, u32[]{:S(2)}, u32[]{:S(2)}) collective-permute-start(bf16[64,1024]{1,0:T(8,128)(2,1)} %refs_0_.1), channel_id=1, source_target_pairs={{0,2},{1,3},{2,4},{3,5},{4,6},{5,7},{6,8},{7,9},{8,10},{9,11},{10,... | collective-permute-start | bytes 393224 | tf_op jit(solution)/shard_map/ppermute | solution.py:30
  16.4 6.9 %collective-permute-start.2 = (bf16[64,1024]{1,0:T(8,128)(2,1)}, bf16[64,1024]{1,0:T(8,128)(2,1)S(1)}, u32[]{:S(2)}, u32[]{:S(2)}) collective-permute-start(bf16[64,1024]{1,0:T(8,128)(2,1)} %refs_0_.1), channel_id=1, source_target_pairs={{0,14},{1,15},{2,0},{3,1},{4,2},{5,3},{6,4},{7,5},{8,6},{9,7},{10,... | collective-permute-start | bytes 393224 | tf_op jit(solution)/shard_map/ppermute | solution.py:30
  21.4 7.2 %collective-permute-start.1 = (bf16[64,1024]{1,0:T(8,128)(2,1)S(1)}, bf16[64,1024]{1,0:T(8,128)(2,1)S(1)}, u32[]{:S(2)}, u32[]{:S(2)}) collective-permute-start(bf16[64,1024]{1,0:T(8,128)(2,1)S(1)} %collective-permute-done.refs_1_), channel_id=1, source_target_pairs={{0,2},{1,3},{2,4},{3,5},{4,6},{5,7},{6,8},{7,9},{8,10},{9,11},{10,... | collective-permute-start | bytes 393224 | tf_op jit(solution)/shard_map/ppermute | solution.py:30
  23.3 6.5 %collective-permute-start.3 = (bf16[64,1024]{1,0:T(8,128)(2,1)S(1)}, bf16[64,1024]{1,0:T(8,128)(2,1)S(1)}, u32[]{:S(2)}, u32[]{:S(2)}) collective-permute-start(bf16[64,1024]{1,0:T(8,128)(2,1)S(1)} %collective-permute-done.2.refs_2_), channel_id=1, source_target_pairs={{0,14},{1,15},{2,0},{3,1},{4,2},{5,3},{6,4},{7,5},{8,6},{9,7},{10,... | collective-permute-start | bytes 393224 | tf_op jit(solution)/shard_map/ppermute | solution.py:30
  32.5 18.9 %copy-start.3 = (bf16[64,1024]{1,0:T(8,128)(2,1)S(1)}, bf16[64,1024]{1,0:T(8,128)(2,1)}, u32[]{:S(2)}) copy-start(bf16[64,1024]{1,0:T(8,128)(2,1)} %refs_0_.1) | copy-start | bytes 393220
  32.5 29.7 %all-to-all-start.1 = ((bf16[4,256,1024]{2,1,0:T(8,128)(2,1)}), bf16[4,256,1024]{2,1,0:T(8,128)(2,1)}, u32[]{:S(2)}, u32[]{:S(2)}) async-start(bf16[4,256,1024]{2,1,0:T(8,128)(2,1)} %copies.3), calls=%async_computation.1 | async-start | bytes 4194304 | tf_op jit(solution)/shard_map/all_to_all | solution.py:51
  37.1 7.0 %collective-permute-start.5 = (bf16[64,1024]{1,0:T(8,128)(2,1)S(1)}, bf16[64,1024]{1,0:T(8,128)(2,1)S(1)}, u32[]{:S(2)}, u32[]{:S(2)}) collective-permute-start(bf16[64,1024]{1,0:T(8,128)(2,1)S(1)} %collective-permute-done.3.refs_4_), channel_id=1, source_target_pairs={{0,14},{1,15},{2,0},{3,1},{4,2},{5,3},{6,4},{7,5},{8,6},{9,7},{10,... | collective-permute-start | bytes 393224 | tf_op jit(solution)/shard_map/ppermute | solution.py:30
  42.2 7.3 %collective-permute-start.4 = (bf16[64,1024]{1,0:T(8,128)(2,1)S(1)}, bf16[64,1024]{1,0:T(8,128)(2,1)S(1)}, u32[]{:S(2)}, u32[]{:S(2)}) collective-permute-start(bf16[64,1024]{1,0:T(8,128)(2,1)S(1)} %collective-permute-done.1.refs_3_), channel_id=1, source_target_pairs={{0,2},{1,3},{2,4},{3,5},{4,6},{5,7},{6,8},{7,9},{8,10},{9,11},{10,... | collective-permute-start | bytes 393224 | tf_op jit(solution)/shard_map/ppermute | solution.py:30
  44.2 7.3 %collective-permute-start.6 = (bf16[64,1024]{1,0:T(8,128)(2,1)S(1)}, bf16[64,1024]{1,0:T(8,128)(2,1)S(1)}, u32[]{:S(2)}, u32[]{:S(2)}) collective-permute-start(bf16[64,1024]{1,0:T(8,128)(2,1)S(1)} %collective-permute-done.5.refs_6_), channel_id=1, source_target_pairs={{0,14},{1,15},{2,0},{3,1},{4,2},{5,3},{6,4},{7,5},{8,6},{9,7},{10,... | collective-permute-start | bytes 393224 | tf_op jit(solution)/shard_map/ppermute | solution.py:30
  52.9 14.2 %collective-permute-start.7 = (bf16[512,1024]{1,0:T(8,128)(2,1)S(1)}, bf16[512,1024]{1,0:T(8,128)(2,1)}, u32[]{:S(2)}, u32[]{:S(2)}) collective-permute-start(bf16[512,1024]{1,0:T(8,128)(2,1)S(1)} %assemble.1), channel_id=1, source_target_pairs={{0,1},{1,0},{2,3},{3,2},{4,5},{5,4},{6,7},{7,6},{8,9},{9,8},{10,11... | collective-permute-start | bytes 3145736 | tf_op jit(solution)/shard_map/ppermute | solution.py:30
  72.2 1.3 copy-start
  73.5 17.2 %all-to-all-start.2 = ((f32[16,8,128]{2,1,0:T(8,128)}), f32[16,8,128]{2,1,0:T(8,128)S(1)}, u32[]{:S(2)}, u32[]{:S(2)}) async-start(f32[16,8,128]{2,1,0:T(8,128)} %first_kernel.1), calls=%async_computation.2 | async-start | bytes 131072 | tf_op jit(solution)/shard_map/all_to_all | solution.py:213
  90.7 1.6 copy-start.1
  92.3 16.7 %copy-start.2 = (f32[512,1024]{1,0:T(8,128)S(1)}, f32[512,1024]{1,0:T(8,128)}, u32[]{:S(2)}) copy-start(f32[512,1024]{1,0:T(8,128)} %copy-done) | copy-start | bytes 6291460
  151.7 13.0 %all-to-all-start.7 = ((f32[32,8,128]{2,1,0:T(8,128)}), f32[32,8,128]{2,1,0:T(8,128)S(1)}, u32[]{:S(2)}, u32[]{:S(2)}) async-start(f32[32,8,128]{2,1,0:T(8,128)} %get-tuple-element.19), calls=%async_computation.7 | async-start | bytes 262144 | tf_op jit(solution)/shard_map/all_to_all | solution.py:217

commit v4 on v2

--- a/solution.py
+++ b/solution.py
@@ -38,7 +38,16 @@
 
 
 def spread(values, count, lines):
-    copies = jnp.broadcast_to(values[None], (count,) + values.shape)
+    copies = pl.pallas_call(
+        copies_kernel,
+        out_shape=jax.ShapeDtypeStruct((count,) + values.shape, values.dtype),
+        in_specs=[HBM],
+        out_specs=HBM,
+        scratch_shapes=[pltpu.SemaphoreType.DMA((count,))],
+        compiler_params=PARAMS,
+        cost_estimate=pl.CostEstimate(flops=0, bytes_accessed=2**22, transcendentals=0),
+        name="copies",
+    )(values)
     out = lax.all_to_all(copies, "row", 0, 0, axis_index_groups=lines)
     return out.reshape((-1,) + values.shape[1:])
 
@@ -73,14 +82,25 @@
         copy.wait()
 
 
+def copies_kernel(values, out, sems):
+    made = [
+        pltpu.make_async_copy(values, out.at[k], sems.at[k]) for k in range(out.shape[0])
+    ]
+    for copy in made:
+        copy.start()
+    for copy in made:
+        copy.wait()
+
+
 def place_kernel(points, out, squares, sems):
     made = []
-    for r in range(GROUPS):
+    groups = squares.shape[0]
+    for r in range(groups):
         rows = pl.ds(r * LANES, LANES)
         made.append(pltpu.make_async_copy(points.at[rows], out.at[rows], sems.at[r]))
         made[-1].start()
     sums = []
-    for r in range(GROUPS):
+    for r in range(groups):
         made[r].wait()
         square = jnp.square(out[pl.ds(r * LANES, LANES), :].astype(F32))
         total = jnp.sum(square, axis=1, keepdims=True)
@@ -167,17 +187,20 @@
 
 
 def place(points):
+    groups = points.shape[0] // LANES
     return pl.pallas_call(
         place_kernel,
         out_shape=(
             jax.ShapeDtypeStruct(points.shape, jnp.bfloat16),
-            jax.ShapeDtypeStruct(SMALL, F32),
+            jax.ShapeDtypeStruct((groups, LANES), F32),
         ),
         in_specs=[HBM],
         out_specs=(VMEM, VMEM),
-        scratch_shapes=[pltpu.SemaphoreType.DMA((GROUPS,))],
-        compiler_params=PARAMS,
-        cost_estimate=COST,
+        scratch_shapes=[pltpu.SemaphoreType.DMA((groups,))],
+        compiler_params=PARAMS,
+        cost_estimate=pl.CostEstimate(
+            flops=2 * points.size, bytes_accessed=2 * points.size, transcendentals=0
+        ),
         name="place",
     )(points)
 
@@ -216,10 +239,12 @@
     masses = core_first(source_logmass * LOG2E), (target_logmass * LOG2E).reshape(SMALL)
     mine, other, target, masses = gather_points(source_points, target_points, masses)
     source_mass, target_mass = masses
+    other, other_sq = place(other)
+    source_sq = jnp.concatenate([squares(mine), other_sq], axis=0)
+    target, other, source_sq = lax.optimization_barrier((target, other, source_sq))
     target, target_sq = place(target)
     tiles = products(mine, target), products(other, target)
     (part,) = call(first_kernel, [(cols,) + SMALL], [WIDE], target_mass, target_sq, *tiles)
-    source_sq = jnp.concatenate([squares(mine), squares(other)], axis=0)
     for step in range(ITERS):
         parts = lax.all_to_all(part, "col", 0, 0)
         part, source_potential = call(

time: 164 us -> 163 us (level)
  blocking collectives: 52.9 us -> 71.9 us
  starting transfers between devices: 59.7 us -> 50.1 us
  waiting for transfers between devices: 21 us -> 15.2 us
  local copies, waits for them, and re-layouts: 8.95 us -> 4.55 us
  Pallas kernels: 12.6 us -> 15.1 us
    all_to_all x2 -> x3, blocking collectives: 24.7 us -> 40.3 us  [local(): parts = lax.all_to_all(part, 'col', 0, 0)]
    all_to_all x1 -> x0, starting transfers between devices: 9.68 us -> none  [local(): parts = lax.all_to_all(part, 'col', 0, 0)]
    all_to_all x1 -> x0, waiting for transfers between devices: 6.29 us -> none  [local(): parts = lax.all_to_all(part, 'col', 0, 0)]
    all_to_all x2, blocking collectives: 28.2 us -> 31.6 us  [local(): parts = lax.all_to_all(part, 'row', 0, 0)]
    broadcast_in_dim x2 -> x0, local copies, waits for them, and re-layouts: 3.3 us -> none  [spread(): copies = jnp.broadcast_to(values[None], (count,) + values.shape)]
    pallas_call x0 -> x2, Pallas kernels: none -> 2.25 us  [spread(): pl.pallas_call(copies_kernel, out_shape=jax.ShapeDtypeStruct((count,) + v...]
    ppermute x8, waiting for transfers between devices: 3.48 us -> 5.46 us  [move_col(): return lax.ppermute(values, 'col', pairs)]
  transfers between devices with their start and end apart: 12 -> 11, of which waited for: 7 -> 6; matrix products, arithmetic and copies ran while one was open for 3% -> 2% of each run, Pallas kernels for 2% -> 1%
where the time goes in v4:
time: 163 us; the launch traced here: 162 us
  blocking collectives  71.9 us (44%)
  starting transfers between devices  50.1 us (31%)
  waiting for transfers between devices  15.2 us (9%)
  Pallas kernels  15.1 us (9%)
  local copies, waits for them, and re-layouts  4.55 us (3%)
  matrix products  2.6 us (2%)
  other arithmetic  1.67 us (1%)
    all_to_all x3, blocking collectives, local(): parts = lax.all_to_all(part, 'col', 0, 0)  40.3 us
    all_to_all x2, blocking collectives, local(): parts = lax.all_to_all(part, 'row', 0, 0)  31.6 us
    ppermute x8, starting transfers between devices, move_col(): return lax.ppermute(values, 'col', pairs)  31.2 us
    all_to_all x2, starting transfers between devices, spread(): out = lax.all_to_all(copies, 'row', 0, 0, axis_index_groups=lines)  15 us
    pallas_call x7, Pallas kernels, call(): pl.pallas_call(kernel, out_shape=[jax.ShapeDtypeStruct(shape, F32) for sh...  9.06 us
    all_to_all x1, waiting for transfers between devices, local(): parts = lax.all_to_all(part, 'row', 0, 0)  8.39 us
    ppermute x8, waiting for transfers between devices, move_col(): return lax.ppermute(values, 'col', pairs)  5.46 us
    all_to_all x1, starting transfers between devices, local(): parts = lax.all_to_all(part, 'row', 0, 0)  3.84 us
  transfers between devices with their start and end apart: 11, of which 6 were waited for; matrix products, arithmetic and copies ran while one was open for 2% of the time, Pallas kernels for 1%

profile of v4, /device:TPU:1, one launch (start us, length us, event | category | flops | bytes accessed | tf_op | source)
XLA Modules:
  0.0 161.9 jit_solution(3146060640699055107)
XLA Ops:
  0.6 0.8 copy-done.5
  1.5 0.9 copies.2
  2.4 10.9 %all-to-all-start = ((bf16[8,32,1024]{2,1,0:T(8,128)(2,1)}), bf16[8,32,1024]{2,1,0:T(8,128)(2,1)S(1)}, u32[]{:S(2)}, u32[]{:S(2)}) async-start(bf16[8,32,1024]{2,1,0:T(8,128)(2,1)} %copies.2), calls=%async_computation | async-start | bytes 1048576 | tf_op jit(solution)/shard_map/all_to_all | solution.py:51
  13.2 3.2 %collective-permute-start = (bf16[64,1024]{1,0:T(8,128)(2,1)}, bf16[64,1024]{1,0:T(8,128)(2,1)S(1)}, u32[]{:S(2)}, u32[]{:S(2)}) collective-permute-start(bf16[64,1024]{1,0:T(8,128)(2,1)} %refs_0_.1), channel_id=1, source_target_pairs={{0,2},{1,3},{2,4},{3,5},{4,6},{5,7},{6,8},{7,9},{8,10},{9,11},{10,... | collective-permute-start | bytes 393224 | tf_op jit(solution)/shard_map/ppermute | solution.py:30
  16.4 3.8 %collective-permute-start.2 = (bf16[64,1024]{1,0:T(8,128)(2,1)}, bf16[64,1024]{1,0:T(8,128)(2,1)S(1)}, u32[]{:S(2)}, u32[]{:S(2)}) collective-permute-start(bf16[64,1024]{1,0:T(8,128)(2,1)} %refs_0_.1), channel_id=1, source_target_pairs={{0,14},{1,15},{2,0},{3,1},{4,2},{5,3},{6,4},{7,5},{8,6},{9,7},{10,... | collective-permute-start | bytes 393224 | tf_op jit(solution)/shard_map/ppermute | solution.py:30
  20.3 0.7 broadcast_multiply_fusion
  21.0 0.1 reshape.32
  21.0 0.1 reshape.33.mass
  21.1 0.3 collective-permute-done.refs_1_
  21.4 1.9 %collective-permute-start.1 = (bf16[64,1024]{1,0:T(8,128)(2,1)S(1)}, bf16[64,1024]{1,0:T(8,128)(2,1)S(1)}, u32[]{:S(2)}, u32[]{:S(2)}) collective-permute-start(bf16[64,1024]{1,0:T(8,128)(2,1)S(1)} %collective-permute-done.refs_1_), channel_id=1, source_target_pairs={{0,2},{1,3},{2,4},{3,5},{4,6},{5,7},{6,8},{7,9},{8,10},{9,11},{10,... | collective-permute-start | bytes 393224 | tf_op jit(solution)/shard_map/ppermute | solution.py:30
  23.4 4.6 %collective-permute-start.3 = (bf16[64,1024]{1,0:T(8,128)(2,1)S(1)}, bf16[64,1024]{1,0:T(8,128)(2,1)S(1)}, u32[]{:S(2)}, u32[]{:S(2)}) collective-permute-start(bf16[64,1024]{1,0:T(8,128)(2,1)S(1)} %collective-permute-done.2.refs_2_), channel_id=1, source_target_pairs={{0,14},{1,15},{2,0},{3,1},{4,2},{5,3},{6,4},{7,5},{8,6},{9,7},{10,... | collective-permute-start | bytes 393224 | tf_op jit(solution)/shard_map/ppermute | solution.py:30
  27.9 0.7 multiply_bitcast_fusion.mass
  28.6 1.2 collective-permute-done.3.refs_4_
  29.9 1.3 all-to-all-done
  31.2 1.4 copies.3
  32.6 4.2 %all-to-all-start.1 = ((bf16[4,256,1024]{2,1,0:T(8,128)(2,1)}), bf16[4,256,1024]{2,1,0:T(8,128)(2,1)S(1)}, u32[]{:S(2)}, u32[]{:S(2)}) async-start(bf16[4,256,1024]{2,1,0:T(8,128)(2,1)} %copies.3), calls=%async_computation.1 | async-start | bytes 4194304 | tf_op jit(solution)/shard_map/all_to_all | solution.py:51
  36.7 5.1 %collective-permute-start.5 = (bf16[64,1024]{1,0:T(8,128)(2,1)S(1)}, bf16[64,1024]{1,0:T(8,128)(2,1)S(1)}, u32[]{:S(2)}, u32[]{:S(2)}) collective-permute-start(bf16[64,1024]{1,0:T(8,128)(2,1)S(1)} %collective-permute-done.3.refs_4_), channel_id=1, source_target_pairs={{0,14},{1,15},{2,0},{3,1},{4,2},{5,3},{6,4},{7,5},{8,6},{9,7},{10,... | collective-permute-start | bytes 393224 | tf_op jit(solution)/shard_map/ppermute | solution.py:30
  41.8 1.9 %collective-permute-start.4 = (bf16[64,1024]{1,0:T(8,128)(2,1)S(1)}, bf16[64,1024]{1,0:T(8,128)(2,1)S(1)}, u32[]{:S(2)}, u32[]{:S(2)}) collective-permute-start(bf16[64,1024]{1,0:T(8,128)(2,1)S(1)} %collective-permute-done.1.refs_3_), channel_id=1, source_target_pairs={{0,2},{1,3},{2,4},{3,5},{4,6},{5,7},{6,8},{7,9},{8,10},{9,11},{10,... | collective-permute-start | bytes 393224 | tf_op jit(solution)/shard_map/ppermute | solution.py:30
  43.8 5.2 %collective-permute-start.6 = (bf16[64,1024]{1,0:T(8,128)(2,1)S(1)}, bf16[64,1024]{1,0:T(8,128)(2,1)S(1)}, u32[]{:S(2)}, u32[]{:S(2)}) collective-permute-start(bf16[64,1024]{1,0:T(8,128)(2,1)S(1)} %collective-permute-done.5.refs_6_), channel_id=1, source_target_pairs={{0,14},{1,15},{2,0},{3,1},{4,2},{5,3},{6,4},{7,5},{8,6},{9,7},{10,... | collective-permute-start | bytes 393224 | tf_op jit(solution)/shard_map/ppermute | solution.py:30
  49.0 0.0 collective-permute-done.4.refs_5_
  49.1 1.9 %collective-permute-done.6.refs_7_ = bf16[64,1024]{1,0:T(8,128)(2,1)S(1)} collective-permute-done((bf16[64,1024]{1,0:T(8,128)(2,1)S(1)}, bf16[64,1024]{1,0:T(8,128)(2,1)S(1)}, u32[]{:S(2)}, u32[]{:S(2)}) %collective-permute-start.6) | collective-permute-done | bytes 131104 | tf_op jit(solution)/shard_map/ppermute | solution.py:30
  51.0 0.9 copy-done.2
  51.9 0.9 copy-done.4
  52.8 1.4 assemble.1
  54.2 5.5 %collective-permute-start.7 = (bf16[512,1024]{1,0:T(8,128)(2,1)S(1)}, bf16[512,1024]{1,0:T(8,128)(2,1)S(1)}, u32[]{:S(2)}, u32[]{:S(2)}) collective-permute-start(bf16[512,1024]{1,0:T(8,128)(2,1)S(1)} %assemble.1), channel_id=1, source_target_pairs={{0,1},{1,0},{2,3},{3,2},{4,5},{5,4},{6,7},{7,6},{8,9},{9,8},{10,11... | collective-permute-start | bytes 3145736 | tf_op jit(solution)/shard_map/ppermute | solution.py:30
  59.7 0.3 multiply_reduce_fusion
  60.0 2.0 %collective-permute-done.7.points = bf16[512,1024]{1,0:T(8,128)(2,1)S(1)} collective-permute-done((bf16[512,1024]{1,0:T(8,128)(2,1)S(1)}, bf16[512,1024]{1,0:T(8,128)(2,1)S(1)}, u32[]{:S(2)}, u32[]{:S(2)}) %collective-permute-start.7) | collective-permute-done | bytes 1048608 | tf_op jit(solution)/shard_map/ppermute | solution.py:30
  62.0 0.8 place.2
  62.8 1.0 copy-done.6
  63.8 1.5 place.3
  65.3 1.3 convolution_multiply_fusion.1.mine
  66.6 1.3 convolution_multiply_fusion.other
  67.9 1.2 first_kernel.1
  69.1 15.6 %all_to_all.40.parts = f32[16,8,128]{2,1,0:T(8,128)S(1)} all-to-all(f32[16,8,128]{2,1,0:T(8,128)S(1)} %first_kernel.1), channel_id=1, replica_groups=mesh['row'=32,'col'=16] {'col'}, dimensions={0} | all-to-all | bytes 131072 | tf_op jit(solution)/shard_map/all_to_all | solution.py:249
  84.7 1.6 target_kernel.3
  86.3 19.2 %all_to_all.41.parts = f32[32,8,128]{2,1,0:T(8,128)S(1)} all-to-all(f32[32,8,128]{2,1,0:T(8,128)S(1)} %get-tuple-element.30), channel_id=1, replica_groups=mesh['row'=32,'col'=16] {'row'}, dimensions={0} | all-to-all | bytes 262144 | tf_op jit(solution)/shard_map/all_to_all | solution.py:253
  105.5 1.2 source_kernel.2
  106.7 12.3 %all_to_all.42.parts = f32[16,8,128]{2,1,0:T(8,128)S(1)} all-to-all(f32[16,8,128]{2,1,0:T(8,128)S(1)} %source_kernel.2), channel_id=1, replica_groups=mesh['row'=32,'col'=16] {'col'}, dimensions={0} | all-to-all | bytes 131072 | tf_op jit(solution)/shard_map/all_to_all | solution.py:249
  119.0 1.6 target_kernel.4
  120.6 12.4 %all_to_all.43.parts = f32[32,8,128]{2,1,0:T(8,128)S(1)} all-to-all(f32[32,8,128]{2,1,0:T(8,128)S(1)} %get-tuple-element.31), channel_id=1, replica_groups=mesh['row'=32,'col'=16] {'row'}, dimensions={0} | all-to-all | bytes 262144 | tf_op jit(solution)/shard_map/all_to_all | solution.py:253
  133.0 1.2 source_kernel.3
  134.2 12.3 %all_to_all.44.parts = f32[16,8,128]{2,1,0:T(8,128)S(1)} all-to-all(f32[16,8,128]{2,1,0:T(8,128)S(1)} %source_kernel.3), channel_id=1, replica_groups=mesh['row'=32,'col'=16] {'col'}, dimensions={0} | all-to-all | bytes 131072 | tf_op jit(solution)/shard_map/all_to_all | solution.py:249
  146.5 1.7 %target_kernel.5 = (f32[32,8,128]{2,1,0:T(8,128)}, f32[8,128]{1,0:T(8,128)S(1)}) custom-call(f32[16,8,128]{2,1,0:T(8,128)S(1)} %all_to_all.44.parts, f32[8,128]{1,0:T(8,128)S(1)} %reshape.33.mass, f32[8,128]{1,0:T(8,128)S(1)} %pad_maximum_fusion.squares, f32[512,1024]{1,0:T(8,128)S(1)} %convolution_multiply_fusion.1.mine, ...), custom_call_target="tpu_custom_call" | custom-call | flops 6291456 | bytes 4194304 | tf_op jit(solution)/shard_map/target_kernel/pallas_call | solution.py:209
  148.2 3.8 %all-to-all-start.7 = ((f32[32,8,128]{2,1,0:T(8,128)}), f32[32,8,128]{2,1,0:T(8,128)S(1)}, u32[]{:S(2)}, u32[]{:S(2)}) async-start(f32[32,8,128]{2,1,0:T(8,128)} %get-tuple-element.33), calls=%async_computation.7 | async-start | bytes 262144 | tf_op jit(solution)/shard_map/all_to_all | solution.py:253
  152.1 0.1 reshape.37
  152.2 0.7 reshape.38
  152.8 8.4 %all-to-all-done.7.parts = f32[32,8,128]{2,1,0:T(8,128)S(1)} async-done(((f32[32,8,128]{2,1,0:T(8,128)}), f32[32,8,128]{2,1,0:T(8,128)S(1)}, u32[]{:S(2)}, u32[]{:S(2)}) %all-to-all-start.7) | async-done | bytes 131104 | tf_op jit(solution)/shard_map/all_to_all | solution.py:253
  161.2 0.7 last_kernel.1
  (19 shorter events, 0.1 us)
Async XLA Ops:
  0.6 0.8 copy-start.5
  2.4 28.8 %all-to-all-start = ((bf16[8,32,1024]{2,1,0:T(8,128)(2,1)}), bf16[8,32,1024]{2,1,0:T(8,128)(2,1)S(1)}, u32[]{:S(2)}, u32[]{:S(2)}) async-start(bf16[8,32,1024]{2,1,0:T(8,128)(2,1)} %copies.2), calls=%async_computation | async-start | bytes 1048576 | tf_op jit(solution)/shard_map/all_to_all | solution.py:51
  13.2 8.2 %collective-permute-start = (bf16[64,1024]{1,0:T(8,128)(2,1)}, bf16[64,1024]{1,0:T(8,128)(2,1)S(1)}, u32[]{:S(2)}, u32[]{:S(2)}) collective-permute-start(bf16[64,1024]{1,0:T(8,128)(2,1)} %refs_0_.1), channel_id=1, source_target_pairs={{0,2},{1,3},{2,4},{3,5},{4,6},{5,7},{6,8},{7,9},{8,10},{9,11},{10,... | collective-permute-start | bytes 393224 | tf_op jit(solution)/shard_map/ppermute | solution.py:30
  16.4 6.9 %collective-permute-start.2 = (bf16[64,1024]{1,0:T(8,128)(2,1)}, bf16[64,1024]{1,0:T(8,128)(2,1)S(1)}, u32[]{:S(2)}, u32[]{:S(2)}) collective-permute-start(bf16[64,1024]{1,0:T(8,128)(2,1)} %refs_0_.1), channel_id=1, source_target_pairs={{0,14},{1,15},{2,0},{3,1},{4,2},{5,3},{6,4},{7,5},{8,6},{9,7},{10,... | collective-permute-start | bytes 393224 | tf_op jit(solution)/shard_map/ppermute | solution.py:30
  21.4 7.2 %collective-permute-start.1 = (bf16[64,1024]{1,0:T(8,128)(2,1)S(1)}, bf16[64,1024]{1,0:T(8,128)(2,1)S(1)}, u32[]{:S(2)}, u32[]{:S(2)}) collective-permute-start(bf16[64,1024]{1,0:T(8,128)(2,1)S(1)} %collective-permute-done.refs_1_), channel_id=1, source_target_pairs={{0,2},{1,3},{2,4},{3,5},{4,6},{5,7},{6,8},{7,9},{8,10},{9,11},{10,... | collective-permute-start | bytes 393224 | tf_op jit(solution)/shard_map/ppermute | solution.py:30
  23.4 6.5 %collective-permute-start.3 = (bf16[64,1024]{1,0:T(8,128)(2,1)S(1)}, bf16[64,1024]{1,0:T(8,128)(2,1)S(1)}, u32[]{:S(2)}, u32[]{:S(2)}) collective-permute-start(bf16[64,1024]{1,0:T(8,128)(2,1)S(1)} %collective-permute-done.2.refs_2_), channel_id=1, source_target_pairs={{0,14},{1,15},{2,0},{3,1},{4,2},{5,3},{6,4},{7,5},{8,6},{9,7},{10,... | collective-permute-start | bytes 393224 | tf_op jit(solution)/shard_map/ppermute | solution.py:30
  28.6 13.2 %copy-start.1 = (bf16[64,1024]{1,0:T(8,128)(2,1)}, bf16[64,1024]{1,0:T(8,128)(2,1)S(1)}, u32[]{:S(2)}) copy-start(bf16[64,1024]{1,0:T(8,128)(2,1)S(1)} %collective-permute-done.1.refs_3_) | copy-start | bytes 393220
  29.9 6.9 %copy-start.3 = (bf16[64,1024]{1,0:T(8,128)(2,1)}, bf16[64,1024]{1,0:T(8,128)(2,1)S(1)}, u32[]{:S(2)}) copy-start(bf16[64,1024]{1,0:T(8,128)(2,1)S(1)} %collective-permute-done.3.refs_4_) | copy-start | bytes 393220
  32.6 18.4 %copy-start = (bf16[64,1024]{1,0:T(8,128)(2,1)S(1)}, bf16[64,1024]{1,0:T(8,128)(2,1)}, u32[]{:S(2)}) copy-start(bf16[64,1024]{1,0:T(8,128)(2,1)} %refs_0_.1) | copy-start | bytes 393220
  32.6 31.2 %all-to-all-start.1 = ((bf16[4,256,1024]{2,1,0:T(8,128)(2,1)}), bf16[4,256,1024]{2,1,0:T(8,128)(2,1)S(1)}, u32[]{:S(2)}, u32[]{:S(2)}) async-start(bf16[4,256,1024]{2,1,0:T(8,128)(2,1)} %copies.3), calls=%async_computation.1 | async-start | bytes 4194304 | tf_op jit(solution)/shard_map/all_to_all | solution.py:51
  36.7 7.0 %collective-permute-start.5 = (bf16[64,1024]{1,0:T(8,128)(2,1)S(1)}, bf16[64,1024]{1,0:T(8,128)(2,1)S(1)}, u32[]{:S(2)}, u32[]{:S(2)}) collective-permute-start(bf16[64,1024]{1,0:T(8,128)(2,1)S(1)} %collective-permute-done.3.refs_4_), channel_id=1, source_target_pairs={{0,14},{1,15},{2,0},{3,1},{4,2},{5,3},{6,4},{7,5},{8,6},{9,7},{10,... | collective-permute-start | bytes 393224 | tf_op jit(solution)/shard_map/ppermute | solution.py:30
  41.8 7.2 %collective-permute-start.4 = (bf16[64,1024]{1,0:T(8,128)(2,1)S(1)}, bf16[64,1024]{1,0:T(8,128)(2,1)S(1)}, u32[]{:S(2)}, u32[]{:S(2)}) collective-permute-start(bf16[64,1024]{1,0:T(8,128)(2,1)S(1)} %collective-permute-done.1.refs_3_), channel_id=1, source_target_pairs={{0,2},{1,3},{2,4},{3,5},{4,6},{5,7},{6,8},{7,9},{8,10},{9,11},{10,... | collective-permute-start | bytes 393224 | tf_op jit(solution)/shard_map/ppermute | solution.py:30
  43.8 7.2 %collective-permute-start.6 = (bf16[64,1024]{1,0:T(8,128)(2,1)S(1)}, bf16[64,1024]{1,0:T(8,128)(2,1)S(1)}, u32[]{:S(2)}, u32[]{:S(2)}) collective-permute-start(bf16[64,1024]{1,0:T(8,128)(2,1)S(1)} %collective-permute-done.5.refs_6_), channel_id=1, source_target_pairs={{0,14},{1,15},{2,0},{3,1},{4,2},{5,3},{6,4},{7,5},{8,6},{9,7},{10,... | collective-permute-start | bytes 393224 | tf_op jit(solution)/shard_map/ppermute | solution.py:30
  51.0 0.9 copy-start.2
  51.9 0.9 copy-start.4
  54.2 7.7 %collective-permute-start.7 = (bf16[512,1024]{1,0:T(8,128)(2,1)S(1)}, bf16[512,1024]{1,0:T(8,128)(2,1)S(1)}, u32[]{:S(2)}, u32[]{:S(2)}) collective-permute-start(bf16[512,1024]{1,0:T(8,128)(2,1)S(1)} %assemble.1), channel_id=1, source_target_pairs={{0,1},{1,0},{2,3},{3,2},{4,5},{5,4},{6,7},{7,6},{8,9},{9,8},{10,11... | collective-permute-start | bytes 3145736 | tf_op jit(solution)/shard_map/ppermute | solution.py:30
  62.7 1.0 copy-start.6
  65.3 1.3 copy-start.7
  148.2 13.0 %all-to-all-start.7 = ((f32[32,8,128]{2,1,0:T(8,128)}), f32[32,8,128]{2,1,0:T(8,128)S(1)}, u32[]{:S(2)}, u32[]{:S(2)}) async-start(f32[32,8,128]{2,1,0:T(8,128)} %get-tuple-element.33), calls=%async_computation.7 | async-start | bytes 262144 | tf_op jit(solution)/shard_map/all_to_all | solution.py:253

commit v5 on v4

--- a/solution.py
+++ b/solution.py
@@ -108,6 +108,15 @@
     squares[...] = jnp.concatenate(sums, axis=0)
 
 
+def squares_kernel(points, same, squares):
+    sums = []
+    for r in range(GROUPS):
+        square = jnp.square(points[pl.ds(r * LANES, LANES), :].astype(F32))
+        total = jnp.sum(square, axis=1, keepdims=True)
+        sums.append(jnp.broadcast_to(total, (LANES, LANES)).T[0:1])
+    squares[...] = jnp.concatenate(sums, axis=0)
+
+
 def columns(values, side):
     for r in range(GROUPS):
         side[pl.ds(r * LANES, LANES), :] = jnp.broadcast_to(values[r : r + 1], (LANES, LANES)).T
@@ -127,14 +136,19 @@
 def over_targets(values, mine, other, part, flat):
     for r in range(GROUPS):
         flat[:, pl.ds(r * LANES, LANES)] = jnp.broadcast_to(values[r : r + 1], SMALL)
+    down = lax.broadcasted_iota(jnp.int32, (LANES, LANES), 0)
+    across = lax.broadcasted_iota(jnp.int32, (LANES, LANES), 1)
     rows = []
     for scaled in (mine, other):
         for r in range(GROUPS // NC):
-            tile = scaled[pl.ds(r * LANES, LANES), :] + flat[0:1, :]
-            top = jnp.max(tile, axis=1, keepdims=True)
-            log = top + jnp.log2(jnp.sum(jnp.exp2(tile - top), axis=1, keepdims=True))
-            rows.append(jnp.broadcast_to(log, (LANES, LANES)).T[0:1])
-    part[...] = jnp.broadcast_to(by_core(jnp.concatenate(rows, axis=0))[None], part.shape)
+            logs = []
+            for start in range(r * LANES, (r + 1) * LANES, 32):
+                tile = scaled[pl.ds(start, 32), :] + flat[0:1, :]
+                top = jnp.max(tile, axis=1, keepdims=True)
+                logs.append(top + jnp.log2(jnp.sum(jnp.exp2(tile - top), axis=1, keepdims=True)))
+            log = jnp.where(down == across, jnp.concatenate(logs, axis=0), 0.0)
+            rows.append(jnp.sum(log, axis=0, keepdims=True))
+    part[...] = by_core(jnp.concatenate(rows, axis=0))
 
 
 def first_kernel(mass, squares, mine, other, part, flat):
@@ -152,9 +166,17 @@
     rows = []
     for r in range(GROUPS):
         at = pl.ds(r * LANES, LANES)
-        tile = jnp.concatenate([mine[:, at], other[:, at]], axis=0) + side[...]
-        top = jnp.max(tile, axis=0, keepdims=True)
-        rows.append(top + jnp.log2(jnp.sum(jnp.exp2(tile - top), axis=0, keepdims=True)))
+        tops, sums = [], []
+        for half, scaled in enumerate((mine, other)):
+            for start in range(0, N // NC, 256):
+                tile = scaled[pl.ds(start, 256), at] + side[pl.ds(half * N // NC + start, 256), :]
+                tops.append(jnp.max(tile, axis=0, keepdims=True))
+                sums.append(jnp.sum(jnp.exp2(tile - tops[-1]), axis=0, keepdims=True))
+        top = tops[0]
+        for other_top in tops[1:]:
+            top = jnp.maximum(top, other_top)
+        total = sum(s * jnp.exp2(t - top) for s, t in zip(sums, tops))
+        rows.append(top + jnp.log2(total))
     part[...] = jnp.broadcast_to(jnp.concatenate(rows, axis=0)[None], part.shape)
 
 
@@ -205,6 +227,22 @@
     )(points)
 
 
+def in_place_squares(points):
+    return pl.pallas_call(
+        squares_kernel,
+        out_shape=(
+            jax.ShapeDtypeStruct(points.shape, jnp.bfloat16),
+            jax.ShapeDtypeStruct(SMALL, F32),
+        ),
+        in_specs=[VMEM],
+        out_specs=(VMEM, VMEM),
+        input_output_aliases={0: 0},
+        compiler_params=PARAMS,
+        cost_estimate=COST,
+        name="in_place_squares",
+    )(points)
+
+
 def call(kernel, shapes, scratch, *args):
     return pl.pallas_call(
         kernel,
@@ -218,6 +256,15 @@
     )(*args)
 
 
+def exchange_col(part):
+    there = move_col(part, lambda y, core: (y, 1 - core))
+    top = jnp.maximum(part, there)
+    merged = top + jnp.log2(jnp.exp2(part - top) + jnp.exp2(there - top))
+    lines = [[y * NC + core for y in range(NY)] for core in range(NC)]
+    copies = jnp.broadcast_to(merged[None], (NY,) + SMALL)
+    return lax.all_to_all(copies, "col", 0, 0, axis_index_groups=lines)
+
+
 def products(a, b):
     return SCALE * lax.dot_general(a, b, (((1,), (1,)), ((), ())), preferred_element_type=F32)
 
@@ -235,24 +282,24 @@
 
 
 def local(source_points, target_points, source_logmass, target_logmass):
-    rows, cols = lax.axis_size("row"), lax.axis_size("col")
+    rows = lax.axis_size("row")
     masses = core_first(source_logmass * LOG2E), (target_logmass * LOG2E).reshape(SMALL)
     mine, other, target, masses = gather_points(source_points, target_points, masses)
     source_mass, target_mass = masses
     other, other_sq = place(other)
     source_sq = jnp.concatenate([squares(mine), other_sq], axis=0)
     target, other, source_sq = lax.optimization_barrier((target, other, source_sq))
-    target, target_sq = place(target)
+    target, target_sq = in_place_squares(target)
     tiles = products(mine, target), products(other, target)
-    (part,) = call(first_kernel, [(cols,) + SMALL], [WIDE], target_mass, target_sq, *tiles)
+    (part,) = call(first_kernel, [SMALL], [WIDE], target_mass, target_sq, *tiles)
     for step in range(ITERS):
-        parts = lax.all_to_all(part, "col", 0, 0)
+        parts = exchange_col(part)
         part, source_potential = call(
             target_kernel, [(rows,) + SMALL, SMALL], [TALL], parts, source_mass, source_sq, *tiles
         )
         parts = lax.all_to_all(part, "row", 0, 0)
         if step < ITERS - 1:
-            (part,) = call(source_kernel, [(cols,) + SMALL], [WIDE], parts, target_mass, *tiles)
+            (part,) = call(source_kernel, [SMALL], [WIDE], parts, target_mass, *tiles)
     (target_potential,) = call(last_kernel, [SMALL], [], parts, target_sq)
     return y_first(source_potential), target_potential.reshape(-1)
 

time: 163 us -> 172 us (1.055)
  starting transfers between devices: 50.1 us -> 62.3 us
  blocking collectives: 71.9 us -> 64.2 us
  waiting for transfers between devices: 15.2 us -> 17.6 us
    ppermute x8 -> x11, starting transfers between devices: 31.2 us -> 43.5 us  [move_col(): return lax.ppermute(values, 'col', pairs)]
    all_to_all x3, blocking collectives: 40.3 us -> 32.5 us  [exchange_col(): return lax.all_to_all(copies, 'col', 0, 0, axis_index_groups=lines)]
    pallas_call x7, Pallas kernels: 9.06 us -> 11.6 us  [call(): pl.pallas_call(kernel, out_shape=[jax.ShapeDtypeStruct(shape, F32) for sh...]
    ppermute x8 -> x11, waiting for transfers between devices: 5.46 us -> 7.87 us  [move_col(): return lax.ppermute(values, 'col', pairs)]
  transfers between devices with their start and end apart: 11 -> 14, of which waited for: 6 -> 9; matrix products, arithmetic and copies ran while one was open for 2% -> 2% of each run, Pallas kernels for 1% -> 1%
where the time goes in v5:
time: 172 us; the launch traced here: 171 us
  blocking collectives  64.2 us (37%)
  starting transfers between devices  62.3 us (36%)
  waiting for transfers between devices  17.6 us (10%)
  Pallas kernels  16.7 us (10%)
  local copies, waits for them, and re-layouts  4.57 us (3%)
  matrix products  2.6 us (2%)
    ppermute x11, starting transfers between devices, move_col(): return lax.ppermute(values, 'col', pairs)  43.5 us
    all_to_all x3, blocking collectives, exchange_col(): return lax.all_to_all(copies, 'col', 0, 0, axis_index_groups=lines)  32.5 us
    all_to_all x2, blocking collectives, local(): parts = lax.all_to_all(part, 'row', 0, 0)  31.7 us
    all_to_all x2, starting transfers between devices, spread(): out = lax.all_to_all(copies, 'row', 0, 0, axis_index_groups=lines)  15 us
    pallas_call x7, Pallas kernels, call(): pl.pallas_call(kernel, out_shape=[jax.ShapeDtypeStruct(shape, F32) for sh...  11.6 us
    all_to_all x1, waiting for transfers between devices, local(): parts = lax.all_to_all(part, 'row', 0, 0)  8.42 us
    ppermute x11, waiting for transfers between devices, move_col(): return lax.ppermute(values, 'col', pairs)  7.87 us
    all_to_all x1, starting transfers between devices, local(): parts = lax.all_to_all(part, 'row', 0, 0)  3.84 us
  transfers between devices with their start and end apart: 14, of which 9 were waited for; matrix products, arithmetic and copies ran while one was open for 2% of the time, Pallas kernels for 1%

profile of v5, /device:TPU:1, one launch (start us, length us, event | category | flops | bytes accessed | tf_op | source)
XLA Modules:
  0.0 170.5 jit_solution(17767271264607947928)
XLA Ops:
  0.6 0.8 copy-done.5
  1.5 0.9 copies.2
  2.4 10.9 %all-to-all-start = ((bf16[8,32,1024]{2,1,0:T(8,128)(2,1)}), bf16[8,32,1024]{2,1,0:T(8,128)(2,1)S(1)}, u32[]{:S(2)}, u32[]{:S(2)}) async-start(bf16[8,32,1024]{2,1,0:T(8,128)(2,1)} %copies.2), calls=%async_computation | async-start | bytes 1048576 | tf_op jit(solution)/shard_map/all_to_all | solution.py:51
  13.2 3.2 %collective-permute-start = (bf16[64,1024]{1,0:T(8,128)(2,1)}, bf16[64,1024]{1,0:T(8,128)(2,1)S(1)}, u32[]{:S(2)}, u32[]{:S(2)}) collective-permute-start(bf16[64,1024]{1,0:T(8,128)(2,1)} %refs_0_.1), channel_id=1, source_target_pairs={{0,2},{1,3},{2,4},{3,5},{4,6},{5,7},{6,8},{7,9},{8,10},{9,11},{10,... | collective-permute-start | bytes 393224 | tf_op jit(solution)/shard_map/ppermute | solution.py:30
  16.4 3.8 %collective-permute-start.2 = (bf16[64,1024]{1,0:T(8,128)(2,1)}, bf16[64,1024]{1,0:T(8,128)(2,1)S(1)}, u32[]{:S(2)}, u32[]{:S(2)}) collective-permute-start(bf16[64,1024]{1,0:T(8,128)(2,1)} %refs_0_.1), channel_id=1, source_target_pairs={{0,14},{1,15},{2,0},{3,1},{4,2},{5,3},{6,4},{7,5},{8,6},{9,7},{10,... | collective-permute-start | bytes 393224 | tf_op jit(solution)/shard_map/ppermute | solution.py:30
  20.3 0.7 broadcast_multiply_fusion
  21.4 1.9 %collective-permute-start.1 = (bf16[64,1024]{1,0:T(8,128)(2,1)S(1)}, bf16[64,1024]{1,0:T(8,128)(2,1)S(1)}, u32[]{:S(2)}, u32[]{:S(2)}) collective-permute-start(bf16[64,1024]{1,0:T(8,128)(2,1)S(1)} %collective-permute-done.refs_1_), channel_id=1, source_target_pairs={{0,2},{1,3},{2,4},{3,5},{4,6},{5,7},{6,8},{7,9},{8,10},{9,11},{10,... | collective-permute-start | bytes 393224 | tf_op jit(solution)/shard_map/ppermute | solution.py:30
  23.4 4.6 %collective-permute-start.3 = (bf16[64,1024]{1,0:T(8,128)(2,1)S(1)}, bf16[64,1024]{1,0:T(8,128)(2,1)S(1)}, u32[]{:S(2)}, u32[]{:S(2)}) collective-permute-start(bf16[64,1024]{1,0:T(8,128)(2,1)S(1)} %collective-permute-done.2.refs_2_), channel_id=1, source_target_pairs={{0,14},{1,15},{2,0},{3,1},{4,2},{5,3},{6,4},{7,5},{8,6},{9,7},{10,... | collective-permute-start | bytes 393224 | tf_op jit(solution)/shard_map/ppermute | solution.py:30
  27.9 0.7 multiply_bitcast_fusion.mass
  28.6 1.2 collective-permute-done.3.refs_4_
  29.9 1.3 all-to-all-done
  31.2 1.4 copies.3
  32.6 4.2 %all-to-all-start.1 = ((bf16[4,256,1024]{2,1,0:T(8,128)(2,1)}), bf16[4,256,1024]{2,1,0:T(8,128)(2,1)S(1)}, u32[]{:S(2)}, u32[]{:S(2)}) async-start(bf16[4,256,1024]{2,1,0:T(8,128)(2,1)} %copies.3), calls=%async_computation.1 | async-start | bytes 4194304 | tf_op jit(solution)/shard_map/all_to_all | solution.py:51
  36.7 5.1 %collective-permute-start.5 = (bf16[64,1024]{1,0:T(8,128)(2,1)S(1)}, bf16[64,1024]{1,0:T(8,128)(2,1)S(1)}, u32[]{:S(2)}, u32[]{:S(2)}) collective-permute-start(bf16[64,1024]{1,0:T(8,128)(2,1)S(1)} %collective-permute-done.3.refs_4_), channel_id=1, source_target_pairs={{0,14},{1,15},{2,0},{3,1},{4,2},{5,3},{6,4},{7,5},{8,6},{9,7},{10,... | collective-permute-start | bytes 393224 | tf_op jit(solution)/shard_map/ppermute | solution.py:30
  41.8 1.9 %collective-permute-start.4 = (bf16[64,1024]{1,0:T(8,128)(2,1)S(1)}, bf16[64,1024]{1,0:T(8,128)(2,1)S(1)}, u32[]{:S(2)}, u32[]{:S(2)}) collective-permute-start(bf16[64,1024]{1,0:T(8,128)(2,1)S(1)} %collective-permute-done.1.refs_3_), channel_id=1, source_target_pairs={{0,2},{1,3},{2,4},{3,5},{4,6},{5,7},{6,8},{7,9},{8,10},{9,11},{10,... | collective-permute-start | bytes 393224 | tf_op jit(solution)/shard_map/ppermute | solution.py:30
  43.8 5.2 %collective-permute-start.6 = (bf16[64,1024]{1,0:T(8,128)(2,1)S(1)}, bf16[64,1024]{1,0:T(8,128)(2,1)S(1)}, u32[]{:S(2)}, u32[]{:S(2)}) collective-permute-start(bf16[64,1024]{1,0:T(8,128)(2,1)S(1)} %collective-permute-done.5.refs_6_), channel_id=1, source_target_pairs={{0,14},{1,15},{2,0},{3,1},{4,2},{5,3},{6,4},{7,5},{8,6},{9,7},{10,... | collective-permute-start | bytes 393224 | tf_op jit(solution)/shard_map/ppermute | solution.py:30
  49.1 1.9 %collective-permute-done.6.refs_7_ = bf16[64,1024]{1,0:T(8,128)(2,1)S(1)} collective-permute-done((bf16[64,1024]{1,0:T(8,128)(2,1)S(1)}, bf16[64,1024]{1,0:T(8,128)(2,1)S(1)}, u32[]{:S(2)}, u32[]{:S(2)}) %collective-permute-start.6) | collective-permute-done | bytes 131104 | tf_op jit(solution)/shard_map/ppermute | solution.py:30
  51.0 0.9 copy-done.2
  51.9 0.9 copy-done.4
  52.8 1.4 assemble.1
  54.2 5.5 %collective-permute-start.7 = (bf16[512,1024]{1,0:T(8,128)(2,1)S(1)}, bf16[512,1024]{1,0:T(8,128)(2,1)S(1)}, u32[]{:S(2)}, u32[]{:S(2)}) collective-permute-start(bf16[512,1024]{1,0:T(8,128)(2,1)S(1)} %assemble.1), channel_id=1, source_target_pairs={{0,1},{1,0},{2,3},{3,2},{4,5},{5,4},{6,7},{7,6},{8,9},{9,8},{10,11... | collective-permute-start | bytes 3145736 | tf_op jit(solution)/shard_map/ppermute | solution.py:30
  60.0 2.0 %collective-permute-done.7.points = bf16[512,1024]{1,0:T(8,128)(2,1)S(1)} collective-permute-done((bf16[512,1024]{1,0:T(8,128)(2,1)S(1)}, bf16[512,1024]{1,0:T(8,128)(2,1)S(1)}, u32[]{:S(2)}, u32[]{:S(2)}) %collective-permute-start.7) | collective-permute-done | bytes 1048608 | tf_op jit(solution)/shard_map/ppermute | solution.py:30
  62.0 0.8 place.1
  62.8 1.0 copy-done.6
  63.8 0.6 in_place_squares.1
  64.3 1.3 convolution_multiply_fusion.1.mine
  65.6 1.3 convolution_multiply_fusion.other
  66.9 2.2 %first_kernel.1 = f32[8,128]{1,0:T(8,128)S(1)} custom-call(f32[8,128]{1,0:T(8,128)S(1)} %multiply_bitcast_fusion.mass, f32[8,128]{1,0:T(8,128)S(1)} %get-tuple-element.25.squares, f32[512,1024]{1,0:T(8,128)S(1)} %convolution_multiply_fusion.1.mine, f32[512,1024]{1,0:T(8,128)S(1)} %convolution_multiply_fusion.other), custom_call_target="tpu_custom_call" | custom-call | flops 6291456 | bytes 4194304 | tf_op jit(solution)/shard_map/first_kernel/pallas_call | solution.py:247
  69.2 2.3 %collective-permute-start.8 = (f32[8,128]{1,0:T(8,128)S(1)}, f32[8,128]{1,0:T(8,128)S(1)}, u32[]{:S(2)}, u32[]{:S(2)}) collective-permute-start(f32[8,128]{1,0:T(8,128)S(1)} %first_kernel.1), channel_id=1, source_target_pairs={{0,1},{1,0},{2,3},{3,2},{4,5},{5,4},{6,7},{7,6},{8,9},{9,8},{10,11... | collective-permute-start | bytes 12296 | tf_op jit(solution)/shard_map/ppermute | solution.py:30
  71.5 0.8 collective-permute-done.8
  72.3 14.0 %all_to_all.40.parts = f32[8,8,128]{2,1,0:T(8,128)S(1)} all-to-all(f32[8,8,128]{2,1,0:T(8,128)S(1)} %broadcast_in_dim.6), channel_id=1, replica_groups={{0,2,4,6,8,10,12,14},{1,3,5,7,9,11,13,15},{16,18,20,22,24,26,28,30},{17..., dimensions={0} | all-to-all | bytes 65536 | tf_op jit(solution)/shard_map/all_to_all | solution.py:265
  86.3 1.5 target_kernel.3
  87.9 19.2 %all_to_all.41.parts = f32[32,8,128]{2,1,0:T(8,128)S(1)} all-to-all(f32[32,8,128]{2,1,0:T(8,128)S(1)} %get-tuple-element.30), channel_id=1, replica_groups=mesh['row'=32,'col'=16] {'row'}, dimensions={0} | all-to-all | bytes 262144 | tf_op jit(solution)/shard_map/all_to_all | solution.py:300
  107.1 2.0 %source_kernel.2 = f32[8,128]{1,0:T(8,128)S(1)} custom-call(f32[32,8,128]{2,1,0:T(8,128)S(1)} %all_to_all.41.parts, f32[8,128]{1,0:T(8,128)S(1)} %multiply_bitcast_fusion.mass, f32[512,1024]{1,0:T(8,128)S(1)} %convolution_multiply_fusion.1.mine, f32[512,1024]{1,0:T(8,128)S(1)} %convolution_multiply_fusion.other), custom_call_target="tpu_custom_call" | custom-call | flops 6291456 | bytes 4194304 | tf_op jit(solution)/shard_map/source_kernel/pallas_call | solution.py:247
  109.1 5.1 %collective-permute-start.9 = (f32[8,128]{1,0:T(8,128)S(1)}, f32[8,128]{1,0:T(8,128)S(1)}, u32[]{:S(2)}, u32[]{:S(2)}) collective-permute-start(f32[8,128]{1,0:T(8,128)S(1)} %source_kernel.2), channel_id=1, source_target_pairs={{0,1},{1,0},{2,3},{3,2},{4,5},{5,4},{6,7},{7,6},{8,9},{9,8},{10,11... | collective-permute-start | bytes 12296 | tf_op jit(solution)/shard_map/ppermute | solution.py:30
  114.2 0.8 collective-permute-done.9
  115.0 9.2 %all_to_all.42.parts = f32[8,8,128]{2,1,0:T(8,128)S(1)} all-to-all(f32[8,8,128]{2,1,0:T(8,128)S(1)} %broadcast_in_dim.7), channel_id=1, replica_groups={{0,2,4,6,8,10,12,14},{1,3,5,7,9,11,13,15},{16,18,20,22,24,26,28,30},{17..., dimensions={0} | all-to-all | bytes 65536 | tf_op jit(solution)/shard_map/all_to_all | solution.py:265
  124.3 1.5 target_kernel.4
  125.8 12.4 %all_to_all.43.parts = f32[32,8,128]{2,1,0:T(8,128)S(1)} all-to-all(f32[32,8,128]{2,1,0:T(8,128)S(1)} %get-tuple-element.31), channel_id=1, replica_groups=mesh['row'=32,'col'=16] {'row'}, dimensions={0} | all-to-all | bytes 262144 | tf_op jit(solution)/shard_map/all_to_all | solution.py:300
  138.3 2.0 %source_kernel.3 = f32[8,128]{1,0:T(8,128)S(1)} custom-call(f32[32,8,128]{2,1,0:T(8,128)S(1)} %all_to_all.43.parts, f32[8,128]{1,0:T(8,128)S(1)} %multiply_bitcast_fusion.mass, f32[512,1024]{1,0:T(8,128)S(1)} %convolution_multiply_fusion.1.mine, f32[512,1024]{1,0:T(8,128)S(1)} %convolution_multiply_fusion.other), custom_call_target="tpu_custom_call" | custom-call | flops 6291456 | bytes 4194304 | tf_op jit(solution)/shard_map/source_kernel/pallas_call | solution.py:247
  140.3 4.8 %collective-permute-start.10 = (f32[8,128]{1,0:T(8,128)S(1)}, f32[8,128]{1,0:T(8,128)S(1)}, u32[]{:S(2)}, u32[]{:S(2)}) collective-permute-start(f32[8,128]{1,0:T(8,128)S(1)} %source_kernel.3), channel_id=1, source_target_pairs={{0,1},{1,0},{2,3},{3,2},{4,5},{5,4},{6,7},{7,6},{8,9},{9,8},{10,11... | collective-permute-start | bytes 12296 | tf_op jit(solution)/shard_map/ppermute | solution.py:30
  145.1 0.8 collective-permute-done.10
  145.9 9.2 %all_to_all.44.parts = f32[8,8,128]{2,1,0:T(8,128)S(1)} all-to-all(f32[8,8,128]{2,1,0:T(8,128)S(1)} %broadcast_in_dim.8), channel_id=1, replica_groups={{0,2,4,6,8,10,12,14},{1,3,5,7,9,11,13,15},{16,18,20,22,24,26,28,30},{17..., dimensions={0} | all-to-all | bytes 65536 | tf_op jit(solution)/shard_map/all_to_all | solution.py:265
  155.2 1.7 target_kernel.5
  156.9 3.8 %all-to-all-start.7 = ((f32[32,8,128]{2,1,0:T(8,128)}), f32[32,8,128]{2,1,0:T(8,128)S(1)}, u32[]{:S(2)}, u32[]{:S(2)}) async-start(f32[32,8,128]{2,1,0:T(8,128)} %get-tuple-element.33), calls=%async_computation.7 | async-start | bytes 262144 | tf_op jit(solution)/shard_map/all_to_all | solution.py:300
  160.8 0.7 reshape.41
  161.5 8.4 %all-to-all-done.7.parts = f32[32,8,128]{2,1,0:T(8,128)S(1)} async-done(((f32[32,8,128]{2,1,0:T(8,128)}), f32[32,8,128]{2,1,0:T(8,128)S(1)}, u32[]{:S(2)}, u32[]{:S(2)}) %all-to-all-start.7) | async-done | bytes 131104 | tf_op jit(solution)/shard_map/all_to_all | solution.py:300
  169.9 0.7 last_kernel.1
  (31 shorter events, 1.0 us)
Async XLA Ops:
  0.6 0.8 copy-start.5
  2.4 28.8 %all-to-all-start = ((bf16[8,32,1024]{2,1,0:T(8,128)(2,1)}), bf16[8,32,1024]{2,1,0:T(8,128)(2,1)S(1)}, u32[]{:S(2)}, u32[]{:S(2)}) async-start(bf16[8,32,1024]{2,1,0:T(8,128)(2,1)} %copies.2), calls=%async_computation | async-start | bytes 1048576 | tf_op jit(solution)/shard_map/all_to_all | solution.py:51
  13.2 8.2 %collective-permute-start = (bf16[64,1024]{1,0:T(8,128)(2,1)}, bf16[64,1024]{1,0:T(8,128)(2,1)S(1)}, u32[]{:S(2)}, u32[]{:S(2)}) collective-permute-start(bf16[64,1024]{1,0:T(8,128)(2,1)} %refs_0_.1), channel_id=1, source_target_pairs={{0,2},{1,3},{2,4},{3,5},{4,6},{5,7},{6,8},{7,9},{8,10},{9,11},{10,... | collective-permute-start | bytes 393224 | tf_op jit(solution)/shard_map/ppermute | solution.py:30
  16.4 6.9 %collective-permute-start.2 = (bf16[64,1024]{1,0:T(8,128)(2,1)}, bf16[64,1024]{1,0:T(8,128)(2,1)S(1)}, u32[]{:S(2)}, u32[]{:S(2)}) collective-permute-start(bf16[64,1024]{1,0:T(8,128)(2,1)} %refs_0_.1), channel_id=1, source_target_pairs={{0,14},{1,15},{2,0},{3,1},{4,2},{5,3},{6,4},{7,5},{8,6},{9,7},{10,... | collective-permute-start | bytes 393224 | tf_op jit(solution)/shard_map/ppermute | solution.py:30
  21.4 7.2 %collective-permute-start.1 = (bf16[64,1024]{1,0:T(8,128)(2,1)S(1)}, bf16[64,1024]{1,0:T(8,128)(2,1)S(1)}, u32[]{:S(2)}, u32[]{:S(2)}) collective-permute-start(bf16[64,1024]{1,0:T(8,128)(2,1)S(1)} %collective-permute-done.refs_1_), channel_id=1, source_target_pairs={{0,2},{1,3},{2,4},{3,5},{4,6},{5,7},{6,8},{7,9},{8,10},{9,11},{10,... | collective-permute-start | bytes 393224 | tf_op jit(solution)/shard_map/ppermute | solution.py:30
  23.4 6.5 %collective-permute-start.3 = (bf16[64,1024]{1,0:T(8,128)(2,1)S(1)}, bf16[64,1024]{1,0:T(8,128)(2,1)S(1)}, u32[]{:S(2)}, u32[]{:S(2)}) collective-permute-start(bf16[64,1024]{1,0:T(8,128)(2,1)S(1)} %collective-permute-done.2.refs_2_), channel_id=1, source_target_pairs={{0,14},{1,15},{2,0},{3,1},{4,2},{5,3},{6,4},{7,5},{8,6},{9,7},{10,... | collective-permute-start | bytes 393224 | tf_op jit(solution)/shard_map/ppermute | solution.py:30
  28.6 13.2 %copy-start.1 = (bf16[64,1024]{1,0:T(8,128)(2,1)}, bf16[64,1024]{1,0:T(8,128)(2,1)S(1)}, u32[]{:S(2)}) copy-start(bf16[64,1024]{1,0:T(8,128)(2,1)S(1)} %collective-permute-done.1.refs_3_) | copy-start | bytes 393220
  29.9 6.9 %copy-start.3 = (bf16[64,1024]{1,0:T(8,128)(2,1)}, bf16[64,1024]{1,0:T(8,128)(2,1)S(1)}, u32[]{:S(2)}) copy-start(bf16[64,1024]{1,0:T(8,128)(2,1)S(1)} %collective-permute-done.3.refs_4_) | copy-start | bytes 393220
  32.6 18.4 %copy-start = (bf16[64,1024]{1,0:T(8,128)(2,1)S(1)}, bf16[64,1024]{1,0:T(8,128)(2,1)}, u32[]{:S(2)}) copy-start(bf16[64,1024]{1,0:T(8,128)(2,1)} %refs_0_.1) | copy-start | bytes 393220
  32.6 31.2 %all-to-all-start.1 = ((bf16[4,256,1024]{2,1,0:T(8,128)(2,1)}), bf16[4,256,1024]{2,1,0:T(8,128)(2,1)S(1)}, u32[]{:S(2)}, u32[]{:S(2)}) async-start(bf16[4,256,1024]{2,1,0:T(8,128)(2,1)} %copies.3), calls=%async_computation.1 | async-start | bytes 4194304 | tf_op jit(solution)/shard_map/all_to_all | solution.py:51
  36.7 7.0 %collective-permute-start.5 = (bf16[64,1024]{1,0:T(8,128)(2,1)S(1)}, bf16[64,1024]{1,0:T(8,128)(2,1)S(1)}, u32[]{:S(2)}, u32[]{:S(2)}) collective-permute-start(bf16[64,1024]{1,0:T(8,128)(2,1)S(1)} %collective-permute-done.3.refs_4_), channel_id=1, source_target_pairs={{0,14},{1,15},{2,0},{3,1},{4,2},{5,3},{6,4},{7,5},{8,6},{9,7},{10,... | collective-permute-start | bytes 393224 | tf_op jit(solution)/shard_map/ppermute | solution.py:30
  41.8 7.2 %collective-permute-start.4 = (bf16[64,1024]{1,0:T(8,128)(2,1)S(1)}, bf16[64,1024]{1,0:T(8,128)(2,1)S(1)}, u32[]{:S(2)}, u32[]{:S(2)}) collective-permute-start(bf16[64,1024]{1,0:T(8,128)(2,1)S(1)} %collective-permute-done.1.refs_3_), channel_id=1, source_target_pairs={{0,2},{1,3},{2,4},{3,5},{4,6},{5,7},{6,8},{7,9},{8,10},{9,11},{10,... | collective-permute-start | bytes 393224 | tf_op jit(solution)/shard_map/ppermute | solution.py:30
  43.8 7.2 %collective-permute-start.6 = (bf16[64,1024]{1,0:T(8,128)(2,1)S(1)}, bf16[64,1024]{1,0:T(8,128)(2,1)S(1)}, u32[]{:S(2)}, u32[]{:S(2)}) collective-permute-start(bf16[64,1024]{1,0:T(8,128)(2,1)S(1)} %collective-permute-done.5.refs_6_), channel_id=1, source_target_pairs={{0,14},{1,15},{2,0},{3,1},{4,2},{5,3},{6,4},{7,5},{8,6},{9,7},{10,... | collective-permute-start | bytes 393224 | tf_op jit(solution)/shard_map/ppermute | solution.py:30
  51.0 0.9 copy-start.2
  51.9 0.9 copy-start.4
  54.2 7.7 %collective-permute-start.7 = (bf16[512,1024]{1,0:T(8,128)(2,1)S(1)}, bf16[512,1024]{1,0:T(8,128)(2,1)S(1)}, u32[]{:S(2)}, u32[]{:S(2)}) collective-permute-start(bf16[512,1024]{1,0:T(8,128)(2,1)S(1)} %assemble.1), channel_id=1, source_target_pairs={{0,1},{1,0},{2,3},{3,2},{4,5},{5,4},{6,7},{7,6},{8,9},{9,8},{10,11... | collective-permute-start | bytes 3145736 | tf_op jit(solution)/shard_map/ppermute | solution.py:30
  62.7 1.0 copy-start.6
  64.3 1.3 copy-start.7
  69.2 3.1 %collective-permute-start.8 = (f32[8,128]{1,0:T(8,128)S(1)}, f32[8,128]{1,0:T(8,128)S(1)}, u32[]{:S(2)}, u32[]{:S(2)}) collective-permute-start(f32[8,128]{1,0:T(8,128)S(1)} %first_kernel.1), channel_id=1, source_target_pairs={{0,1},{1,0},{2,3},{3,2},{4,5},{5,4},{6,7},{7,6},{8,9},{9,8},{10,11... | collective-permute-start | bytes 12296 | tf_op jit(solution)/shard_map/ppermute | solution.py:30
  109.1 5.9 %collective-permute-start.9 = (f32[8,128]{1,0:T(8,128)S(1)}, f32[8,128]{1,0:T(8,128)S(1)}, u32[]{:S(2)}, u32[]{:S(2)}) collective-permute-start(f32[8,128]{1,0:T(8,128)S(1)} %source_kernel.2), channel_id=1, source_target_pairs={{0,1},{1,0},{2,3},{3,2},{4,5},{5,4},{6,7},{7,6},{8,9},{9,8},{10,11... | collective-permute-start | bytes 12296 | tf_op jit(solution)/shard_map/ppermute | solution.py:30
  140.3 5.6 %collective-permute-start.10 = (f32[8,128]{1,0:T(8,128)S(1)}, f32[8,128]{1,0:T(8,128)S(1)}, u32[]{:S(2)}, u32[]{:S(2)}) collective-permute-start(f32[8,128]{1,0:T(8,128)S(1)} %source_kernel.3), channel_id=1, source_target_pairs={{0,1},{1,0},{2,3},{3,2},{4,5},{5,4},{6,7},{7,6},{8,9},{9,8},{10,11... | collective-permute-start | bytes 12296 | tf_op jit(solution)/shard_map/ppermute | solution.py:30
  156.9 13.0 %all-to-all-start.7 = ((f32[32,8,128]{2,1,0:T(8,128)}), f32[32,8,128]{2,1,0:T(8,128)S(1)}, u32[]{:S(2)}, u32[]{:S(2)}) async-start(f32[32,8,128]{2,1,0:T(8,128)} %get-tuple-element.33), calls=%async_computation.7 | async-start | bytes 262144 | tf_op jit(solution)/shard_map/all_to_all | solution.py:300

commit v6 on v4

--- a/solution.py
+++ b/solution.py
@@ -52,20 +52,22 @@
     return out.reshape((-1,) + values.shape[1:])
 
 
-def gather_points(source_points, target_points, masses):
+def gather_points(source_points, target_points):
     along_z = [[x * NZ + z for z in range(NZ)] for x in range(NX)]
     along_x = [[x * NZ + z for x in range(NX)] for z in range(NZ)]
     line = spread(target_points, NZ, along_z)
     held = {0: source_points}
+    held[4] = move_col(source_points, lambda y, core: (y + 4, core))
     held[-1], held[1] = ring_step(source_points, source_points)
+    held[-1], held[1], held[4], line = lax.optimization_barrier(
+        (held[-1], held[1], held[4], line)
+    )
+    target = spread(line, NX, along_x)
     held[-2], held[2] = ring_step(held[-1], held[1])
-    held[-2], held[2], line, masses = lax.optimization_barrier((held[-2], held[2], line, masses))
-    target = spread(line, NX, along_x)
     held[-3], held[3] = ring_step(held[-2], held[2])
-    held[4] = move_col(held[3], lambda y, core: (y - 1, core))
     mine = assemble([held[place] for place in RING])
     other = move_col(mine, lambda y, core: (y, 1 - core))
-    return mine, other, target, masses
+    return mine, other, target
 
 
 def assemble_kernel(*refs):
@@ -108,6 +110,15 @@
     squares[...] = jnp.concatenate(sums, axis=0)
 
 
+def squares_kernel(points, same, squares):
+    sums = []
+    for r in range(GROUPS):
+        square = jnp.square(points[pl.ds(r * LANES, LANES), :].astype(F32))
+        total = jnp.sum(square, axis=1, keepdims=True)
+        sums.append(jnp.broadcast_to(total, (LANES, LANES)).T[0:1])
+    squares[...] = jnp.concatenate(sums, axis=0)
+
+
 def columns(values, side):
     for r in range(GROUPS):
         side[pl.ds(r * LANES, LANES), :] = jnp.broadcast_to(values[r : r + 1], (LANES, LANES)).T
@@ -205,6 +216,22 @@
     )(points)
 
 
+def in_place_squares(points):
+    return pl.pallas_call(
+        squares_kernel,
+        out_shape=(
+            jax.ShapeDtypeStruct(points.shape, jnp.bfloat16),
+            jax.ShapeDtypeStruct(SMALL, F32),
+        ),
+        in_specs=[VMEM],
+        out_specs=(VMEM, VMEM),
+        input_output_aliases={0: 0},
+        compiler_params=PARAMS,
+        cost_estimate=COST,
+        name="in_place_squares",
+    )(points)
+
+
 def call(kernel, shapes, scratch, *args):
     return pl.pallas_call(
         kernel,
@@ -236,13 +263,15 @@
 
 def local(source_points, target_points, source_logmass, target_logmass):
     rows, cols = lax.axis_size("row"), lax.axis_size("col")
-    masses = core_first(source_logmass * LOG2E), (target_logmass * LOG2E).reshape(SMALL)
-    mine, other, target, masses = gather_points(source_points, target_points, masses)
-    source_mass, target_mass = masses
+    mine, other, target = gather_points(source_points, target_points)
     other, other_sq = place(other)
     source_sq = jnp.concatenate([squares(mine), other_sq], axis=0)
-    target, other, source_sq = lax.optimization_barrier((target, other, source_sq))
-    target, target_sq = place(target)
+    source_mass = core_first(source_logmass * LOG2E)
+    target_mass = (target_logmass * LOG2E).reshape(SMALL)
+    target, other, source_sq, source_mass, target_mass = lax.optimization_barrier(
+        (target, other, source_sq, source_mass, target_mass)
+    )
+    target, target_sq = in_place_squares(target)
     tiles = products(mine, target), products(other, target)
     (part,) = call(first_kernel, [(cols,) + SMALL], [WIDE], target_mass, target_sq, *tiles)
     for step in range(ITERS):

time: 163 us -> 164 us (level)
  waiting for transfers between devices: 15.2 us -> 18.1 us
  starting transfers between devices: 50.1 us -> 52.4 us
    ppermute x8, waiting for transfers between devices: 5.46 us -> 8.95 us  [move_col(): return lax.ppermute(values, 'col', pairs)]
    ppermute x8, starting transfers between devices: 31.2 us -> 33.5 us  [move_col(): return lax.ppermute(values, 'col', pairs)]
  transfers between devices with their start and end apart: 11 -> 11, of which waited for: 6 -> 7; matrix products, arithmetic and copies ran while one was open for 2% -> 1% of each run, Pallas kernels for 1% -> 2%
where the time goes in v6:
time: 164 us; the launch traced here: 163 us
  blocking collectives  70.5 us (43%)
  starting transfers between devices  52.4 us (32%)
  waiting for transfers between devices  18.1 us (11%)
  Pallas kernels  15 us (9%)
  local copies, waits for them, and re-layouts  3.65 us (2%)
  matrix products  2.59 us (2%)
    all_to_all x3, blocking collectives, local(): parts = lax.all_to_all(part, 'col', 0, 0)  39 us
    ppermute x8, starting transfers between devices, move_col(): return lax.ppermute(values, 'col', pairs)  33.5 us
    all_to_all x2, blocking collectives, local(): parts = lax.all_to_all(part, 'row', 0, 0)  31.5 us
    all_to_all x2, starting transfers between devices, spread(): out = lax.all_to_all(copies, 'row', 0, 0, axis_index_groups=lines)  15 us
    pallas_call x7, Pallas kernels, call(): pl.pallas_call(kernel, out_shape=[jax.ShapeDtypeStruct(shape, F32) for sh...  9.06 us
    ppermute x8, waiting for transfers between devices, move_col(): return lax.ppermute(values, 'col', pairs)  8.95 us
    all_to_all x1, waiting for transfers between devices, local(): parts = lax.all_to_all(part, 'row', 0, 0)  8.39 us
    all_to_all x1, starting transfers between devices, local(): parts = lax.all_to_all(part, 'row', 0, 0)  3.84 us
  transfers between devices with their start and end apart: 11, of which 7 were waited for; matrix products, arithmetic and copies ran while one was open for 1% of the time, Pallas kernels for 2%

profile of v6, /device:TPU:1, one launch (start us, length us, event | category | flops | bytes accessed | tf_op | source)
XLA Modules:
  0.0 163.4 jit_solution(3124100192047091063)
XLA Ops:
  0.6 0.8 copy-done.3
  1.5 0.9 copies.2
  2.4 10.9 %all-to-all-start = ((bf16[8,32,1024]{2,1,0:T(8,128)(2,1)}), bf16[8,32,1024]{2,1,0:T(8,128)(2,1)S(1)}, u32[]{:S(2)}, u32[]{:S(2)}) async-start(bf16[8,32,1024]{2,1,0:T(8,128)(2,1)} %copies.2), calls=%async_computation | async-start | bytes 1048576 | tf_op jit(solution)/shard_map/all_to_all | solution.py:51
  13.2 5.1 %collective-permute-start.1 = (bf16[64,1024]{1,0:T(8,128)(2,1)}, bf16[64,1024]{1,0:T(8,128)(2,1)S(1)}, u32[]{:S(2)}, u32[]{:S(2)}) collective-permute-start(bf16[64,1024]{1,0:T(8,128)(2,1)} %refs_0_.1), channel_id=1, source_target_pairs={{0,14},{1,15},{2,0},{3,1},{4,2},{5,3},{6,4},{7,5},{8,6},{9,7},{10,... | collective-permute-start | bytes 393224 | tf_op jit(solution)/shard_map/ppermute | solution.py:30
  18.3 1.9 %collective-permute-start = (bf16[64,1024]{1,0:T(8,128)(2,1)}, bf16[64,1024]{1,0:T(8,128)(2,1)S(1)}, u32[]{:S(2)}, u32[]{:S(2)}) collective-permute-start(bf16[64,1024]{1,0:T(8,128)(2,1)} %refs_0_.1), channel_id=1, source_target_pairs={{0,2},{1,3},{2,4},{3,5},{4,6},{5,7},{6,8},{7,9},{8,10},{9,11},{10,... | collective-permute-start | bytes 393224 | tf_op jit(solution)/shard_map/ppermute | solution.py:30
  20.3 5.7 %collective-permute-start.2 = (bf16[64,1024]{1,0:T(8,128)(2,1)}, bf16[64,1024]{1,0:T(8,128)(2,1)S(1)}, u32[]{:S(2)}, u32[]{:S(2)}) collective-permute-start(bf16[64,1024]{1,0:T(8,128)(2,1)} %refs_0_.1), channel_id=1, source_target_pairs={{0,8},{1,9},{2,10},{3,11},{4,12},{5,13},{6,14},{7,15},{8,0},{9,1},... | collective-permute-start | bytes 393224 | tf_op jit(solution)/shard_map/ppermute | solution.py:30
  26.0 4.4 %collective-permute-done.2.refs_7_ = bf16[64,1024]{1,0:T(8,128)(2,1)S(1)} collective-permute-done((bf16[64,1024]{1,0:T(8,128)(2,1)}, bf16[64,1024]{1,0:T(8,128)(2,1)S(1)}, u32[]{:S(2)}, u32[]{:S(2)}) %collective-permute-start.2) | collective-permute-done | bytes 131104 | tf_op jit(solution)/shard_map/ppermute | solution.py:30
  30.4 0.8 all-to-all-done
  31.2 1.4 copies.3
  32.6 0.0 copy-start
  32.6 0.0 copy-start.6
  32.6 0.0 copy-start.7
  32.6 4.2 %all-to-all-start.1 = ((bf16[4,256,1024]{2,1,0:T(8,128)(2,1)}), bf16[4,256,1024]{2,1,0:T(8,128)(2,1)S(1)}, u32[]{:S(2)}, u32[]{:S(2)}) async-start(bf16[4,256,1024]{2,1,0:T(8,128)(2,1)} %copies.3), calls=%async_computation.1 | async-start | bytes 4194304 | tf_op jit(solution)/shard_map/all_to_all | solution.py:51
  36.8 3.2 %collective-permute-start.3 = (bf16[64,1024]{1,0:T(8,128)(2,1)S(1)}, bf16[64,1024]{1,0:T(8,128)(2,1)S(1)}, u32[]{:S(2)}, u32[]{:S(2)}) collective-permute-start(bf16[64,1024]{1,0:T(8,128)(2,1)S(1)} %collective-permute-done.refs_1_), channel_id=1, source_target_pairs={{0,2},{1,3},{2,4},{3,5},{4,6},{5,7},{6,8},{7,9},{8,10},{9,11},{10,... | collective-permute-start | bytes 393224 | tf_op jit(solution)/shard_map/ppermute | solution.py:30
  40.0 5.0 %collective-permute-start.4 = (bf16[64,1024]{1,0:T(8,128)(2,1)S(1)}, bf16[64,1024]{1,0:T(8,128)(2,1)S(1)}, u32[]{:S(2)}, u32[]{:S(2)}) collective-permute-start(bf16[64,1024]{1,0:T(8,128)(2,1)S(1)} %collective-permute-done.1.refs_2_), channel_id=1, source_target_pairs={{0,14},{1,15},{2,0},{3,1},{4,2},{5,3},{6,4},{7,5},{8,6},{9,7},{10,... | collective-permute-start | bytes 393224 | tf_op jit(solution)/shard_map/ppermute | solution.py:30
  45.0 0.7 collective-permute-done.3.refs_3_
  45.7 1.9 %collective-permute-start.5 = (bf16[64,1024]{1,0:T(8,128)(2,1)S(1)}, bf16[64,1024]{1,0:T(8,128)(2,1)S(1)}, u32[]{:S(2)}, u32[]{:S(2)}) collective-permute-start(bf16[64,1024]{1,0:T(8,128)(2,1)S(1)} %collective-permute-done.3.refs_3_), channel_id=1, source_target_pairs={{0,2},{1,3},{2,4},{3,5},{4,6},{5,7},{6,8},{7,9},{8,10},{9,11},{10,... | collective-permute-start | bytes 393224 | tf_op jit(solution)/shard_map/ppermute | solution.py:30
  47.6 4.6 %collective-permute-start.6 = (bf16[64,1024]{1,0:T(8,128)(2,1)S(1)}, bf16[64,1024]{1,0:T(8,128)(2,1)S(1)}, u32[]{:S(2)}, u32[]{:S(2)}) collective-permute-start(bf16[64,1024]{1,0:T(8,128)(2,1)S(1)} %collective-permute-done.4.refs_4_), channel_id=1, source_target_pairs={{0,14},{1,15},{2,0},{3,1},{4,2},{5,3},{6,4},{7,5},{8,6},{9,7},{10,... | collective-permute-start | bytes 393224 | tf_op jit(solution)/shard_map/ppermute | solution.py:30
  52.2 0.7 collective-permute-done.5.refs_5_
  52.9 1.2 collective-permute-done.6.refs_6_
  54.1 0.9 copy-done.2
  55.0 1.4 assemble.1
  56.5 6.1 %collective-permute-start.7 = (bf16[512,1024]{1,0:T(8,128)(2,1)S(1)}, bf16[512,1024]{1,0:T(8,128)(2,1)}, u32[]{:S(2)}, u32[]{:S(2)}) collective-permute-start(bf16[512,1024]{1,0:T(8,128)(2,1)S(1)} %assemble.1), channel_id=1, source_target_pairs={{0,1},{1,0},{2,3},{3,2},{4,5},{5,4},{6,7},{7,6},{8,9},{9,8},{10,11... | collective-permute-start | bytes 3145736 | tf_op jit(solution)/shard_map/ppermute | solution.py:30
  62.6 0.1 reshape.34
  62.7 0.1 reshape.35.mass
  62.8 0.3 multiply_reduce_fusion
  63.0 1.9 %collective-permute-done.7.points = bf16[512,1024]{1,0:T(8,128)(2,1)} collective-permute-done((bf16[512,1024]{1,0:T(8,128)(2,1)S(1)}, bf16[512,1024]{1,0:T(8,128)(2,1)}, u32[]{:S(2)}, u32[]{:S(2)}) %collective-permute-start.7) | collective-permute-done | bytes 1048608 | tf_op jit(solution)/shard_map/ppermute | solution.py:30
  65.0 1.6 %place.1 = (bf16[512,1024]{1,0:T(8,128)(2,1)S(1)}, f32[4,128]{1,0:T(4,128)S(1)}) custom-call(bf16[512,1024]{1,0:T(8,128)(2,1)} %collective-permute-done.7.points), custom_call_target="tpu_custom_call" | custom-call | flops 1048576 | bytes 1048576 | tf_op jit(solution)/shard_map/place/pallas_call | solution.py:202
  66.6 1.0 copy-done.4
  67.6 0.6 in_place_squares.1
  68.2 1.3 convolution_multiply_fusion.1.mine
  69.5 1.3 convolution_multiply_fusion.other
  70.8 1.2 first_kernel.1
  72.0 14.3 %all_to_all.40.parts = f32[16,8,128]{2,1,0:T(8,128)S(1)} all-to-all(f32[16,8,128]{2,1,0:T(8,128)S(1)} %first_kernel.1), channel_id=1, replica_groups=mesh['row'=32,'col'=16] {'col'}, dimensions={0} | all-to-all | bytes 131072 | tf_op jit(solution)/shard_map/all_to_all | solution.py:278
  86.3 1.6 target_kernel.3
  87.9 19.1 %all_to_all.41.parts = f32[32,8,128]{2,1,0:T(8,128)S(1)} all-to-all(f32[32,8,128]{2,1,0:T(8,128)S(1)} %get-tuple-element.32), channel_id=1, replica_groups=mesh['row'=32,'col'=16] {'row'}, dimensions={0} | all-to-all | bytes 262144 | tf_op jit(solution)/shard_map/all_to_all | solution.py:282
  107.0 1.2 source_kernel.2
  108.1 12.3 %all_to_all.42.parts = f32[16,8,128]{2,1,0:T(8,128)S(1)} all-to-all(f32[16,8,128]{2,1,0:T(8,128)S(1)} %source_kernel.2), channel_id=1, replica_groups=mesh['row'=32,'col'=16] {'col'}, dimensions={0} | all-to-all | bytes 131072 | tf_op jit(solution)/shard_map/all_to_all | solution.py:278
  120.5 1.6 target_kernel.4
  122.1 12.4 %all_to_all.43.parts = f32[32,8,128]{2,1,0:T(8,128)S(1)} all-to-all(f32[32,8,128]{2,1,0:T(8,128)S(1)} %get-tuple-element.33), channel_id=1, replica_groups=mesh['row'=32,'col'=16] {'row'}, dimensions={0} | all-to-all | bytes 262144 | tf_op jit(solution)/shard_map/all_to_all | solution.py:282
  134.5 1.2 source_kernel.3
  135.7 12.3 %all_to_all.44.parts = f32[16,8,128]{2,1,0:T(8,128)S(1)} all-to-all(f32[16,8,128]{2,1,0:T(8,128)S(1)} %source_kernel.3), channel_id=1, replica_groups=mesh['row'=32,'col'=16] {'col'}, dimensions={0} | all-to-all | bytes 131072 | tf_op jit(solution)/shard_map/all_to_all | solution.py:278
  148.0 1.7 %target_kernel.5 = (f32[32,8,128]{2,1,0:T(8,128)}, f32[8,128]{1,0:T(8,128)S(1)}) custom-call(f32[16,8,128]{2,1,0:T(8,128)S(1)} %all_to_all.44.parts, f32[8,128]{1,0:T(8,128)S(1)} %reshape.35.mass, f32[8,128]{1,0:T(8,128)S(1)} %pad_maximum_fusion.squares, f32[512,1024]{1,0:T(8,128)S(1)} %convolution_multiply_fusion.1.mine, ...), custom_call_target="tpu_custom_call" | custom-call | flops 6291456 | bytes 4194304 | tf_op jit(solution)/shard_map/target_kernel/pallas_call | solution.py:236
  149.7 3.8 %all-to-all-start.7 = ((f32[32,8,128]{2,1,0:T(8,128)}), f32[32,8,128]{2,1,0:T(8,128)S(1)}, u32[]{:S(2)}, u32[]{:S(2)}) async-start(f32[32,8,128]{2,1,0:T(8,128)} %get-tuple-element.35), calls=%async_computation.7 | async-start | bytes 262144 | tf_op jit(solution)/shard_map/all_to_all | solution.py:282
  153.6 0.1 reshape.37
  153.6 0.7 reshape.38
  154.3 8.4 %all-to-all-done.7.parts = f32[32,8,128]{2,1,0:T(8,128)S(1)} async-done(((f32[32,8,128]{2,1,0:T(8,128)}), f32[32,8,128]{2,1,0:T(8,128)S(1)}, u32[]{:S(2)}, u32[]{:S(2)}) %all-to-all-start.7) | async-done | bytes 131104 | tf_op jit(solution)/shard_map/all_to_all | solution.py:282
  162.7 0.7 last_kernel.1
  (19 shorter events, 0.1 us)
Async XLA Ops:
  0.6 0.8 copy-start.3
  2.4 28.8 %all-to-all-start = ((bf16[8,32,1024]{2,1,0:T(8,128)(2,1)}), bf16[8,32,1024]{2,1,0:T(8,128)(2,1)S(1)}, u32[]{:S(2)}, u32[]{:S(2)}) async-start(bf16[8,32,1024]{2,1,0:T(8,128)(2,1)} %copies.2), calls=%async_computation | async-start | bytes 1048576 | tf_op jit(solution)/shard_map/all_to_all | solution.py:51
  13.2 12.8 %collective-permute-start.1 = (bf16[64,1024]{1,0:T(8,128)(2,1)}, bf16[64,1024]{1,0:T(8,128)(2,1)S(1)}, u32[]{:S(2)}, u32[]{:S(2)}) collective-permute-start(bf16[64,1024]{1,0:T(8,128)(2,1)} %refs_0_.1), channel_id=1, source_target_pairs={{0,14},{1,15},{2,0},{3,1},{4,2},{5,3},{6,4},{7,5},{8,6},{9,7},{10,... | collective-permute-start | bytes 393224 | tf_op jit(solution)/shard_map/ppermute | solution.py:30
  18.3 7.7 %collective-permute-start = (bf16[64,1024]{1,0:T(8,128)(2,1)}, bf16[64,1024]{1,0:T(8,128)(2,1)S(1)}, u32[]{:S(2)}, u32[]{:S(2)}) collective-permute-start(bf16[64,1024]{1,0:T(8,128)(2,1)} %refs_0_.1), channel_id=1, source_target_pairs={{0,2},{1,3},{2,4},{3,5},{4,6},{5,7},{6,8},{7,9},{8,10},{9,11},{10,... | collective-permute-start | bytes 393224 | tf_op jit(solution)/shard_map/ppermute | solution.py:30
  20.3 10.1 %collective-permute-start.2 = (bf16[64,1024]{1,0:T(8,128)(2,1)}, bf16[64,1024]{1,0:T(8,128)(2,1)S(1)}, u32[]{:S(2)}, u32[]{:S(2)}) collective-permute-start(bf16[64,1024]{1,0:T(8,128)(2,1)} %refs_0_.1), channel_id=1, source_target_pairs={{0,8},{1,9},{2,10},{3,11},{4,12},{5,13},{6,14},{7,15},{8,0},{9,1},... | collective-permute-start | bytes 393224 | tf_op jit(solution)/shard_map/ppermute | solution.py:30
  30.4 2.2 %copy-start.1 = (bf16[64,1024]{1,0:T(8,128)(2,1)}, bf16[64,1024]{1,0:T(8,128)(2,1)S(1)}, u32[]{:S(2)}) copy-start(bf16[64,1024]{1,0:T(8,128)(2,1)S(1)} %collective-permute-done.2.refs_7_) | copy-start | bytes 393220
  32.6 21.5 %copy-start = (bf16[64,1024]{1,0:T(8,128)(2,1)S(1)}, bf16[64,1024]{1,0:T(8,128)(2,1)}, u32[]{:S(2)}) copy-start(bf16[64,1024]{1,0:T(8,128)(2,1)} %refs_0_.1) | copy-start | bytes 393220
  32.6 30.0 %copy-start.6 = (f32[1024]{0:T(1024)S(1)}, f32[1024]{0:T(1024)}, u32[]{:S(2)}) copy-start(f32[1024]{0:T(1024)} %param.6) | copy-start | bytes 12292
  32.6 30.2 %copy-start.7 = (f32[1024]{0:T(1024)S(1)}, f32[1024]{0:T(1024)}, u32[]{:S(2)}) copy-start(f32[1024]{0:T(1024)} %param.7) | copy-start | bytes 12292
  32.6 35.0 %all-to-all-start.1 = ((bf16[4,256,1024]{2,1,0:T(8,128)(2,1)}), bf16[4,256,1024]{2,1,0:T(8,128)(2,1)S(1)}, u32[]{:S(2)}, u32[]{:S(2)}) async-start(bf16[4,256,1024]{2,1,0:T(8,128)(2,1)} %copies.3), calls=%async_computation.1 | async-start | bytes 4194304 | tf_op jit(solution)/shard_map/all_to_all | solution.py:51
  36.8 8.9 %collective-permute-start.3 = (bf16[64,1024]{1,0:T(8,128)(2,1)S(1)}, bf16[64,1024]{1,0:T(8,128)(2,1)S(1)}, u32[]{:S(2)}, u32[]{:S(2)}) collective-permute-start(bf16[64,1024]{1,0:T(8,128)(2,1)S(1)} %collective-permute-done.refs_1_), channel_id=1, source_target_pairs={{0,2},{1,3},{2,4},{3,5},{4,6},{5,7},{6,8},{7,9},{8,10},{9,11},{10,... | collective-permute-start | bytes 393224 | tf_op jit(solution)/shard_map/ppermute | solution.py:30
  40.0 7.6 %collective-permute-start.4 = (bf16[64,1024]{1,0:T(8,128)(2,1)S(1)}, bf16[64,1024]{1,0:T(8,128)(2,1)S(1)}, u32[]{:S(2)}, u32[]{:S(2)}) collective-permute-start(bf16[64,1024]{1,0:T(8,128)(2,1)S(1)} %collective-permute-done.1.refs_2_), channel_id=1, source_target_pairs={{0,14},{1,15},{2,0},{3,1},{4,2},{5,3},{6,4},{7,5},{8,6},{9,7},{10,... | collective-permute-start | bytes 393224 | tf_op jit(solution)/shard_map/ppermute | solution.py:30
  45.7 7.2 %collective-permute-start.5 = (bf16[64,1024]{1,0:T(8,128)(2,1)S(1)}, bf16[64,1024]{1,0:T(8,128)(2,1)S(1)}, u32[]{:S(2)}, u32[]{:S(2)}) collective-permute-start(bf16[64,1024]{1,0:T(8,128)(2,1)S(1)} %collective-permute-done.3.refs_3_), channel_id=1, source_target_pairs={{0,2},{1,3},{2,4},{3,5},{4,6},{5,7},{6,8},{7,9},{8,10},{9,11},{10,... | collective-permute-start | bytes 393224 | tf_op jit(solution)/shard_map/ppermute | solution.py:30
  47.6 6.5 %collective-permute-start.6 = (bf16[64,1024]{1,0:T(8,128)(2,1)S(1)}, bf16[64,1024]{1,0:T(8,128)(2,1)S(1)}, u32[]{:S(2)}, u32[]{:S(2)}) collective-permute-start(bf16[64,1024]{1,0:T(8,128)(2,1)S(1)} %collective-permute-done.4.refs_4_), channel_id=1, source_target_pairs={{0,14},{1,15},{2,0},{3,1},{4,2},{5,3},{6,4},{7,5},{8,6},{9,7},{10,... | collective-permute-start | bytes 393224 | tf_op jit(solution)/shard_map/ppermute | solution.py:30
  54.1 0.9 copy-start.2
  56.5 8.5 %collective-permute-start.7 = (bf16[512,1024]{1,0:T(8,128)(2,1)S(1)}, bf16[512,1024]{1,0:T(8,128)(2,1)}, u32[]{:S(2)}, u32[]{:S(2)}) collective-permute-start(bf16[512,1024]{1,0:T(8,128)(2,1)S(1)} %assemble.1), channel_id=1, source_target_pairs={{0,1},{1,0},{2,3},{3,2},{4,5},{5,4},{6,7},{7,6},{8,9},{9,8},{10,11... | collective-permute-start | bytes 3145736 | tf_op jit(solution)/shard_map/ppermute | solution.py:30
  66.6 1.0 copy-start.4
  68.2 1.3 copy-start.5
  149.7 13.0 %all-to-all-start.7 = ((f32[32,8,128]{2,1,0:T(8,128)}), f32[32,8,128]{2,1,0:T(8,128)S(1)}, u32[]{:S(2)}, u32[]{:S(2)}) async-start(f32[32,8,128]{2,1,0:T(8,128)} %get-tuple-element.35), calls=%async_computation.7 | async-start | bytes 262144 | tf_op jit(solution)/shard_map/all_to_all | solution.py:282

commit v7 on v6

--- a/solution.py
+++ b/solution.py
@@ -43,7 +43,7 @@
         out_shape=jax.ShapeDtypeStruct((count,) + values.shape, values.dtype),
         in_specs=[HBM],
         out_specs=HBM,
-        scratch_shapes=[pltpu.SemaphoreType.DMA((count,))],
+        scratch_shapes=[pltpu.SemaphoreType.DMA((count, max(1, values.shape[0] // 64)))],
         compiler_params=PARAMS,
         cost_estimate=pl.CostEstimate(flops=0, bytes_accessed=2**22, transcendentals=0),
         name="copies",
@@ -57,14 +57,12 @@
     along_x = [[x * NZ + z for x in range(NX)] for z in range(NZ)]
     line = spread(target_points, NZ, along_z)
     held = {0: source_points}
-    held[4] = move_col(source_points, lambda y, core: (y + 4, core))
     held[-1], held[1] = ring_step(source_points, source_points)
-    held[-1], held[1], held[4], line = lax.optimization_barrier(
-        (held[-1], held[1], held[4], line)
-    )
+    held[-2], held[2] = ring_step(held[-1], held[1])
+    held[-2], held[2], line = lax.optimization_barrier((held[-2], held[2], line))
     target = spread(line, NX, along_x)
-    held[-2], held[2] = ring_step(held[-1], held[1])
     held[-3], held[3] = ring_step(held[-2], held[2])
+    held[4] = move_col(held[3], lambda y, core: (y - 1, core))
     mine = assemble([held[place] for place in RING])
     other = move_col(mine, lambda y, core: (y, 1 - core))
     return mine, other, target
@@ -85,8 +83,16 @@
 
 
 def copies_kernel(values, out, sems):
+    count, parts = sems.shape
+    rows = values.shape[0] // parts
     made = [
-        pltpu.make_async_copy(values, out.at[k], sems.at[k]) for k in range(out.shape[0])
+        pltpu.make_async_copy(
+            values.at[pl.ds(part * rows, rows)],
+            out.at[k, pl.ds(part * rows, rows)],
+            sems.at[k, part],
+        )
+        for k in range(count)
+        for part in range(parts)
     ]
     for copy in made:
         copy.start()

time: 164 us -> 163 us (level)
  starting transfers between devices: 52.4 us -> 50.1 us
    ppermute x8, starting transfers between devices: 33.5 us -> 31.2 us  [move_col(): return lax.ppermute(values, 'col', pairs)]
    ppermute x8, waiting for transfers between devices: 8.95 us -> 6.96 us  [move_col(): return lax.ppermute(values, 'col', pairs)]
    unnamed x16 -> x20, local copies, waits for them, and re-layouts: 2.75 us -> 3.64 us
where the time goes in v7:
time: 163 us; the launch traced here: 162 us
  blocking collectives  71.9 us (44%)
  starting transfers between devices  50.1 us (31%)
  waiting for transfers between devices  16.7 us (10%)
  Pallas kernels  15.1 us (9%)
  local copies, waits for them, and re-layouts  4.55 us (3%)
  matrix products  2.59 us (2%)
    all_to_all x3, blocking collectives, local(): parts = lax.all_to_all(part, 'col', 0, 0)  40.3 us
    all_to_all x2, blocking collectives, local(): parts = lax.all_to_all(part, 'row', 0, 0)  31.6 us
    ppermute x8, starting transfers between devices, move_col(): return lax.ppermute(values, 'col', pairs)  31.2 us
    all_to_all x2, starting transfers between devices, spread(): out = lax.all_to_all(copies, 'row', 0, 0, axis_index_groups=lines)  15 us
    pallas_call x7, Pallas kernels, call(): pl.pallas_call(kernel, out_shape=[jax.ShapeDtypeStruct(shape, F32) for sh...  9.07 us
    all_to_all x1, waiting for transfers between devices, local(): parts = lax.all_to_all(part, 'row', 0, 0)  8.39 us
    ppermute x8, waiting for transfers between devices, move_col(): return lax.ppermute(values, 'col', pairs)  6.96 us
    all_to_all x1, starting transfers between devices, local(): parts = lax.all_to_all(part, 'row', 0, 0)  3.85 us
  transfers between devices with their start and end apart: 11, of which 7 were waited for; matrix products, arithmetic and copies ran while one was open for 1% of the time, Pallas kernels for 2%

profile of v7, /device:TPU:1, one launch (start us, length us, event | category | flops | bytes accessed | tf_op | source)
XLA Modules:
  0.0 162.0 jit_solution(6563008577721588852)
XLA Ops:
  0.6 0.8 copy-done.5
  1.5 0.9 copies.2
  2.3 10.9 %all-to-all-start = ((bf16[8,32,1024]{2,1,0:T(8,128)(2,1)}), bf16[8,32,1024]{2,1,0:T(8,128)(2,1)S(1)}, u32[]{:S(2)}, u32[]{:S(2)}) async-start(bf16[8,32,1024]{2,1,0:T(8,128)(2,1)} %copies.2), calls=%async_computation | async-start | bytes 1048576 | tf_op jit(solution)/shard_map/all_to_all | solution.py:51
  13.2 3.2 %collective-permute-start = (bf16[64,1024]{1,0:T(8,128)(2,1)}, bf16[64,1024]{1,0:T(8,128)(2,1)S(1)}, u32[]{:S(2)}, u32[]{:S(2)}) collective-permute-start(bf16[64,1024]{1,0:T(8,128)(2,1)} %refs_0_.1), channel_id=1, source_target_pairs={{0,2},{1,3},{2,4},{3,5},{4,6},{5,7},{6,8},{7,9},{8,10},{9,11},{10,... | collective-permute-start | bytes 393224 | tf_op jit(solution)/shard_map/ppermute | solution.py:30
  16.4 3.8 %collective-permute-start.2 = (bf16[64,1024]{1,0:T(8,128)(2,1)}, bf16[64,1024]{1,0:T(8,128)(2,1)S(1)}, u32[]{:S(2)}, u32[]{:S(2)}) collective-permute-start(bf16[64,1024]{1,0:T(8,128)(2,1)} %refs_0_.1), channel_id=1, source_target_pairs={{0,14},{1,15},{2,0},{3,1},{4,2},{5,3},{6,4},{7,5},{8,6},{9,7},{10,... | collective-permute-start | bytes 393224 | tf_op jit(solution)/shard_map/ppermute | solution.py:30
  20.2 1.2 collective-permute-done.refs_1_
  21.4 1.9 %collective-permute-start.1 = (bf16[64,1024]{1,0:T(8,128)(2,1)S(1)}, bf16[64,1024]{1,0:T(8,128)(2,1)S(1)}, u32[]{:S(2)}, u32[]{:S(2)}) collective-permute-start(bf16[64,1024]{1,0:T(8,128)(2,1)S(1)} %collective-permute-done.refs_1_), channel_id=1, source_target_pairs={{0,2},{1,3},{2,4},{3,5},{4,6},{5,7},{6,8},{7,9},{8,10},{9,11},{10,... | collective-permute-start | bytes 393224 | tf_op jit(solution)/shard_map/ppermute | solution.py:30
  23.3 4.6 %collective-permute-start.3 = (bf16[64,1024]{1,0:T(8,128)(2,1)S(1)}, bf16[64,1024]{1,0:T(8,128)(2,1)S(1)}, u32[]{:S(2)}, u32[]{:S(2)}) collective-permute-start(bf16[64,1024]{1,0:T(8,128)(2,1)S(1)} %collective-permute-done.2.refs_2_), channel_id=1, source_target_pairs={{0,14},{1,15},{2,0},{3,1},{4,2},{5,3},{6,4},{7,5},{8,6},{9,7},{10,... | collective-permute-start | bytes 393224 | tf_op jit(solution)/shard_map/ppermute | solution.py:30
  27.9 0.4 collective-permute-done.1.refs_3_
  28.3 1.5 collective-permute-done.3.refs_4_
  29.9 1.3 all-to-all-done
  31.2 1.5 copies.3
  32.7 0.0 copy-start.8
  32.7 4.2 %all-to-all-start.1 = ((bf16[4,256,1024]{2,1,0:T(8,128)(2,1)}), bf16[4,256,1024]{2,1,0:T(8,128)(2,1)S(1)}, u32[]{:S(2)}, u32[]{:S(2)}) async-start(bf16[4,256,1024]{2,1,0:T(8,128)(2,1)} %copies.3), calls=%async_computation.1 | async-start | bytes 4194304 | tf_op jit(solution)/shard_map/all_to_all | solution.py:51
  36.9 5.1 %collective-permute-start.5 = (bf16[64,1024]{1,0:T(8,128)(2,1)S(1)}, bf16[64,1024]{1,0:T(8,128)(2,1)S(1)}, u32[]{:S(2)}, u32[]{:S(2)}) collective-permute-start(bf16[64,1024]{1,0:T(8,128)(2,1)S(1)} %collective-permute-done.3.refs_4_), channel_id=1, source_target_pairs={{0,14},{1,15},{2,0},{3,1},{4,2},{5,3},{6,4},{7,5},{8,6},{9,7},{10,... | collective-permute-start | bytes 393224 | tf_op jit(solution)/shard_map/ppermute | solution.py:30
  42.0 1.9 %collective-permute-start.4 = (bf16[64,1024]{1,0:T(8,128)(2,1)S(1)}, bf16[64,1024]{1,0:T(8,128)(2,1)S(1)}, u32[]{:S(2)}, u32[]{:S(2)}) collective-permute-start(bf16[64,1024]{1,0:T(8,128)(2,1)S(1)} %collective-permute-done.1.refs_3_), channel_id=1, source_target_pairs={{0,2},{1,3},{2,4},{3,5},{4,6},{5,7},{6,8},{7,9},{8,10},{9,11},{10,... | collective-permute-start | bytes 393224 | tf_op jit(solution)/shard_map/ppermute | solution.py:30
  43.9 5.2 %collective-permute-start.6 = (bf16[64,1024]{1,0:T(8,128)(2,1)S(1)}, bf16[64,1024]{1,0:T(8,128)(2,1)S(1)}, u32[]{:S(2)}, u32[]{:S(2)}) collective-permute-start(bf16[64,1024]{1,0:T(8,128)(2,1)S(1)} %collective-permute-done.5.refs_6_), channel_id=1, source_target_pairs={{0,14},{1,15},{2,0},{3,1},{4,2},{5,3},{6,4},{7,5},{8,6},{9,7},{10,... | collective-permute-start | bytes 393224 | tf_op jit(solution)/shard_map/ppermute | solution.py:30
  49.2 0.0 collective-permute-done.4.refs_5_
  49.2 1.9 %collective-permute-done.6.refs_7_ = bf16[64,1024]{1,0:T(8,128)(2,1)S(1)} collective-permute-done((bf16[64,1024]{1,0:T(8,128)(2,1)S(1)}, bf16[64,1024]{1,0:T(8,128)(2,1)S(1)}, u32[]{:S(2)}, u32[]{:S(2)}) %collective-permute-start.6) | collective-permute-done | bytes 131104 | tf_op jit(solution)/shard_map/ppermute | solution.py:30
  51.1 0.9 copy-done.2
  52.0 0.9 copy-done.4
  52.9 1.4 assemble.1
  54.3 5.5 %collective-permute-start.7 = (bf16[512,1024]{1,0:T(8,128)(2,1)S(1)}, bf16[512,1024]{1,0:T(8,128)(2,1)}, u32[]{:S(2)}, u32[]{:S(2)}) collective-permute-start(bf16[512,1024]{1,0:T(8,128)(2,1)S(1)} %assemble.1), channel_id=1, source_target_pairs={{0,1},{1,0},{2,3},{3,2},{4,5},{5,4},{6,7},{7,6},{8,9},{9,8},{10,11... | collective-permute-start | bytes 3145736 | tf_op jit(solution)/shard_map/ppermute | solution.py:30
  59.8 0.1 reshape.34
  59.9 0.1 reshape.35.mass
  60.0 0.3 multiply_reduce_fusion
  60.3 1.9 %collective-permute-done.7.points = bf16[512,1024]{1,0:T(8,128)(2,1)} collective-permute-done((bf16[512,1024]{1,0:T(8,128)(2,1)S(1)}, bf16[512,1024]{1,0:T(8,128)(2,1)}, u32[]{:S(2)}, u32[]{:S(2)}) %collective-permute-start.7) | collective-permute-done | bytes 1048608 | tf_op jit(solution)/shard_map/ppermute | solution.py:30
  62.2 1.6 %place.1 = (bf16[512,1024]{1,0:T(8,128)(2,1)S(1)}, f32[4,128]{1,0:T(4,128)S(1)}) custom-call(bf16[512,1024]{1,0:T(8,128)(2,1)} %collective-permute-done.7.points), custom_call_target="tpu_custom_call" | custom-call | flops 1048576 | bytes 1048576 | tf_op jit(solution)/shard_map/place/pallas_call | solution.py:208
  63.9 1.0 copy-done.6
  64.9 0.6 in_place_squares.1
  65.4 1.3 convolution_multiply_fusion.1.mine
  66.8 1.3 convolution_multiply_fusion.other
  68.0 1.2 first_kernel.1
  69.2 15.6 %all_to_all.40.parts = f32[16,8,128]{2,1,0:T(8,128)S(1)} all-to-all(f32[16,8,128]{2,1,0:T(8,128)S(1)} %first_kernel.1), channel_id=1, replica_groups=mesh['row'=32,'col'=16] {'col'}, dimensions={0} | all-to-all | bytes 131072 | tf_op jit(solution)/shard_map/all_to_all | solution.py:284
  84.8 1.6 target_kernel.3
  86.4 19.2 %all_to_all.41.parts = f32[32,8,128]{2,1,0:T(8,128)S(1)} all-to-all(f32[32,8,128]{2,1,0:T(8,128)S(1)} %get-tuple-element.30), channel_id=1, replica_groups=mesh['row'=32,'col'=16] {'row'}, dimensions={0} | all-to-all | bytes 262144 | tf_op jit(solution)/shard_map/all_to_all | solution.py:288
  105.6 1.2 source_kernel.2
  106.8 12.3 %all_to_all.42.parts = f32[16,8,128]{2,1,0:T(8,128)S(1)} all-to-all(f32[16,8,128]{2,1,0:T(8,128)S(1)} %source_kernel.2), channel_id=1, replica_groups=mesh['row'=32,'col'=16] {'col'}, dimensions={0} | all-to-all | bytes 131072 | tf_op jit(solution)/shard_map/all_to_all | solution.py:284
  119.1 1.6 target_kernel.4
  120.7 12.4 %all_to_all.43.parts = f32[32,8,128]{2,1,0:T(8,128)S(1)} all-to-all(f32[32,8,128]{2,1,0:T(8,128)S(1)} %get-tuple-element.31), channel_id=1, replica_groups=mesh['row'=32,'col'=16] {'row'}, dimensions={0} | all-to-all | bytes 262144 | tf_op jit(solution)/shard_map/all_to_all | solution.py:288
  133.1 1.2 source_kernel.3
  134.3 12.3 %all_to_all.44.parts = f32[16,8,128]{2,1,0:T(8,128)S(1)} all-to-all(f32[16,8,128]{2,1,0:T(8,128)S(1)} %source_kernel.3), channel_id=1, replica_groups=mesh['row'=32,'col'=16] {'col'}, dimensions={0} | all-to-all | bytes 131072 | tf_op jit(solution)/shard_map/all_to_all | solution.py:284
  146.6 1.7 %target_kernel.5 = (f32[32,8,128]{2,1,0:T(8,128)}, f32[8,128]{1,0:T(8,128)S(1)}) custom-call(f32[16,8,128]{2,1,0:T(8,128)S(1)} %all_to_all.44.parts, f32[8,128]{1,0:T(8,128)S(1)} %reshape.35.mass, f32[8,128]{1,0:T(8,128)S(1)} %pad_maximum_fusion.squares, f32[512,1024]{1,0:T(8,128)S(1)} %convolution_multiply_fusion.1.mine, ...), custom_call_target="tpu_custom_call" | custom-call | flops 6291456 | bytes 4194304 | tf_op jit(solution)/shard_map/target_kernel/pallas_call | solution.py:242
  148.4 3.9 %all-to-all-start.7 = ((f32[32,8,128]{2,1,0:T(8,128)}), f32[32,8,128]{2,1,0:T(8,128)S(1)}, u32[]{:S(2)}, u32[]{:S(2)}) async-start(f32[32,8,128]{2,1,0:T(8,128)} %get-tuple-element.33), calls=%async_computation.7 | async-start | bytes 262144 | tf_op jit(solution)/shard_map/all_to_all | solution.py:288
  152.2 0.1 reshape.37
  152.3 0.7 reshape.38
  153.0 8.4 %all-to-all-done.7.parts = f32[32,8,128]{2,1,0:T(8,128)S(1)} async-done(((f32[32,8,128]{2,1,0:T(8,128)}), f32[32,8,128]{2,1,0:T(8,128)S(1)}, u32[]{:S(2)}, u32[]{:S(2)}) %all-to-all-start.7) | async-done | bytes 131104 | tf_op jit(solution)/shard_map/all_to_all | solution.py:288
  161.4 0.7 last_kernel.1
  (23 shorter events, 0.1 us)
Async XLA Ops:
  0.6 0.8 copy-start.5
  2.3 28.8 %all-to-all-start = ((bf16[8,32,1024]{2,1,0:T(8,128)(2,1)}), bf16[8,32,1024]{2,1,0:T(8,128)(2,1)S(1)}, u32[]{:S(2)}, u32[]{:S(2)}) async-start(bf16[8,32,1024]{2,1,0:T(8,128)(2,1)} %copies.2), calls=%async_computation | async-start | bytes 1048576 | tf_op jit(solution)/shard_map/all_to_all | solution.py:51
  13.2 8.2 %collective-permute-start = (bf16[64,1024]{1,0:T(8,128)(2,1)}, bf16[64,1024]{1,0:T(8,128)(2,1)S(1)}, u32[]{:S(2)}, u32[]{:S(2)}) collective-permute-start(bf16[64,1024]{1,0:T(8,128)(2,1)} %refs_0_.1), channel_id=1, source_target_pairs={{0,2},{1,3},{2,4},{3,5},{4,6},{5,7},{6,8},{7,9},{8,10},{9,11},{10,... | collective-permute-start | bytes 393224 | tf_op jit(solution)/shard_map/ppermute | solution.py:30
  16.4 6.9 %collective-permute-start.2 = (bf16[64,1024]{1,0:T(8,128)(2,1)}, bf16[64,1024]{1,0:T(8,128)(2,1)S(1)}, u32[]{:S(2)}, u32[]{:S(2)}) collective-permute-start(bf16[64,1024]{1,0:T(8,128)(2,1)} %refs_0_.1), channel_id=1, source_target_pairs={{0,14},{1,15},{2,0},{3,1},{4,2},{5,3},{6,4},{7,5},{8,6},{9,7},{10,... | collective-permute-start | bytes 393224 | tf_op jit(solution)/shard_map/ppermute | solution.py:30
  21.4 6.9 %collective-permute-start.1 = (bf16[64,1024]{1,0:T(8,128)(2,1)S(1)}, bf16[64,1024]{1,0:T(8,128)(2,1)S(1)}, u32[]{:S(2)}, u32[]{:S(2)}) collective-permute-start(bf16[64,1024]{1,0:T(8,128)(2,1)S(1)} %collective-permute-done.refs_1_), channel_id=1, source_target_pairs={{0,2},{1,3},{2,4},{3,5},{4,6},{5,7},{6,8},{7,9},{8,10},{9,11},{10,... | collective-permute-start | bytes 393224 | tf_op jit(solution)/shard_map/ppermute | solution.py:30
  23.3 6.5 %collective-permute-start.3 = (bf16[64,1024]{1,0:T(8,128)(2,1)S(1)}, bf16[64,1024]{1,0:T(8,128)(2,1)S(1)}, u32[]{:S(2)}, u32[]{:S(2)}) collective-permute-start(bf16[64,1024]{1,0:T(8,128)(2,1)S(1)} %collective-permute-done.2.refs_2_), channel_id=1, source_target_pairs={{0,14},{1,15},{2,0},{3,1},{4,2},{5,3},{6,4},{7,5},{8,6},{9,7},{10,... | collective-permute-start | bytes 393224 | tf_op jit(solution)/shard_map/ppermute | solution.py:30
  28.3 13.6 %copy-start.1 = (bf16[64,1024]{1,0:T(8,128)(2,1)}, bf16[64,1024]{1,0:T(8,128)(2,1)S(1)}, u32[]{:S(2)}) copy-start(bf16[64,1024]{1,0:T(8,128)(2,1)S(1)} %collective-permute-done.1.refs_3_) | copy-start | bytes 393220
  29.9 7.0 %copy-start.3 = (bf16[64,1024]{1,0:T(8,128)(2,1)}, bf16[64,1024]{1,0:T(8,128)(2,1)S(1)}, u32[]{:S(2)}) copy-start(bf16[64,1024]{1,0:T(8,128)(2,1)S(1)} %collective-permute-done.3.refs_4_) | copy-start | bytes 393220
  32.7 18.4 %copy-start = (bf16[64,1024]{1,0:T(8,128)(2,1)S(1)}, bf16[64,1024]{1,0:T(8,128)(2,1)}, u32[]{:S(2)}) copy-start(bf16[64,1024]{1,0:T(8,128)(2,1)} %refs_0_.1) | copy-start | bytes 393220
  32.7 27.1 %copy-start.8 = (f32[1024]{0:T(1024)S(1)}, f32[1024]{0:T(1024)}, u32[]{:S(2)}) copy-start(f32[1024]{0:T(1024)} %param.6) | copy-start | bytes 12292
  32.7 27.3 %copy-start.9 = (f32[1024]{0:T(1024)S(1)}, f32[1024]{0:T(1024)}, u32[]{:S(2)}) copy-start(f32[1024]{0:T(1024)} %param.7) | copy-start | bytes 12292
  32.7 32.2 %all-to-all-start.1 = ((bf16[4,256,1024]{2,1,0:T(8,128)(2,1)}), bf16[4,256,1024]{2,1,0:T(8,128)(2,1)S(1)}, u32[]{:S(2)}, u32[]{:S(2)}) async-start(bf16[4,256,1024]{2,1,0:T(8,128)(2,1)} %copies.3), calls=%async_computation.1 | async-start | bytes 4194304 | tf_op jit(solution)/shard_map/all_to_all | solution.py:51
  36.9 7.0 %collective-permute-start.5 = (bf16[64,1024]{1,0:T(8,128)(2,1)S(1)}, bf16[64,1024]{1,0:T(8,128)(2,1)S(1)}, u32[]{:S(2)}, u32[]{:S(2)}) collective-permute-start(bf16[64,1024]{1,0:T(8,128)(2,1)S(1)} %collective-permute-done.3.refs_4_), channel_id=1, source_target_pairs={{0,14},{1,15},{2,0},{3,1},{4,2},{5,3},{6,4},{7,5},{8,6},{9,7},{10,... | collective-permute-start | bytes 393224 | tf_op jit(solution)/shard_map/ppermute | solution.py:30
  42.0 7.2 %collective-permute-start.4 = (bf16[64,1024]{1,0:T(8,128)(2,1)S(1)}, bf16[64,1024]{1,0:T(8,128)(2,1)S(1)}, u32[]{:S(2)}, u32[]{:S(2)}) collective-permute-start(bf16[64,1024]{1,0:T(8,128)(2,1)S(1)} %collective-permute-done.1.refs_3_), channel_id=1, source_target_pairs={{0,2},{1,3},{2,4},{3,5},{4,6},{5,7},{6,8},{7,9},{8,10},{9,11},{10,... | collective-permute-start | bytes 393224 | tf_op jit(solution)/shard_map/ppermute | solution.py:30
  43.9 7.2 %collective-permute-start.6 = (bf16[64,1024]{1,0:T(8,128)(2,1)S(1)}, bf16[64,1024]{1,0:T(8,128)(2,1)S(1)}, u32[]{:S(2)}, u32[]{:S(2)}) collective-permute-start(bf16[64,1024]{1,0:T(8,128)(2,1)S(1)} %collective-permute-done.5.refs_6_), channel_id=1, source_target_pairs={{0,14},{1,15},{2,0},{3,1},{4,2},{5,3},{6,4},{7,5},{8,6},{9,7},{10,... | collective-permute-start | bytes 393224 | tf_op jit(solution)/shard_map/ppermute | solution.py:30
  51.1 0.9 copy-start.2
  52.0 0.9 copy-start.4
  54.3 7.9 %collective-permute-start.7 = (bf16[512,1024]{1,0:T(8,128)(2,1)S(1)}, bf16[512,1024]{1,0:T(8,128)(2,1)}, u32[]{:S(2)}, u32[]{:S(2)}) collective-permute-start(bf16[512,1024]{1,0:T(8,128)(2,1)S(1)} %assemble.1), channel_id=1, source_target_pairs={{0,1},{1,0},{2,3},{3,2},{4,5},{5,4},{6,7},{7,6},{8,9},{9,8},{10,11... | collective-permute-start | bytes 3145736 | tf_op jit(solution)/shard_map/ppermute | solution.py:30
  63.9 1.0 copy-start.6
  65.4 1.3 copy-start.7
  148.4 13.0 %all-to-all-start.7 = ((f32[32,8,128]{2,1,0:T(8,128)}), f32[32,8,128]{2,1,0:T(8,128)S(1)}, u32[]{:S(2)}, u32[]{:S(2)}) async-start(f32[32,8,128]{2,1,0:T(8,128)} %get-tuple-element.33), calls=%async_computation.7 | async-start | bytes 262144 | tf_op jit(solution)/shard_map/all_to_all | solution.py:288

commit v8 on v3

--- a/solution.py
+++ b/solution.py
@@ -41,9 +41,9 @@
     copies = pl.pallas_call(
         copies_kernel,
         out_shape=jax.ShapeDtypeStruct((count,) + values.shape, values.dtype),
-        in_specs=[ANY],
-        out_specs=ANY,
-        scratch_shapes=[pltpu.SemaphoreType.DMA((count,))],
+        in_specs=[HBM],
+        out_specs=HBM,
+        scratch_shapes=[pltpu.SemaphoreType.DMA((count, max(1, values.shape[0] // 64)))],
         compiler_params=PARAMS,
         cost_estimate=pl.CostEstimate(flops=0, bytes_accessed=2**22, transcendentals=0),
         name="copies",
@@ -52,20 +52,21 @@
     return out.reshape((-1,) + values.shape[1:])
 
 
-def gather_points(source_points, target_points, masses):
+def gather_points(source_points, target_points):
     along_z = [[x * NZ + z for z in range(NZ)] for x in range(NX)]
     along_x = [[x * NZ + z for x in range(NX)] for z in range(NZ)]
     line = spread(target_points, NZ, along_z)
     held = {0: source_points}
     held[-1], held[1] = ring_step(source_points, source_points)
-    held[-2], held[2] = ring_step(held[-1], held[1])
-    held[-2], held[2], line, masses = lax.optimization_barrier((held[-2], held[2], line, masses))
+    held[-2] = move_col(held[-1], lambda y, core: (y + 1, core))
+    held[1], held[-2], line = lax.optimization_barrier((held[1], held[-2], line))
     target = spread(line, NX, along_x)
+    held[2] = move_col(held[1], lambda y, core: (y - 1, core))
     held[-3], held[3] = ring_step(held[-2], held[2])
     held[4] = move_col(held[3], lambda y, core: (y - 1, core))
     mine = assemble([held[place] for place in RING])
     other = move_col(mine, lambda y, core: (y, 1 - core))
-    return mine, other, target, masses
+    return mine, other, target
 
 
 def assemble_kernel(*refs):
@@ -83,13 +84,43 @@
 
 
 def copies_kernel(values, out, sems):
+    count, parts = sems.shape
+    rows = values.shape[0] // parts
     made = [
-        pltpu.make_async_copy(values, out.at[k], sems.at[k]) for k in range(out.shape[0])
+        pltpu.make_async_copy(
+            values.at[pl.ds(part * rows, rows)],
+            out.at[k, pl.ds(part * rows, rows)],
+            sems.at[k, part],
+        )
+        for k in range(count)
+        for part in range(parts)
     ]
     for copy in made:
         copy.start()
     for copy in made:
         copy.wait()
+
+
+def row_squares(points, groups):
+    sums = []
+    for r in range(groups):
+        square = jnp.square(points[pl.ds(r * LANES, LANES), :].astype(F32))
+        total = jnp.sum(square, axis=1, keepdims=True)
+        sums.append(jnp.broadcast_to(total, (LANES, LANES)).T[0:1])
+    return jnp.concatenate(sums, axis=0)
+
+
+def settle_kernel(target, other, same, placed, target_sq, other_sq, sems):
+    groups = other_sq.shape[0]
+    made = []
+    for r in range(groups):
+        rows = pl.ds(r * LANES, LANES)
+        made.append(pltpu.make_async_copy(other.at[rows], placed.at[rows], sems.at[r]))
+        made[-1].start()
+    target_sq[...] = row_squares(target, target_sq.shape[0])
+    for copy in made:
+        copy.wait()
+    other_sq[...] = row_squares(placed, groups)
 
 
 def columns(values, side):
@@ -148,8 +179,7 @@
 
 VMEM = pl.BlockSpec(memory_space=pltpu.VMEM)
 HBM = pl.BlockSpec(memory_space=pltpu.HBM)
-ANY = pl.BlockSpec(memory_space=pl.ANY)
-PARAMS = pltpu.CompilerParams(vmem_limit_bytes=4 * 2**20)
+PARAMS = pltpu.CompilerParams(vmem_limit_bytes=16 * 2**20)
 COST = pl.CostEstimate(flops=6 * N * N, bytes_accessed=4 * N * N, transcendentals=N * N)
 
 
@@ -171,6 +201,26 @@
 TALL = pltpu.VMEM((N, LANES), F32)
 
 
+def settle(target, other):
+    groups = other.shape[0] // LANES
+    return pl.pallas_call(
+        settle_kernel,
+        out_shape=(
+            jax.ShapeDtypeStruct(target.shape, jnp.bfloat16),
+            jax.ShapeDtypeStruct(other.shape, jnp.bfloat16),
+            jax.ShapeDtypeStruct(SMALL, F32),
+            jax.ShapeDtypeStruct((groups, LANES), F32),
+        ),
+        in_specs=[VMEM, HBM],
+        out_specs=[VMEM] * 4,
+        input_output_aliases={0: 0},
+        scratch_shapes=[pltpu.SemaphoreType.DMA((groups,))],
+        compiler_params=PARAMS,
+        cost_estimate=COST,
+        name="settle",
+    )(target, other)
+
+
 def call(kernel, shapes, scratch, *args):
     return pl.pallas_call(
         kernel,
@@ -202,13 +252,17 @@
 
 def local(source_points, target_points, source_logmass, target_logmass):
     rows, cols = lax.axis_size("row"), lax.axis_size("col")
-    masses = core_first(source_logmass * LOG2E), (target_logmass * LOG2E).reshape(SMALL)
-    mine, other, target, masses = gather_points(source_points, target_points, masses)
-    source_mass, target_mass = masses
-    target_sq = squares(target)
+    mine, other, target = gather_points(source_points, target_points)
+    mine_sq = squares(mine)
+    source_mass = core_first(source_logmass * LOG2E)
+    target_mass = (target_logmass * LOG2E).reshape(SMALL)
+    target, other, mine_sq, source_mass, target_mass = lax.optimization_barrier(
+        (target, other, mine_sq, source_mass, target_mass)
+    )
+    target, other, target_sq, other_sq = settle(target, other)
+    source_sq = jnp.concatenate([mine_sq, other_sq], axis=0)
     tiles = products(mine, target), products(other, target)
     (part,) = call(first_kernel, [(cols,) + SMALL], [WIDE], target_mass, target_sq, *tiles)
-    source_sq = jnp.concatenate([squares(mine), squares(other)], axis=0)
     for step in range(ITERS):
         parts = lax.all_to_all(part, "col", 0, 0)
         part, source_potential = call(

time: 166 us -> 170 us (1.024)
  waiting for transfers between devices: 23.4 us -> 31 us
  other arithmetic: 5.25 us -> 0.29 us
  starting transfers between devices: 59.6 us -> 56.2 us
  blocking collectives: 52.3 us -> 54.6 us
  local copies, waits for them, and re-layouts: 4.69 us -> 6.94 us
  matrix products: 6.08 us -> 4.32 us
    ppermute x8, waiting for transfers between devices: 3.48 us -> 11.9 us  [move_col(): return lax.ppermute(values, 'col', pairs)]
    all_to_all x1, starting transfers between devices: 9.4 us -> 5.44 us  [local(): parts = lax.all_to_all(part, 'col', 0, 0)]
    reduce_sum x3 -> x1, other arithmetic: 3.85 us -> 0.28 us  [squares(): return jnp.sum(jnp.square(points.astype(F32)), axis=1).reshape(-1, LANES)]
    all_to_all x2, waiting for transfers between devices: 5.24 us -> 2.85 us  [spread(): out = lax.all_to_all(copies, 'row', 0, 0, axis_index_groups=lines)]
    all_to_all x2, blocking collectives: 27.6 us -> 29.9 us  [local(): parts = lax.all_to_all(part, 'row', 0, 0)]
    unnamed x10 -> x22, local copies, waits for them, and re-layouts: 3.77 us -> 6.04 us
    dot_general x2, matrix products: 6.08 us -> 4.32 us  [products(): lax.dot_general(a, b, (((1,), (1,)), ((), ())), preferred_element_type=F32)]
  transfers between devices with their start and end apart: 12 -> 12, of which waited for: 7 -> 8; matrix products, arithmetic and copies ran while one was open for 5% -> 1% of each run, Pallas kernels for 1% -> 1%
where the time goes in v8:
time: 170 us; the launch traced here: 169 us
  starting transfers between devices  56.2 us (33%)
  blocking collectives  54.6 us (32%)
  waiting for transfers between devices  31 us (18%)
  Pallas kernels  14.8 us (9%)
  local copies, waits for them, and re-layouts  6.94 us (4%)
  matrix products  4.32 us (3%)
    ppermute x8, starting transfers between devices, move_col(): return lax.ppermute(values, 'col', pairs)  31.9 us
    all_to_all x2, blocking collectives, local(): parts = lax.all_to_all(part, 'row', 0, 0)  29.9 us
    all_to_all x2, blocking collectives, local(): parts = lax.all_to_all(part, 'col', 0, 0)  24.7 us
    all_to_all x2, starting transfers between devices, spread(): out = lax.all_to_all(copies, 'row', 0, 0, axis_index_groups=lines)  15 us
    ppermute x8, waiting for transfers between devices, move_col(): return lax.ppermute(values, 'col', pairs)  11.9 us
    pallas_call x7, Pallas kernels, call(): pl.pallas_call(kernel, out_shape=[jax.ShapeDtypeStruct(shape, F32) for sh...  9.45 us
    all_to_all x1, waiting for transfers between devices, local(): parts = lax.all_to_all(part, 'row', 0, 0)  8.39 us
    all_to_all x1, waiting for transfers between devices, local(): parts = lax.all_to_all(part, 'col', 0, 0)  7.8 us
  transfers between devices with their start and end apart: 12, of which 8 were waited for; matrix products, arithmetic and copies ran while one was open for 1% of the time, Pallas kernels for 1%

profile of v8, /device:TPU:1, one launch (start us, length us, event | category | flops | bytes accessed | tf_op | source)
XLA Modules:
  0.0 169.0 jit_solution(8150101936424548586)
XLA Ops:
  0.6 0.8 copy-done.8
  1.5 0.9 copies.2
  2.4 10.9 %all-to-all-start = ((bf16[8,32,1024]{2,1,0:T(8,128)(2,1)}), bf16[8,32,1024]{2,1,0:T(8,128)(2,1)S(1)}, u32[]{:S(2)}, u32[]{:S(2)}) async-start(bf16[8,32,1024]{2,1,0:T(8,128)(2,1)} %copies.2), calls=%async_computation | async-start | bytes 1048576 | tf_op jit(solution)/shard_map/all_to_all | solution.py:51
  13.2 3.2 %collective-permute-start.1 = (bf16[64,1024]{1,0:T(8,128)(2,1)}, bf16[64,1024]{1,0:T(8,128)(2,1)S(1)}, u32[]{:S(2)}, u32[]{:S(2)}) collective-permute-start(bf16[64,1024]{1,0:T(8,128)(2,1)} %refs_0_.1), channel_id=1, source_target_pairs={{0,2},{1,3},{2,4},{3,5},{4,6},{5,7},{6,8},{7,9},{8,10},{9,11},{10,... | collective-permute-start | bytes 393224 | tf_op jit(solution)/shard_map/ppermute | solution.py:30
  16.4 3.8 %collective-permute-start = (bf16[64,1024]{1,0:T(8,128)(2,1)}, bf16[64,1024]{1,0:T(8,128)(2,1)S(1)}, u32[]{:S(2)}, u32[]{:S(2)}) collective-permute-start(bf16[64,1024]{1,0:T(8,128)(2,1)} %refs_0_.1), channel_id=1, source_target_pairs={{0,14},{1,15},{2,0},{3,1},{4,2},{5,3},{6,4},{7,5},{8,6},{9,7},{10,... | collective-permute-start | bytes 393224 | tf_op jit(solution)/shard_map/ppermute | solution.py:30
  20.3 1.2 collective-permute-done.1.refs_1_
  21.4 1.9 %collective-permute-start.2 = (bf16[64,1024]{1,0:T(8,128)(2,1)S(1)}, bf16[64,1024]{1,0:T(8,128)(2,1)S(1)}, u32[]{:S(2)}, u32[]{:S(2)}) collective-permute-start(bf16[64,1024]{1,0:T(8,128)(2,1)S(1)} %collective-permute-done.1.refs_1_), channel_id=1, source_target_pairs={{0,2},{1,3},{2,4},{3,5},{4,6},{5,7},{6,8},{7,9},{8,10},{9,11},{10,... | collective-permute-start | bytes 393224 | tf_op jit(solution)/shard_map/ppermute | solution.py:30
  23.4 5.0 %collective-permute-done.2.refs_3_ = bf16[64,1024]{1,0:T(8,128)(2,1)S(1)} collective-permute-done((bf16[64,1024]{1,0:T(8,128)(2,1)S(1)}, bf16[64,1024]{1,0:T(8,128)(2,1)S(1)}, u32[]{:S(2)}, u32[]{:S(2)}) %collective-permute-start.2) | collective-permute-done | bytes 131104 | tf_op jit(solution)/shard_map/ppermute | solution.py:30
  28.3 2.8 %all-to-all-done = bf16[8,32,1024]{2,1,0:T(8,128)(2,1)S(1)} async-done(((bf16[8,32,1024]{2,1,0:T(8,128)(2,1)}), bf16[8,32,1024]{2,1,0:T(8,128)(2,1)S(1)}, u32[]{:S(2)}, u32[]{:S(2)}) %all-to-all-start) | async-done | bytes 524320 | tf_op jit(solution)/shard_map/all_to_all | solution.py:51
  31.2 1.5 copies.3
  32.7 4.2 %all-to-all-start.1 = ((bf16[4,256,1024]{2,1,0:T(8,128)(2,1)}), bf16[4,256,1024]{2,1,0:T(8,128)(2,1)S(1)}, u32[]{:S(2)}, u32[]{:S(2)}) async-start(bf16[4,256,1024]{2,1,0:T(8,128)(2,1)} %copies.3), calls=%async_computation.1 | async-start | bytes 4194304 | tf_op jit(solution)/shard_map/all_to_all | solution.py:51
  36.9 5.1 %collective-permute-start.3 = (bf16[64,1024]{1,0:T(8,128)(2,1)S(1)}, bf16[64,1024]{1,0:T(8,128)(2,1)S(1)}, u32[]{:S(2)}, u32[]{:S(2)}) collective-permute-start(bf16[64,1024]{1,0:T(8,128)(2,1)S(1)} %collective-permute-done.refs_2_), channel_id=1, source_target_pairs={{0,14},{1,15},{2,0},{3,1},{4,2},{5,3},{6,4},{7,5},{8,6},{9,7},{10,... | collective-permute-start | bytes 393224 | tf_op jit(solution)/shard_map/ppermute | solution.py:30
  42.0 1.9 %collective-permute-done.3.refs_4_ = bf16[64,1024]{1,0:T(8,128)(2,1)S(1)} collective-permute-done((bf16[64,1024]{1,0:T(8,128)(2,1)S(1)}, bf16[64,1024]{1,0:T(8,128)(2,1)S(1)}, u32[]{:S(2)}, u32[]{:S(2)}) %collective-permute-start.3) | collective-permute-done | bytes 131104 | tf_op jit(solution)/shard_map/ppermute | solution.py:30
  43.9 5.4 %collective-permute-start.5 = (bf16[64,1024]{1,0:T(8,128)(2,1)S(1)}, bf16[64,1024]{1,0:T(8,128)(2,1)S(1)}, u32[]{:S(2)}, u32[]{:S(2)}) collective-permute-start(bf16[64,1024]{1,0:T(8,128)(2,1)S(1)} %collective-permute-done.3.refs_4_), channel_id=1, source_target_pairs={{0,14},{1,15},{2,0},{3,1},{4,2},{5,3},{6,4},{7,5},{8,6},{9,7},{10,... | collective-permute-start | bytes 393224 | tf_op jit(solution)/shard_map/ppermute | solution.py:30
  49.3 1.9 %collective-permute-start.4 = (bf16[64,1024]{1,0:T(8,128)(2,1)S(1)}, bf16[64,1024]{1,0:T(8,128)(2,1)S(1)}, u32[]{:S(2)}, u32[]{:S(2)}) collective-permute-start(bf16[64,1024]{1,0:T(8,128)(2,1)S(1)} %collective-permute-done.2.refs_3_), channel_id=1, source_target_pairs={{0,2},{1,3},{2,4},{3,5},{4,6},{5,7},{6,8},{7,9},{8,10},{9,11},{10,... | collective-permute-start | bytes 393224 | tf_op jit(solution)/shard_map/ppermute | solution.py:30
  51.3 5.2 %collective-permute-start.6 = (bf16[64,1024]{1,0:T(8,128)(2,1)S(1)}, bf16[64,1024]{1,0:T(8,128)(2,1)S(1)}, u32[]{:S(2)}, u32[]{:S(2)}) collective-permute-start(bf16[64,1024]{1,0:T(8,128)(2,1)S(1)} %collective-permute-done.5.refs_6_), channel_id=1, source_target_pairs={{0,14},{1,15},{2,0},{3,1},{4,2},{5,3},{6,4},{7,5},{8,6},{9,7},{10,... | collective-permute-start | bytes 393224 | tf_op jit(solution)/shard_map/ppermute | solution.py:30
  56.5 0.0 collective-permute-done.4.refs_5_
  56.5 1.9 %collective-permute-done.6.refs_7_ = bf16[64,1024]{1,0:T(8,128)(2,1)S(1)} collective-permute-done((bf16[64,1024]{1,0:T(8,128)(2,1)S(1)}, bf16[64,1024]{1,0:T(8,128)(2,1)S(1)}, u32[]{:S(2)}, u32[]{:S(2)}) %collective-permute-start.6) | collective-permute-done | bytes 131104 | tf_op jit(solution)/shard_map/ppermute | solution.py:30
  58.5 0.9 copy-done.7
  59.4 1.4 assemble.1
  60.8 5.3 %collective-permute-start.7 = (bf16[512,1024]{1,0:T(8,128)(2,1)S(1)}, bf16[512,1024]{1,0:T(8,128)(2,1)}, u32[]{:S(2)}, u32[]{:S(2)}) collective-permute-start(bf16[512,1024]{1,0:T(8,128)(2,1)S(1)} %assemble.1), channel_id=1, source_target_pairs={{0,1},{1,0},{2,3},{3,2},{4,5},{5,4},{6,7},{7,6},{8,9},{9,8},{10,11... | collective-permute-start | bytes 3145736 | tf_op jit(solution)/shard_map/ppermute | solution.py:30
  66.1 0.1 reshape.34
  66.2 0.1 reshape.35.mass
  66.3 0.3 multiply_reduce_fusion
  66.6 1.9 %collective-permute-done.7.other = bf16[512,1024]{1,0:T(8,128)(2,1)} collective-permute-done((bf16[512,1024]{1,0:T(8,128)(2,1)S(1)}, bf16[512,1024]{1,0:T(8,128)(2,1)}, u32[]{:S(2)}, u32[]{:S(2)}) %collective-permute-start.7) | collective-permute-done | bytes 1048608 | tf_op jit(solution)/shard_map/ppermute | solution.py:30
  68.5 1.6 settle.1
  70.1 1.3 copy-done.3
  71.4 3.0 %convolution_multiply_fusion.1.mine = f32[512,1024]{1,0:T(8,128)S(1)} fusion(bf16[512,1024]{1,0:T(8,128)(2,1)S(1)} %assemble.1, bf16[1024,1024]{1,0:T(8,128)(2,1)} %copy-done.3), kind=kOutput, calls=%fused_computation.2 | convolution fusion | flops 1074266112 | bytes 5242880 | tf_op jit(solution)/shard_map/dot_general | solution.py:238
  74.4 1.3 convolution_multiply_fusion.other
  75.7 1.8 %first_kernel.1 = f32[16,8,128]{2,1,0:T(8,128)} custom-call(f32[8,128]{1,0:T(8,128)S(1)} %multiply_bitcast_fusion.mass, f32[8,128]{1,0:T(8,128)S(1)} %get-tuple-element.24.squares, f32[512,1024]{1,0:T(8,128)S(1)} %convolution_multiply_fusion.1.mine, f32[512,1024]{1,0:T(8,128)S(1)} %convolution_multiply_fusion.other), custom_call_target="tpu_custom_call" | custom-call | flops 6291456 | bytes 4194304 | tf_op jit(solution)/shard_map/first_kernel/pallas_call | solution.py:225
  77.6 1.3 copy-done
  78.9 5.4 %all-to-all-start.2 = ((f32[16,8,128]{2,1,0:T(8,128)}), f32[16,8,128]{2,1,0:T(8,128)S(1)}, u32[]{:S(2)}, u32[]{:S(2)}) async-start(f32[16,8,128]{2,1,0:T(8,128)} %first_kernel.1), calls=%async_computation.2 | async-start | bytes 131072 | tf_op jit(solution)/shard_map/all_to_all | solution.py:267
  84.3 7.8 %all-to-all-done.2.parts = f32[16,8,128]{2,1,0:T(8,128)S(1)} async-done(((f32[16,8,128]{2,1,0:T(8,128)}), f32[16,8,128]{2,1,0:T(8,128)S(1)}, u32[]{:S(2)}, u32[]{:S(2)}) %all-to-all-start.2) | async-done | bytes 65568 | tf_op jit(solution)/shard_map/all_to_all | solution.py:267
  92.1 1.6 copy-done.1
  93.7 1.5 target_kernel.3
  95.2 17.5 %all_to_all.40.parts = f32[32,8,128]{2,1,0:T(8,128)S(1)} all-to-all(f32[32,8,128]{2,1,0:T(8,128)S(1)} %get-tuple-element.30), channel_id=1, replica_groups=mesh['row'=32,'col'=16] {'row'}, dimensions={0} | all-to-all | bytes 262144 | tf_op jit(solution)/shard_map/all_to_all | solution.py:271
  112.7 1.2 source_kernel.2
  113.9 12.3 %all_to_all.41.parts = f32[16,8,128]{2,1,0:T(8,128)S(1)} all-to-all(f32[16,8,128]{2,1,0:T(8,128)S(1)} %source_kernel.2), channel_id=1, replica_groups=mesh['row'=32,'col'=16] {'col'}, dimensions={0} | all-to-all | bytes 131072 | tf_op jit(solution)/shard_map/all_to_all | solution.py:267
  126.3 1.5 target_kernel.4
  127.8 12.4 %all_to_all.42.parts = f32[32,8,128]{2,1,0:T(8,128)S(1)} all-to-all(f32[32,8,128]{2,1,0:T(8,128)S(1)} %get-tuple-element.31), channel_id=1, replica_groups=mesh['row'=32,'col'=16] {'row'}, dimensions={0} | all-to-all | bytes 262144 | tf_op jit(solution)/shard_map/all_to_all | solution.py:271
  140.2 1.2 source_kernel.3
  141.3 12.3 %all_to_all.43.parts = f32[16,8,128]{2,1,0:T(8,128)S(1)} all-to-all(f32[16,8,128]{2,1,0:T(8,128)S(1)} %source_kernel.3), channel_id=1, replica_groups=mesh['row'=32,'col'=16] {'col'}, dimensions={0} | all-to-all | bytes 131072 | tf_op jit(solution)/shard_map/all_to_all | solution.py:267
  153.7 1.6 target_kernel.5
  155.3 3.9 %all-to-all-start.7 = ((f32[32,8,128]{2,1,0:T(8,128)}), f32[32,8,128]{2,1,0:T(8,128)S(1)}, u32[]{:S(2)}, u32[]{:S(2)}) async-start(f32[32,8,128]{2,1,0:T(8,128)} %get-tuple-element.33), calls=%async_computation.7 | async-start | bytes 262144 | tf_op jit(solution)/shard_map/all_to_all | solution.py:271
  159.2 0.1 reshape.37
  159.3 0.7 reshape.38
  159.9 8.4 %all-to-all-done.7.parts = f32[32,8,128]{2,1,0:T(8,128)S(1)} async-done(((f32[32,8,128]{2,1,0:T(8,128)}), f32[32,8,128]{2,1,0:T(8,128)S(1)}, u32[]{:S(2)}, u32[]{:S(2)}) %all-to-all-start.7) | async-done | bytes 131104 | tf_op jit(solution)/shard_map/all_to_all | solution.py:271
  168.3 0.7 last_kernel.1
  (25 shorter events, 0.1 us)
Async XLA Ops:
  0.6 0.8 copy-start.8
  2.4 28.8 %all-to-all-start = ((bf16[8,32,1024]{2,1,0:T(8,128)(2,1)}), bf16[8,32,1024]{2,1,0:T(8,128)(2,1)S(1)}, u32[]{:S(2)}, u32[]{:S(2)}) async-start(bf16[8,32,1024]{2,1,0:T(8,128)(2,1)} %copies.2), calls=%async_computation | async-start | bytes 1048576 | tf_op jit(solution)/shard_map/all_to_all | solution.py:51
  13.2 8.2 %collective-permute-start.1 = (bf16[64,1024]{1,0:T(8,128)(2,1)}, bf16[64,1024]{1,0:T(8,128)(2,1)S(1)}, u32[]{:S(2)}, u32[]{:S(2)}) collective-permute-start(bf16[64,1024]{1,0:T(8,128)(2,1)} %refs_0_.1), channel_id=1, source_target_pairs={{0,2},{1,3},{2,4},{3,5},{4,6},{5,7},{6,8},{7,9},{8,10},{9,11},{10,... | collective-permute-start | bytes 393224 | tf_op jit(solution)/shard_map/ppermute | solution.py:30
  16.4 6.9 %collective-permute-start = (bf16[64,1024]{1,0:T(8,128)(2,1)}, bf16[64,1024]{1,0:T(8,128)(2,1)S(1)}, u32[]{:S(2)}, u32[]{:S(2)}) collective-permute-start(bf16[64,1024]{1,0:T(8,128)(2,1)} %refs_0_.1), channel_id=1, source_target_pairs={{0,14},{1,15},{2,0},{3,1},{4,2},{5,3},{6,4},{7,5},{8,6},{9,7},{10,... | collective-permute-start | bytes 393224 | tf_op jit(solution)/shard_map/ppermute | solution.py:30
  21.4 6.9 %collective-permute-start.2 = (bf16[64,1024]{1,0:T(8,128)(2,1)S(1)}, bf16[64,1024]{1,0:T(8,128)(2,1)S(1)}, u32[]{:S(2)}, u32[]{:S(2)}) collective-permute-start(bf16[64,1024]{1,0:T(8,128)(2,1)S(1)} %collective-permute-done.1.refs_1_), channel_id=1, source_target_pairs={{0,2},{1,3},{2,4},{3,5},{4,6},{5,7},{6,8},{7,9},{8,10},{9,11},{10,... | collective-permute-start | bytes 393224 | tf_op jit(solution)/shard_map/ppermute | solution.py:30
  28.3 21.0 %copy-start.6 = (bf16[64,1024]{1,0:T(8,128)(2,1)}, bf16[64,1024]{1,0:T(8,128)(2,1)S(1)}, u32[]{:S(2)}) copy-start(bf16[64,1024]{1,0:T(8,128)(2,1)S(1)} %collective-permute-done.2.refs_3_) | copy-start | bytes 393220
  32.7 25.8 %copy-start.5 = (bf16[64,1024]{1,0:T(8,128)(2,1)S(1)}, bf16[64,1024]{1,0:T(8,128)(2,1)}, u32[]{:S(2)}) copy-start(bf16[64,1024]{1,0:T(8,128)(2,1)} %refs_0_.1) | copy-start | bytes 393220
  32.7 33.4 %copy-start.9 = (f32[1024]{0:T(1024)S(1)}, f32[1024]{0:T(1024)}, u32[]{:S(2)}) copy-start(f32[1024]{0:T(1024)} %param.6) | copy-start | bytes 12292
  32.7 33.6 %copy-start.10 = (f32[1024]{0:T(1024)S(1)}, f32[1024]{0:T(1024)}, u32[]{:S(2)}) copy-start(f32[1024]{0:T(1024)} %param.7) | copy-start | bytes 12292
  32.7 35.8 %all-to-all-start.1 = ((bf16[4,256,1024]{2,1,0:T(8,128)(2,1)}), bf16[4,256,1024]{2,1,0:T(8,128)(2,1)S(1)}, u32[]{:S(2)}, u32[]{:S(2)}) async-start(bf16[4,256,1024]{2,1,0:T(8,128)(2,1)} %copies.3), calls=%async_computation.1 | async-start | bytes 4194304 | tf_op jit(solution)/shard_map/all_to_all | solution.py:51
  36.9 7.0 %collective-permute-start.3 = (bf16[64,1024]{1,0:T(8,128)(2,1)S(1)}, bf16[64,1024]{1,0:T(8,128)(2,1)S(1)}, u32[]{:S(2)}, u32[]{:S(2)}) collective-permute-start(bf16[64,1024]{1,0:T(8,128)(2,1)S(1)} %collective-permute-done.refs_2_), channel_id=1, source_target_pairs={{0,14},{1,15},{2,0},{3,1},{4,2},{5,3},{6,4},{7,5},{8,6},{9,7},{10,... | collective-permute-start | bytes 393224 | tf_op jit(solution)/shard_map/ppermute | solution.py:30
  43.9 7.4 %collective-permute-start.5 = (bf16[64,1024]{1,0:T(8,128)(2,1)S(1)}, bf16[64,1024]{1,0:T(8,128)(2,1)S(1)}, u32[]{:S(2)}, u32[]{:S(2)}) collective-permute-start(bf16[64,1024]{1,0:T(8,128)(2,1)S(1)} %collective-permute-done.3.refs_4_), channel_id=1, source_target_pairs={{0,14},{1,15},{2,0},{3,1},{4,2},{5,3},{6,4},{7,5},{8,6},{9,7},{10,... | collective-permute-start | bytes 393224 | tf_op jit(solution)/shard_map/ppermute | solution.py:30
  49.3 7.2 %collective-permute-start.4 = (bf16[64,1024]{1,0:T(8,128)(2,1)S(1)}, bf16[64,1024]{1,0:T(8,128)(2,1)S(1)}, u32[]{:S(2)}, u32[]{:S(2)}) collective-permute-start(bf16[64,1024]{1,0:T(8,128)(2,1)S(1)} %collective-permute-done.2.refs_3_), channel_id=1, source_target_pairs={{0,2},{1,3},{2,4},{3,5},{4,6},{5,7},{6,8},{7,9},{8,10},{9,11},{10,... | collective-permute-start | bytes 393224 | tf_op jit(solution)/shard_map/ppermute | solution.py:30
  51.3 7.2 %collective-permute-start.6 = (bf16[64,1024]{1,0:T(8,128)(2,1)S(1)}, bf16[64,1024]{1,0:T(8,128)(2,1)S(1)}, u32[]{:S(2)}, u32[]{:S(2)}) collective-permute-start(bf16[64,1024]{1,0:T(8,128)(2,1)S(1)} %collective-permute-done.5.refs_6_), channel_id=1, source_target_pairs={{0,14},{1,15},{2,0},{3,1},{4,2},{5,3},{6,4},{7,5},{8,6},{9,7},{10,... | collective-permute-start | bytes 393224 | tf_op jit(solution)/shard_map/ppermute | solution.py:30
  58.5 0.9 copy-start.7
  60.8 7.7 %collective-permute-start.7 = (bf16[512,1024]{1,0:T(8,128)(2,1)S(1)}, bf16[512,1024]{1,0:T(8,128)(2,1)}, u32[]{:S(2)}, u32[]{:S(2)}) collective-permute-start(bf16[512,1024]{1,0:T(8,128)(2,1)S(1)} %assemble.1), channel_id=1, source_target_pairs={{0,1},{1,0},{2,3},{3,2},{4,5},{5,4},{6,7},{7,6},{8,9},{9,8},{10,11... | collective-permute-start | bytes 3145736 | tf_op jit(solution)/shard_map/ppermute | solution.py:30
  70.0 1.3 copy-start.3
  71.4 3.0 %copy-start.4 = (bf16[1024,1024]{1,0:T(8,128)(2,1)S(1)}, bf16[1024,1024]{1,0:T(8,128)(2,1)}, u32[]{:S(2)}) copy-start(bf16[1024,1024]{1,0:T(8,128)(2,1)} %copy-done.3) | copy-start | bytes 6291460
  77.5 1.3 copy-start
  78.9 13.3 %all-to-all-start.2 = ((f32[16,8,128]{2,1,0:T(8,128)}), f32[16,8,128]{2,1,0:T(8,128)S(1)}, u32[]{:S(2)}, u32[]{:S(2)}) async-start(f32[16,8,128]{2,1,0:T(8,128)} %first_kernel.1), calls=%async_computation.2 | async-start | bytes 131072 | tf_op jit(solution)/shard_map/all_to_all | solution.py:267
  92.1 1.6 copy-start.1
  93.7 19.0 %copy-start.2 = (f32[512,1024]{1,0:T(8,128)S(1)}, f32[512,1024]{1,0:T(8,128)}, u32[]{:S(2)}) copy-start(f32[512,1024]{1,0:T(8,128)} %copy-done) | copy-start | bytes 6291460
  155.3 13.0 %all-to-all-start.7 = ((f32[32,8,128]{2,1,0:T(8,128)}), f32[32,8,128]{2,1,0:T(8,128)S(1)}, u32[]{:S(2)}, u32[]{:S(2)}) async-start(f32[32,8,128]{2,1,0:T(8,128)} %get-tuple-element.33), calls=%async_computation.7 | async-start | bytes 262144 | tf_op jit(solution)/shard_map/all_to_all | solution.py:271

commit v9 on v6

--- a/solution.py
+++ b/solution.py
@@ -52,22 +52,20 @@
     return out.reshape((-1,) + values.shape[1:])
 
 
-def gather_points(source_points, target_points):
+def gather_points(source_points, target_points, masses):
     along_z = [[x * NZ + z for z in range(NZ)] for x in range(NX)]
     along_x = [[x * NZ + z for x in range(NX)] for z in range(NZ)]
     line = spread(target_points, NZ, along_z)
     held = {0: source_points}
-    held[4] = move_col(source_points, lambda y, core: (y + 4, core))
     held[-1], held[1] = ring_step(source_points, source_points)
-    held[-1], held[1], held[4], line = lax.optimization_barrier(
-        (held[-1], held[1], held[4], line)
-    )
+    held[-2], held[2] = ring_step(held[-1], held[1])
+    held[-2], held[2], line, masses = lax.optimization_barrier((held[-2], held[2], line, masses))
     target = spread(line, NX, along_x)
-    held[-2], held[2] = ring_step(held[-1], held[1])
     held[-3], held[3] = ring_step(held[-2], held[2])
+    held[4] = move_col(held[3], lambda y, core: (y - 1, core))
     mine = assemble([held[place] for place in RING])
     other = move_col(mine, lambda y, core: (y, 1 - core))
-    return mine, other, target
+    return mine, other, target, masses
 
 
 def assemble_kernel(*refs):
@@ -263,14 +261,12 @@
 
 def local(source_points, target_points, source_logmass, target_logmass):
     rows, cols = lax.axis_size("row"), lax.axis_size("col")
-    mine, other, target = gather_points(source_points, target_points)
+    masses = core_first(source_logmass * LOG2E), (target_logmass * LOG2E).reshape(SMALL)
+    mine, other, target, masses = gather_points(source_points, target_points, masses)
+    source_mass, target_mass = masses
     other, other_sq = place(other)
     source_sq = jnp.concatenate([squares(mine), other_sq], axis=0)
-    source_mass = core_first(source_logmass * LOG2E)
-    target_mass = (target_logmass * LOG2E).reshape(SMALL)
-    target, other, source_sq, source_mass, target_mass = lax.optimization_barrier(
-        (target, other, source_sq, source_mass, target_mass)
-    )
+    target, other, source_sq = lax.optimization_barrier((target, other, source_sq))
     target, target_sq = in_place_squares(target)
     tiles = products(mine, target), products(other, target)
     (part,) = call(first_kernel, [(cols,) + SMALL], [WIDE], target_mass, target_sq, *tiles)

time: 164 us -> 162 us (0.988)
  waiting for transfers between devices: 18.1 us -> 15.2 us
  starting transfers between devices: 52.4 us -> 50.1 us
    ppermute x8, waiting for transfers between devices: 8.95 us -> 5.46 us  [move_col(): return lax.ppermute(values, 'col', pairs)]
    ppermute x8, starting transfers between devices: 33.5 us -> 31.2 us  [move_col(): return lax.ppermute(values, 'col', pairs)]
  transfers between devices with their start and end apart: 11 -> 11, of which waited for: 7 -> 6; matrix products, arithmetic and copies ran while one was open for 1% -> 2% of each run, Pallas kernels for 2% -> 1%
where the time goes in v9:
time: 162 us; the launch traced here: 161 us
  blocking collectives  71.9 us (44%)
  starting transfers between devices  50.1 us (31%)
  waiting for transfers between devices  15.2 us (9%)
  Pallas kernels  14.1 us (9%)
  local copies, waits for them, and re-layouts  4.55 us (3%)
  matrix products  2.6 us (2%)
  other arithmetic  1.67 us (1%)
    all_to_all x3, blocking collectives, local(): parts = lax.all_to_all(part, 'col', 0, 0)  40.3 us
    all_to_all x2, blocking collectives, local(): parts = lax.all_to_all(part, 'row', 0, 0)  31.6 us
    ppermute x8, starting transfers between devices, move_col(): return lax.ppermute(values, 'col', pairs)  31.2 us
    all_to_all x2, starting transfers between devices, spread(): out = lax.all_to_all(copies, 'row', 0, 0, axis_index_groups=lines)  15 us
    pallas_call x7, Pallas kernels, call(): pl.pallas_call(kernel, out_shape=[jax.ShapeDtypeStruct(shape, F32) for sh...  9.06 us
    all_to_all x1, waiting for transfers between devices, local(): parts = lax.all_to_all(part, 'row', 0, 0)  8.39 us
    ppermute x8, waiting for transfers between devices, move_col(): return lax.ppermute(values, 'col', pairs)  5.46 us
    all_to_all x1, starting transfers between devices, local(): parts = lax.all_to_all(part, 'row', 0, 0)  3.84 us
  transfers between devices with their start and end apart: 11, of which 6 were waited for; matrix products, arithmetic and copies ran while one was open for 2% of the time, Pallas kernels for 1%

profile of v9, /device:TPU:1, one launch (start us, length us, event | category | flops | bytes accessed | tf_op | source)
XLA Modules:
  0.0 160.9 jit_solution(14080642931915955468)
XLA Ops:
  0.6 0.8 copy-done.5
  1.5 0.9 copies.2
  2.4 10.9 %all-to-all-start = ((bf16[8,32,1024]{2,1,0:T(8,128)(2,1)}), bf16[8,32,1024]{2,1,0:T(8,128)(2,1)S(1)}, u32[]{:S(2)}, u32[]{:S(2)}) async-start(bf16[8,32,1024]{2,1,0:T(8,128)(2,1)} %copies.2), calls=%async_computation | async-start | bytes 1048576 | tf_op jit(solution)/shard_map/all_to_all | solution.py:51
  13.2 3.2 %collective-permute-start = (bf16[64,1024]{1,0:T(8,128)(2,1)}, bf16[64,1024]{1,0:T(8,128)(2,1)S(1)}, u32[]{:S(2)}, u32[]{:S(2)}) collective-permute-start(bf16[64,1024]{1,0:T(8,128)(2,1)} %refs_0_.1), channel_id=1, source_target_pairs={{0,2},{1,3},{2,4},{3,5},{4,6},{5,7},{6,8},{7,9},{8,10},{9,11},{10,... | collective-permute-start | bytes 393224 | tf_op jit(solution)/shard_map/ppermute | solution.py:30
  16.4 3.8 %collective-permute-start.2 = (bf16[64,1024]{1,0:T(8,128)(2,1)}, bf16[64,1024]{1,0:T(8,128)(2,1)S(1)}, u32[]{:S(2)}, u32[]{:S(2)}) collective-permute-start(bf16[64,1024]{1,0:T(8,128)(2,1)} %refs_0_.1), channel_id=1, source_target_pairs={{0,14},{1,15},{2,0},{3,1},{4,2},{5,3},{6,4},{7,5},{8,6},{9,7},{10,... | collective-permute-start | bytes 393224 | tf_op jit(solution)/shard_map/ppermute | solution.py:30
  20.3 0.7 broadcast_multiply_fusion
  21.0 0.1 reshape.32
  21.0 0.1 reshape.33.mass
  21.1 0.3 collective-permute-done.refs_1_
  21.4 1.9 %collective-permute-start.1 = (bf16[64,1024]{1,0:T(8,128)(2,1)S(1)}, bf16[64,1024]{1,0:T(8,128)(2,1)S(1)}, u32[]{:S(2)}, u32[]{:S(2)}) collective-permute-start(bf16[64,1024]{1,0:T(8,128)(2,1)S(1)} %collective-permute-done.refs_1_), channel_id=1, source_target_pairs={{0,2},{1,3},{2,4},{3,5},{4,6},{5,7},{6,8},{7,9},{8,10},{9,11},{10,... | collective-permute-start | bytes 393224 | tf_op jit(solution)/shard_map/ppermute | solution.py:30
  23.4 4.6 %collective-permute-start.3 = (bf16[64,1024]{1,0:T(8,128)(2,1)S(1)}, bf16[64,1024]{1,0:T(8,128)(2,1)S(1)}, u32[]{:S(2)}, u32[]{:S(2)}) collective-permute-start(bf16[64,1024]{1,0:T(8,128)(2,1)S(1)} %collective-permute-done.2.refs_2_), channel_id=1, source_target_pairs={{0,14},{1,15},{2,0},{3,1},{4,2},{5,3},{6,4},{7,5},{8,6},{9,7},{10,... | collective-permute-start | bytes 393224 | tf_op jit(solution)/shard_map/ppermute | solution.py:30
  27.9 0.7 multiply_bitcast_fusion.mass
  28.6 1.2 collective-permute-done.3.refs_4_
  29.9 1.3 all-to-all-done
  31.2 1.4 copies.3
  32.6 4.2 %all-to-all-start.1 = ((bf16[4,256,1024]{2,1,0:T(8,128)(2,1)}), bf16[4,256,1024]{2,1,0:T(8,128)(2,1)S(1)}, u32[]{:S(2)}, u32[]{:S(2)}) async-start(bf16[4,256,1024]{2,1,0:T(8,128)(2,1)} %copies.3), calls=%async_computation.1 | async-start | bytes 4194304 | tf_op jit(solution)/shard_map/all_to_all | solution.py:51
  36.7 5.1 %collective-permute-start.5 = (bf16[64,1024]{1,0:T(8,128)(2,1)S(1)}, bf16[64,1024]{1,0:T(8,128)(2,1)S(1)}, u32[]{:S(2)}, u32[]{:S(2)}) collective-permute-start(bf16[64,1024]{1,0:T(8,128)(2,1)S(1)} %collective-permute-done.3.refs_4_), channel_id=1, source_target_pairs={{0,14},{1,15},{2,0},{3,1},{4,2},{5,3},{6,4},{7,5},{8,6},{9,7},{10,... | collective-permute-start | bytes 393224 | tf_op jit(solution)/shard_map/ppermute | solution.py:30
  41.8 1.9 %collective-permute-start.4 = (bf16[64,1024]{1,0:T(8,128)(2,1)S(1)}, bf16[64,1024]{1,0:T(8,128)(2,1)S(1)}, u32[]{:S(2)}, u32[]{:S(2)}) collective-permute-start(bf16[64,1024]{1,0:T(8,128)(2,1)S(1)} %collective-permute-done.1.refs_3_), channel_id=1, source_target_pairs={{0,2},{1,3},{2,4},{3,5},{4,6},{5,7},{6,8},{7,9},{8,10},{9,11},{10,... | collective-permute-start | bytes 393224 | tf_op jit(solution)/shard_map/ppermute | solution.py:30
  43.8 5.2 %collective-permute-start.6 = (bf16[64,1024]{1,0:T(8,128)(2,1)S(1)}, bf16[64,1024]{1,0:T(8,128)(2,1)S(1)}, u32[]{:S(2)}, u32[]{:S(2)}) collective-permute-start(bf16[64,1024]{1,0:T(8,128)(2,1)S(1)} %collective-permute-done.5.refs_6_), channel_id=1, source_target_pairs={{0,14},{1,15},{2,0},{3,1},{4,2},{5,3},{6,4},{7,5},{8,6},{9,7},{10,... | collective-permute-start | bytes 393224 | tf_op jit(solution)/shard_map/ppermute | solution.py:30
  49.0 0.0 collective-permute-done.4.refs_5_
  49.1 1.9 %collective-permute-done.6.refs_7_ = bf16[64,1024]{1,0:T(8,128)(2,1)S(1)} collective-permute-done((bf16[64,1024]{1,0:T(8,128)(2,1)S(1)}, bf16[64,1024]{1,0:T(8,128)(2,1)S(1)}, u32[]{:S(2)}, u32[]{:S(2)}) %collective-permute-start.6) | collective-permute-done | bytes 131104 | tf_op jit(solution)/shard_map/ppermute | solution.py:30
  51.0 0.9 copy-done.2
  51.9 0.9 copy-done.4
  52.8 1.4 assemble.1
  54.2 5.5 %collective-permute-start.7 = (bf16[512,1024]{1,0:T(8,128)(2,1)S(1)}, bf16[512,1024]{1,0:T(8,128)(2,1)S(1)}, u32[]{:S(2)}, u32[]{:S(2)}) collective-permute-start(bf16[512,1024]{1,0:T(8,128)(2,1)S(1)} %assemble.1), channel_id=1, source_target_pairs={{0,1},{1,0},{2,3},{3,2},{4,5},{5,4},{6,7},{7,6},{8,9},{9,8},{10,11... | collective-permute-start | bytes 3145736 | tf_op jit(solution)/shard_map/ppermute | solution.py:30
  59.7 0.3 multiply_reduce_fusion
  60.0 2.0 %collective-permute-done.7.points = bf16[512,1024]{1,0:T(8,128)(2,1)S(1)} collective-permute-done((bf16[512,1024]{1,0:T(8,128)(2,1)S(1)}, bf16[512,1024]{1,0:T(8,128)(2,1)S(1)}, u32[]{:S(2)}, u32[]{:S(2)}) %collective-permute-start.7) | collective-permute-done | bytes 1048608 | tf_op jit(solution)/shard_map/ppermute | solution.py:30
  62.0 0.8 place.1
  62.8 1.0 copy-done.6
  63.8 0.6 in_place_squares.1
  64.3 1.3 convolution_multiply_fusion.1.mine
  65.6 1.3 convolution_multiply_fusion.other
  66.9 1.2 first_kernel.1
  68.1 15.6 %all_to_all.40.parts = f32[16,8,128]{2,1,0:T(8,128)S(1)} all-to-all(f32[16,8,128]{2,1,0:T(8,128)S(1)} %first_kernel.1), channel_id=1, replica_groups=mesh['row'=32,'col'=16] {'col'}, dimensions={0} | all-to-all | bytes 131072 | tf_op jit(solution)/shard_map/all_to_all | solution.py:274
  83.7 1.6 target_kernel.3
  85.3 19.2 %all_to_all.41.parts = f32[32,8,128]{2,1,0:T(8,128)S(1)} all-to-all(f32[32,8,128]{2,1,0:T(8,128)S(1)} %get-tuple-element.30), channel_id=1, replica_groups=mesh['row'=32,'col'=16] {'row'}, dimensions={0} | all-to-all | bytes 262144 | tf_op jit(solution)/shard_map/all_to_all | solution.py:278
  104.5 1.2 source_kernel.2
  105.7 12.3 %all_to_all.42.parts = f32[16,8,128]{2,1,0:T(8,128)S(1)} all-to-all(f32[16,8,128]{2,1,0:T(8,128)S(1)} %source_kernel.2), channel_id=1, replica_groups=mesh['row'=32,'col'=16] {'col'}, dimensions={0} | all-to-all | bytes 131072 | tf_op jit(solution)/shard_map/all_to_all | solution.py:274
  118.0 1.6 target_kernel.4
  119.6 12.4 %all_to_all.43.parts = f32[32,8,128]{2,1,0:T(8,128)S(1)} all-to-all(f32[32,8,128]{2,1,0:T(8,128)S(1)} %get-tuple-element.31), channel_id=1, replica_groups=mesh['row'=32,'col'=16] {'row'}, dimensions={0} | all-to-all | bytes 262144 | tf_op jit(solution)/shard_map/all_to_all | solution.py:278
  132.0 1.2 source_kernel.3
  133.2 12.3 %all_to_all.44.parts = f32[16,8,128]{2,1,0:T(8,128)S(1)} all-to-all(f32[16,8,128]{2,1,0:T(8,128)S(1)} %source_kernel.3), channel_id=1, replica_groups=mesh['row'=32,'col'=16] {'col'}, dimensions={0} | all-to-all | bytes 131072 | tf_op jit(solution)/shard_map/all_to_all | solution.py:274
  145.5 1.7 %target_kernel.5 = (f32[32,8,128]{2,1,0:T(8,128)}, f32[8,128]{1,0:T(8,128)S(1)}) custom-call(f32[16,8,128]{2,1,0:T(8,128)S(1)} %all_to_all.44.parts, f32[8,128]{1,0:T(8,128)S(1)} %reshape.33.mass, f32[8,128]{1,0:T(8,128)S(1)} %pad_maximum_fusion.squares, f32[512,1024]{1,0:T(8,128)S(1)} %convolution_multiply_fusion.1.mine, ...), custom_call_target="tpu_custom_call" | custom-call | flops 6291456 | bytes 4194304 | tf_op jit(solution)/shard_map/target_kernel/pallas_call | solution.py:234
  147.2 3.8 %all-to-all-start.7 = ((f32[32,8,128]{2,1,0:T(8,128)}), f32[32,8,128]{2,1,0:T(8,128)S(1)}, u32[]{:S(2)}, u32[]{:S(2)}) async-start(f32[32,8,128]{2,1,0:T(8,128)} %get-tuple-element.33), calls=%async_computation.7 | async-start | bytes 262144 | tf_op jit(solution)/shard_map/all_to_all | solution.py:278
  151.1 0.1 reshape.37
  151.2 0.7 reshape.38
  151.8 8.4 %all-to-all-done.7.parts = f32[32,8,128]{2,1,0:T(8,128)S(1)} async-done(((f32[32,8,128]{2,1,0:T(8,128)}), f32[32,8,128]{2,1,0:T(8,128)S(1)}, u32[]{:S(2)}, u32[]{:S(2)}) %all-to-all-start.7) | async-done | bytes 131104 | tf_op jit(solution)/shard_map/all_to_all | solution.py:278
  160.2 0.7 last_kernel.1
  (19 shorter events, 0.1 us)
Async XLA Ops:
  0.6 0.8 copy-start.5
  2.4 28.8 %all-to-all-start = ((bf16[8,32,1024]{2,1,0:T(8,128)(2,1)}), bf16[8,32,1024]{2,1,0:T(8,128)(2,1)S(1)}, u32[]{:S(2)}, u32[]{:S(2)}) async-start(bf16[8,32,1024]{2,1,0:T(8,128)(2,1)} %copies.2), calls=%async_computation | async-start | bytes 1048576 | tf_op jit(solution)/shard_map/all_to_all | solution.py:51
  13.2 8.2 %collective-permute-start = (bf16[64,1024]{1,0:T(8,128)(2,1)}, bf16[64,1024]{1,0:T(8,128)(2,1)S(1)}, u32[]{:S(2)}, u32[]{:S(2)}) collective-permute-start(bf16[64,1024]{1,0:T(8,128)(2,1)} %refs_0_.1), channel_id=1, source_target_pairs={{0,2},{1,3},{2,4},{3,5},{4,6},{5,7},{6,8},{7,9},{8,10},{9,11},{10,... | collective-permute-start | bytes 393224 | tf_op jit(solution)/shard_map/ppermute | solution.py:30
  16.4 6.9 %collective-permute-start.2 = (bf16[64,1024]{1,0:T(8,128)(2,1)}, bf16[64,1024]{1,0:T(8,128)(2,1)S(1)}, u32[]{:S(2)}, u32[]{:S(2)}) collective-permute-start(bf16[64,1024]{1,0:T(8,128)(2,1)} %refs_0_.1), channel_id=1, source_target_pairs={{0,14},{1,15},{2,0},{3,1},{4,2},{5,3},{6,4},{7,5},{8,6},{9,7},{10,... | collective-permute-start | bytes 393224 | tf_op jit(solution)/shard_map/ppermute | solution.py:30
  21.4 7.2 %collective-permute-start.1 = (bf16[64,1024]{1,0:T(8,128)(2,1)S(1)}, bf16[64,1024]{1,0:T(8,128)(2,1)S(1)}, u32[]{:S(2)}, u32[]{:S(2)}) collective-permute-start(bf16[64,1024]{1,0:T(8,128)(2,1)S(1)} %collective-permute-done.refs_1_), channel_id=1, source_target_pairs={{0,2},{1,3},{2,4},{3,5},{4,6},{5,7},{6,8},{7,9},{8,10},{9,11},{10,... | collective-permute-start | bytes 393224 | tf_op jit(solution)/shard_map/ppermute | solution.py:30
  23.4 6.5 %collective-permute-start.3 = (bf16[64,1024]{1,0:T(8,128)(2,1)S(1)}, bf16[64,1024]{1,0:T(8,128)(2,1)S(1)}, u32[]{:S(2)}, u32[]{:S(2)}) collective-permute-start(bf16[64,1024]{1,0:T(8,128)(2,1)S(1)} %collective-permute-done.2.refs_2_), channel_id=1, source_target_pairs={{0,14},{1,15},{2,0},{3,1},{4,2},{5,3},{6,4},{7,5},{8,6},{9,7},{10,... | collective-permute-start | bytes 393224 | tf_op jit(solution)/shard_map/ppermute | solution.py:30
  28.6 13.2 %copy-start.1 = (bf16[64,1024]{1,0:T(8,128)(2,1)}, bf16[64,1024]{1,0:T(8,128)(2,1)S(1)}, u32[]{:S(2)}) copy-start(bf16[64,1024]{1,0:T(8,128)(2,1)S(1)} %collective-permute-done.1.refs_3_) | copy-start | bytes 393220
  29.9 6.9 %copy-start.3 = (bf16[64,1024]{1,0:T(8,128)(2,1)}, bf16[64,1024]{1,0:T(8,128)(2,1)S(1)}, u32[]{:S(2)}) copy-start(bf16[64,1024]{1,0:T(8,128)(2,1)S(1)} %collective-permute-done.3.refs_4_) | copy-start | bytes 393220
  32.6 18.4 %copy-start = (bf16[64,1024]{1,0:T(8,128)(2,1)S(1)}, bf16[64,1024]{1,0:T(8,128)(2,1)}, u32[]{:S(2)}) copy-start(bf16[64,1024]{1,0:T(8,128)(2,1)} %refs_0_.1) | copy-start | bytes 393220
  32.6 31.2 %all-to-all-start.1 = ((bf16[4,256,1024]{2,1,0:T(8,128)(2,1)}), bf16[4,256,1024]{2,1,0:T(8,128)(2,1)S(1)}, u32[]{:S(2)}, u32[]{:S(2)}) async-start(bf16[4,256,1024]{2,1,0:T(8,128)(2,1)} %copies.3), calls=%async_computation.1 | async-start | bytes 4194304 | tf_op jit(solution)/shard_map/all_to_all | solution.py:51
  36.7 7.0 %collective-permute-start.5 = (bf16[64,1024]{1,0:T(8,128)(2,1)S(1)}, bf16[64,1024]{1,0:T(8,128)(2,1)S(1)}, u32[]{:S(2)}, u32[]{:S(2)}) collective-permute-start(bf16[64,1024]{1,0:T(8,128)(2,1)S(1)} %collective-permute-done.3.refs_4_), channel_id=1, source_target_pairs={{0,14},{1,15},{2,0},{3,1},{4,2},{5,3},{6,4},{7,5},{8,6},{9,7},{10,... | collective-permute-start | bytes 393224 | tf_op jit(solution)/shard_map/ppermute | solution.py:30
  41.8 7.2 %collective-permute-start.4 = (bf16[64,1024]{1,0:T(8,128)(2,1)S(1)}, bf16[64,1024]{1,0:T(8,128)(2,1)S(1)}, u32[]{:S(2)}, u32[]{:S(2)}) collective-permute-start(bf16[64,1024]{1,0:T(8,128)(2,1)S(1)} %collective-permute-done.1.refs_3_), channel_id=1, source_target_pairs={{0,2},{1,3},{2,4},{3,5},{4,6},{5,7},{6,8},{7,9},{8,10},{9,11},{10,... | collective-permute-start | bytes 393224 | tf_op jit(solution)/shard_map/ppermute | solution.py:30
  43.8 7.2 %collective-permute-start.6 = (bf16[64,1024]{1,0:T(8,128)(2,1)S(1)}, bf16[64,1024]{1,0:T(8,128)(2,1)S(1)}, u32[]{:S(2)}, u32[]{:S(2)}) collective-permute-start(bf16[64,1024]{1,0:T(8,128)(2,1)S(1)} %collective-permute-done.5.refs_6_), channel_id=1, source_target_pairs={{0,14},{1,15},{2,0},{3,1},{4,2},{5,3},{6,4},{7,5},{8,6},{9,7},{10,... | collective-permute-start | bytes 393224 | tf_op jit(solution)/shard_map/ppermute | solution.py:30
  51.0 0.9 copy-start.2
  51.9 0.9 copy-start.4
  54.2 7.7 %collective-permute-start.7 = (bf16[512,1024]{1,0:T(8,128)(2,1)S(1)}, bf16[512,1024]{1,0:T(8,128)(2,1)S(1)}, u32[]{:S(2)}, u32[]{:S(2)}) collective-permute-start(bf16[512,1024]{1,0:T(8,128)(2,1)S(1)} %assemble.1), channel_id=1, source_target_pairs={{0,1},{1,0},{2,3},{3,2},{4,5},{5,4},{6,7},{7,6},{8,9},{9,8},{10,11... | collective-permute-start | bytes 3145736 | tf_op jit(solution)/shard_map/ppermute | solution.py:30
  62.7 1.0 copy-start.6
  64.3 1.3 copy-start.7
  147.2 13.0 %all-to-all-start.7 = ((f32[32,8,128]{2,1,0:T(8,128)}), f32[32,8,128]{2,1,0:T(8,128)S(1)}, u32[]{:S(2)}, u32[]{:S(2)}) async-start(f32[32,8,128]{2,1,0:T(8,128)} %get-tuple-element.33), calls=%async_computation.7 | async-start | bytes 262144 | tf_op jit(solution)/shard_map/all_to_all | solution.py:278

commit v10 on v9

--- a/solution.py
+++ b/solution.py
@@ -13,7 +13,6 @@
 SCALE = 2.0 / EPSILON * LOG2E
 BACK = EPSILON / LOG2E
 NX, NZ, NY, NC = 4, 8, 8, 2
-RING = (0, -1, 1, -2, 2, -3, 3, 4)
 N = 1024
 LANES = 128
 GROUPS = N // LANES
@@ -30,11 +29,12 @@
     return lax.ppermute(values, "col", pairs)
 
 
+def move_y(values, steps):
+    return move_col(values, lambda y, core: (y + steps, core))
+
+
 def ring_step(ahead, back):
-    return (
-        move_col(ahead, lambda y, core: (y + 1, core)),
-        move_col(back, lambda y, core: (y - 1, core)),
-    )
+    return move_y(ahead, 1), move_y(back, -1)
 
 
 def spread(values, count, lines):
@@ -56,27 +56,34 @@
     along_z = [[x * NZ + z for z in range(NZ)] for x in range(NX)]
     along_x = [[x * NZ + z for x in range(NX)] for z in range(NZ)]
     line = spread(target_points, NZ, along_z)
-    held = {0: source_points}
-    held[-1], held[1] = ring_step(source_points, source_points)
-    held[-2], held[2] = ring_step(held[-1], held[1])
-    held[-2], held[2], line, masses = lax.optimization_barrier((held[-2], held[2], line, masses))
+    before, after = ring_step(source_points, source_points)
+    before, after, line, masses = lax.optimization_barrier((before, after, line, masses))
     target = spread(line, NX, along_x)
-    held[-3], held[3] = ring_step(held[-2], held[2])
-    held[4] = move_col(held[3], lambda y, core: (y - 1, core))
-    mine = assemble([held[place] for place in RING])
+    half = source_points.shape[0] // 2
+    two_before = move_y(jnp.concatenate([source_points, before], axis=0), 2)
+    two_after = move_y(jnp.concatenate([source_points, after], axis=0), -2)
+    far_low, far_high = move_y(after[:half], -3), move_y(before[half:], 3)
+    mine = assemble([source_points, before, after, two_before, two_after, far_low, far_high])
     other = move_col(mine, lambda y, core: (y, 1 - core))
     return mine, other, target, masses
 
 
 def assemble_kernel(*refs):
-    pieces = refs[: len(RING)]
-    out, sems = refs[len(RING) :]
+    pieces, (out, sems) = refs[:7], refs[7:]
+    rows = pieces[0].shape[0]
+    half = rows // 2
+    moves = [(0, 0, 0, 0), (1, 0, -1, 0), (2, 0, 1, 0), (3, 0, -2, 0), (3, rows, -3, 0)]
+    moves += [(4, 0, 2, 0), (4, rows, 3, 0), (5, 0, 4, 0), (6, 0, 4, half)]
     y = lax.axis_index("col") // NC
     made = []
-    for k, ref in enumerate(pieces):
-        rows = ref.shape[0]
-        start = pl.multiple_of((y + RING[k] + NY) % NY * rows, rows)
-        made.append(pltpu.make_async_copy(ref, out.at[pl.ds(start, rows)], sems.at[k]))
+    for k, (piece, first, place, offset) in enumerate(moves):
+        size = min(rows, pieces[piece].shape[0])
+        start = pl.multiple_of((y + place + NY) % NY * rows + offset, half)
+        made.append(
+            pltpu.make_async_copy(
+                pieces[piece].at[pl.ds(first, size)], out.at[pl.ds(start, size)], sems.at[k]
+            )
+        )
         made[-1].start()
     for copy in made:
         copy.wait()
@@ -182,9 +189,9 @@
     return pl.pallas_call(
         assemble_kernel,
         out_shape=jax.ShapeDtypeStruct((NY * rows, depth), jnp.bfloat16),
-        in_specs=[HBM] * len(RING),
+        in_specs=[HBM] * len(pieces),
         out_specs=VMEM,
-        scratch_shapes=[pltpu.SemaphoreType.DMA((len(RING),))],
+        scratch_shapes=[pltpu.SemaphoreType.DMA((9,))],
         compiler_params=PARAMS,
         cost_estimate=pl.CostEstimate(flops=0, bytes_accessed=2**22, transcendentals=0),
         name="assemble",

time: 162 us -> 161 us (level)
  waiting for transfers between devices: 15.2 us -> 29.3 us
  blocking collectives: 71.9 us -> 63 us
  starting transfers between devices: 50.1 us -> 45.6 us
  local copies, waits for them, and re-layouts: 4.55 us -> 2.74 us
    ppermute x8 -> x7, waiting for transfers between devices: 5.46 us -> 15.5 us  [move_col(): return lax.ppermute(values, 'col', pairs)]
    all_to_all x2, blocking collectives: 31.6 us -> 25.9 us  [local(): parts = lax.all_to_all(part, 'row', 0, 0)]
    ppermute x8 -> x7, starting transfers between devices: 31.2 us -> 26.7 us  [move_col(): return lax.ppermute(values, 'col', pairs)]
    all_to_all x2, waiting for transfers between devices: 1.33 us -> 5.43 us  [spread(): out = lax.all_to_all(copies, 'row', 0, 0, axis_index_groups=lines)]
    all_to_all x3, blocking collectives: 40.3 us -> 37.1 us  [local(): parts = lax.all_to_all(part, 'col', 0, 0)]
    unnamed x16 -> x8, local copies, waits for them, and re-layouts: 3.64 us -> 1.82 us
  transfers between devices with their start and end apart: 11 -> 10, of which waited for: 6 -> 6; matrix products, arithmetic and copies ran while one was open for 2% -> 2% of each run, Pallas kernels for 1% -> 1%
where the time goes in v10:
time: 161 us; the launch traced here: 160 us
  blocking collectives  63 us (39%)
  starting transfers between devices  45.6 us (28%)
  waiting for transfers between devices  29.3 us (18%)
  Pallas kernels  14.1 us (9%)
  local copies, waits for them, and re-layouts  2.74 us (2%)
  matrix products  2.59 us (2%)
  other arithmetic  1.71 us (1%)
    all_to_all x3, blocking collectives, local(): parts = lax.all_to_all(part, 'col', 0, 0)  37.1 us
    ppermute x7, starting transfers between devices, move_col(): return lax.ppermute(values, 'col', pairs)  26.7 us
    all_to_all x2, blocking collectives, local(): parts = lax.all_to_all(part, 'row', 0, 0)  25.9 us
    ppermute x7, waiting for transfers between devices, move_col(): return lax.ppermute(values, 'col', pairs)  15.5 us
    all_to_all x2, starting transfers between devices, spread(): out = lax.all_to_all(copies, 'row', 0, 0, axis_index_groups=lines)  15 us
    pallas_call x7, Pallas kernels, call(): pl.pallas_call(kernel, out_shape=[jax.ShapeDtypeStruct(shape, F32) for sh...  9.06 us
    all_to_all x1, waiting for transfers between devices, local(): parts = lax.all_to_all(part, 'row', 0, 0)  8.39 us
    all_to_all x2, waiting for transfers between devices, spread(): out = lax.all_to_all(copies, 'row', 0, 0, axis_index_groups=lines)  5.43 us
  transfers between devices with their start and end apart: 10, of which 6 were waited for; matrix products, arithmetic and copies ran while one was open for 2% of the time, Pallas kernels for 1%

profile of v10, /device:TPU:1, one launch (start us, length us, event | category | flops | bytes accessed | tf_op | source)
XLA Modules:
  0.0 159.9 jit_solution(2407801415775033077)
XLA Ops:
  0.6 0.8 copy-done.1
  1.5 0.9 copies.2
  2.3 10.9 %all-to-all-start = ((bf16[8,32,1024]{2,1,0:T(8,128)(2,1)}), bf16[8,32,1024]{2,1,0:T(8,128)(2,1)S(1)}, u32[]{:S(2)}, u32[]{:S(2)}) async-start(bf16[8,32,1024]{2,1,0:T(8,128)(2,1)} %copies.2), calls=%async_computation | async-start | bytes 1048576 | tf_op jit(solution)/shard_map/all_to_all | solution.py:51
  13.2 5.1 %collective-permute-start.1 = (bf16[64,1024]{1,0:T(8,128)(2,1)}, bf16[64,1024]{1,0:T(8,128)(2,1)S(1)}, u32[]{:S(2)}, u32[]{:S(2)}) collective-permute-start(bf16[64,1024]{1,0:T(8,128)(2,1)} %refs_0_.1), channel_id=1, source_target_pairs={{0,14},{1,15},{2,0},{3,1},{4,2},{5,3},{6,4},{7,5},{8,6},{9,7},{10,... | collective-permute-start | bytes 393224 | tf_op jit(solution)/shard_map/ppermute | solution.py:29
  18.3 1.9 %collective-permute-start = (bf16[64,1024]{1,0:T(8,128)(2,1)}, bf16[64,1024]{1,0:T(8,128)(2,1)S(1)}, u32[]{:S(2)}, u32[]{:S(2)}) collective-permute-start(bf16[64,1024]{1,0:T(8,128)(2,1)} %refs_0_.1), channel_id=1, source_target_pairs={{0,2},{1,3},{2,4},{3,5},{4,6},{5,7},{6,8},{7,9},{8,10},{9,11},{10,... | collective-permute-start | bytes 393224 | tf_op jit(solution)/shard_map/ppermute | solution.py:29
  20.2 0.7 broadcast_multiply_fusion
  20.9 0.1 reshape.32
  21.0 0.1 reshape.33.mass
  21.1 0.7 multiply_bitcast_fusion.mass
  21.8 0.0 collective-permute-done.1.refs_2_
  21.8 4.0 %collective-permute-done.refs_1_ = bf16[64,1024]{1,0:T(8,128)(2,1)S(1)} collective-permute-done((bf16[64,1024]{1,0:T(8,128)(2,1)}, bf16[64,1024]{1,0:T(8,128)(2,1)S(1)}, u32[]{:S(2)}, u32[]{:S(2)}) %collective-permute-start) | collective-permute-done | bytes 131104 | tf_op jit(solution)/shard_map/ppermute | solution.py:29
  25.7 5.4 %all-to-all-done = bf16[8,32,1024]{2,1,0:T(8,128)(2,1)S(1)} async-done(((bf16[8,32,1024]{2,1,0:T(8,128)(2,1)}), bf16[8,32,1024]{2,1,0:T(8,128)(2,1)S(1)}, u32[]{:S(2)}, u32[]{:S(2)}) %all-to-all-start) | async-done | bytes 524320 | tf_op jit(solution)/shard_map/all_to_all | solution.py:51
  31.2 1.4 copies.3
  32.6 0.0 copy-start
  32.6 4.2 %all-to-all-start.1 = ((bf16[4,256,1024]{2,1,0:T(8,128)(2,1)}), bf16[4,256,1024]{2,1,0:T(8,128)(2,1)S(1)}, u32[]{:S(2)}, u32[]{:S(2)}) async-start(bf16[4,256,1024]{2,1,0:T(8,128)(2,1)} %copies.3), calls=%async_computation.1 | async-start | bytes 4194304 | tf_op jit(solution)/shard_map/all_to_all | solution.py:51
  36.8 5.9 %collective-permute-start.3 = (bf16[128,1024]{1,0:T(8,128)(2,1)S(1)}, bf16[128,1024]{1,0:T(8,128)(2,1)S(1)}, u32[]{:S(2)}, u32[]{:S(2)}) collective-permute-start(bf16[128,1024]{1,0:T(8,128)(2,1)S(1)} %get-tuple-element.34), channel_id=1, source_target_pairs={{0,12},{1,13},{2,14},{3,15},{4,0},{5,1},{6,2},{7,3},{8,4},{9,5},{1... | collective-permute-start | bytes 786440 | tf_op jit(solution)/shard_map/ppermute | solution.py:29
  42.7 1.9 %collective-permute-start.2 = (bf16[128,1024]{1,0:T(8,128)(2,1)S(1)}, bf16[128,1024]{1,0:T(8,128)(2,1)S(1)}, u32[]{:S(2)}, u32[]{:S(2)}) collective-permute-start(bf16[128,1024]{1,0:T(8,128)(2,1)S(1)} %get-tuple-element.35), channel_id=1, source_target_pairs={{0,4},{1,5},{2,6},{3,7},{4,8},{5,9},{6,10},{7,11},{8,12},{9,13},{1... | collective-permute-start | bytes 786440 | tf_op jit(solution)/shard_map/ppermute | solution.py:29
  44.6 5.0 %collective-permute-start.4 = (bf16[32,1024]{1,0:T(8,128)(2,1)S(1)}, bf16[32,1024]{1,0:T(8,128)(2,1)S(1)}, u32[]{:S(2)}, u32[]{:S(2)}) collective-permute-start(bf16[32,1024]{1,0:T(8,128)(2,1)S(1)} %slice.6), channel_id=1, source_target_pairs={{0,10},{1,11},{2,12},{3,13},{4,14},{5,15},{6,0},{7,1},{8,2},{9,3},... | collective-permute-start | bytes 196616 | tf_op jit(solution)/shard_map/ppermute | solution.py:29
  49.7 2.0 %collective-permute-start.5 = (bf16[32,1024]{1,0:T(8,128)(2,1)S(1)}, bf16[32,1024]{1,0:T(8,128)(2,1)S(1)}, u32[]{:S(2)}, u32[]{:S(2)}) collective-permute-start(bf16[32,1024]{1,0:T(8,128)(2,1)S(1)} %slice.7), channel_id=1, source_target_pairs={{0,6},{1,7},{2,8},{3,9},{4,10},{5,11},{6,12},{7,13},{8,14},{9,15},... | collective-permute-start | bytes 196616 | tf_op jit(solution)/shard_map/ppermute | solution.py:29
  51.7 6.5 %collective-permute-done.4.refs_5_ = bf16[32,1024]{1,0:T(8,128)(2,1)S(1)} collective-permute-done((bf16[32,1024]{1,0:T(8,128)(2,1)S(1)}, bf16[32,1024]{1,0:T(8,128)(2,1)S(1)}, u32[]{:S(2)}, u32[]{:S(2)}) %collective-permute-start.4) | collective-permute-done | bytes 65568 | tf_op jit(solution)/shard_map/ppermute | solution.py:29
  58.2 3.0 %collective-permute-done.5.refs_6_ = bf16[32,1024]{1,0:T(8,128)(2,1)S(1)} collective-permute-done((bf16[32,1024]{1,0:T(8,128)(2,1)S(1)}, bf16[32,1024]{1,0:T(8,128)(2,1)S(1)}, u32[]{:S(2)}, u32[]{:S(2)}) %collective-permute-start.5) | collective-permute-done | bytes 65568 | tf_op jit(solution)/shard_map/ppermute | solution.py:29
  61.2 0.0 collective-permute-done.3.refs_4_
  61.3 1.5 assemble.1
  62.7 4.8 %collective-permute-start.6 = (bf16[512,1024]{1,0:T(8,128)(2,1)S(1)}, bf16[512,1024]{1,0:T(8,128)(2,1)S(1)}, u32[]{:S(2)}, u32[]{:S(2)}) collective-permute-start(bf16[512,1024]{1,0:T(8,128)(2,1)S(1)} %assemble.1), channel_id=1, source_target_pairs={{0,1},{1,0},{2,3},{3,2},{4,5},{5,4},{6,7},{7,6},{8,9},{9,8},{10,11... | collective-permute-start | bytes 3145736 | tf_op jit(solution)/shard_map/ppermute | solution.py:29
  67.6 0.3 multiply_reduce_fusion
  67.8 2.0 %collective-permute-done.6.points = bf16[512,1024]{1,0:T(8,128)(2,1)S(1)} collective-permute-done((bf16[512,1024]{1,0:T(8,128)(2,1)S(1)}, bf16[512,1024]{1,0:T(8,128)(2,1)S(1)}, u32[]{:S(2)}, u32[]{:S(2)}) %collective-permute-start.6) | collective-permute-done | bytes 1048608 | tf_op jit(solution)/shard_map/ppermute | solution.py:29
  69.8 0.8 place.1
  70.6 1.0 copy-done.2
  71.6 0.0 all-to-all-done.1
  71.6 0.6 in_place_squares.1
  72.2 1.3 convolution_multiply_fusion.1.mine
  73.5 1.3 convolution_multiply_fusion.other
  74.8 1.2 first_kernel.1
  76.0 12.4 %all_to_all.40.parts = f32[16,8,128]{2,1,0:T(8,128)S(1)} all-to-all(f32[16,8,128]{2,1,0:T(8,128)S(1)} %first_kernel.1), channel_id=1, replica_groups=mesh['row'=32,'col'=16] {'col'}, dimensions={0} | all-to-all | bytes 131072 | tf_op jit(solution)/shard_map/all_to_all | solution.py:281
  88.4 1.6 target_kernel.3
  89.9 13.5 %all_to_all.41.parts = f32[32,8,128]{2,1,0:T(8,128)S(1)} all-to-all(f32[32,8,128]{2,1,0:T(8,128)S(1)} %get-tuple-element.30), channel_id=1, replica_groups=mesh['row'=32,'col'=16] {'row'}, dimensions={0} | all-to-all | bytes 262144 | tf_op jit(solution)/shard_map/all_to_all | solution.py:285
  103.5 1.2 source_kernel.2
  104.7 12.3 %all_to_all.42.parts = f32[16,8,128]{2,1,0:T(8,128)S(1)} all-to-all(f32[16,8,128]{2,1,0:T(8,128)S(1)} %source_kernel.2), channel_id=1, replica_groups=mesh['row'=32,'col'=16] {'col'}, dimensions={0} | all-to-all | bytes 131072 | tf_op jit(solution)/shard_map/all_to_all | solution.py:281
  117.0 1.6 target_kernel.4
  118.6 12.4 %all_to_all.43.parts = f32[32,8,128]{2,1,0:T(8,128)S(1)} all-to-all(f32[32,8,128]{2,1,0:T(8,128)S(1)} %get-tuple-element.31), channel_id=1, replica_groups=mesh['row'=32,'col'=16] {'row'}, dimensions={0} | all-to-all | bytes 262144 | tf_op jit(solution)/shard_map/all_to_all | solution.py:285
  131.0 1.2 source_kernel.3
  132.2 12.3 %all_to_all.44.parts = f32[16,8,128]{2,1,0:T(8,128)S(1)} all-to-all(f32[16,8,128]{2,1,0:T(8,128)S(1)} %source_kernel.3), channel_id=1, replica_groups=mesh['row'=32,'col'=16] {'col'}, dimensions={0} | all-to-all | bytes 131072 | tf_op jit(solution)/shard_map/all_to_all | solution.py:281
  144.5 1.7 %target_kernel.5 = (f32[32,8,128]{2,1,0:T(8,128)}, f32[8,128]{1,0:T(8,128)S(1)}) custom-call(f32[16,8,128]{2,1,0:T(8,128)S(1)} %all_to_all.44.parts, f32[8,128]{1,0:T(8,128)S(1)} %reshape.33.mass, f32[8,128]{1,0:T(8,128)S(1)} %pad_maximum_fusion.2.squares, f32[512,1024]{1,0:T(8,128)S(1)} %convolution_multiply_fusion.1.mine, ...), custom_call_target="tpu_custom_call" | custom-call | flops 6291456 | bytes 4194304 | tf_op jit(solution)/shard_map/target_kernel/pallas_call | solution.py:241
  146.2 3.9 %all-to-all-start.7 = ((f32[32,8,128]{2,1,0:T(8,128)}), f32[32,8,128]{2,1,0:T(8,128)S(1)}, u32[]{:S(2)}, u32[]{:S(2)}) async-start(f32[32,8,128]{2,1,0:T(8,128)} %get-tuple-element.33), calls=%async_computation.7 | async-start | bytes 262144 | tf_op jit(solution)/shard_map/all_to_all | solution.py:285
  150.1 0.1 reshape.37
  150.2 0.7 reshape.38
  150.9 8.4 %all-to-all-done.7.parts = f32[32,8,128]{2,1,0:T(8,128)S(1)} async-done(((f32[32,8,128]{2,1,0:T(8,128)}), f32[32,8,128]{2,1,0:T(8,128)S(1)}, u32[]{:S(2)}, u32[]{:S(2)}) %all-to-all-start.7) | async-done | bytes 131104 | tf_op jit(solution)/shard_map/all_to_all | solution.py:285
  159.2 0.7 last_kernel.1
  (12 shorter events, 0.1 us)
Async XLA Ops:
  0.6 0.8 copy-start.1
  2.3 28.8 %all-to-all-start = ((bf16[8,32,1024]{2,1,0:T(8,128)(2,1)}), bf16[8,32,1024]{2,1,0:T(8,128)(2,1)S(1)}, u32[]{:S(2)}, u32[]{:S(2)}) async-start(bf16[8,32,1024]{2,1,0:T(8,128)(2,1)} %copies.2), calls=%async_computation | async-start | bytes 1048576 | tf_op jit(solution)/shard_map/all_to_all | solution.py:51
  13.2 8.6 %collective-permute-start.1 = (bf16[64,1024]{1,0:T(8,128)(2,1)}, bf16[64,1024]{1,0:T(8,128)(2,1)S(1)}, u32[]{:S(2)}, u32[]{:S(2)}) collective-permute-start(bf16[64,1024]{1,0:T(8,128)(2,1)} %refs_0_.1), channel_id=1, source_target_pairs={{0,14},{1,15},{2,0},{3,1},{4,2},{5,3},{6,4},{7,5},{8,6},{9,7},{10,... | collective-permute-start | bytes 393224 | tf_op jit(solution)/shard_map/ppermute | solution.py:29
  18.3 7.4 %collective-permute-start = (bf16[64,1024]{1,0:T(8,128)(2,1)}, bf16[64,1024]{1,0:T(8,128)(2,1)S(1)}, u32[]{:S(2)}, u32[]{:S(2)}) collective-permute-start(bf16[64,1024]{1,0:T(8,128)(2,1)} %refs_0_.1), channel_id=1, source_target_pairs={{0,2},{1,3},{2,4},{3,5},{4,6},{5,7},{6,8},{7,9},{8,10},{9,11},{10,... | collective-permute-start | bytes 393224 | tf_op jit(solution)/shard_map/ppermute | solution.py:29
  32.6 4.2 %copy-start = (bf16[64,1024]{1,0:T(8,128)(2,1)S(1)}, bf16[64,1024]{1,0:T(8,128)(2,1)}, u32[]{:S(2)}) copy-start(bf16[64,1024]{1,0:T(8,128)(2,1)} %refs_0_.1) | copy-start | bytes 393220
  32.6 39.0 %all-to-all-start.1 = ((bf16[4,256,1024]{2,1,0:T(8,128)(2,1)}), bf16[4,256,1024]{2,1,0:T(8,128)(2,1)S(1)}, u32[]{:S(2)}, u32[]{:S(2)}) async-start(bf16[4,256,1024]{2,1,0:T(8,128)(2,1)} %copies.3), calls=%async_computation.1 | async-start | bytes 4194304 | tf_op jit(solution)/shard_map/all_to_all | solution.py:51
  36.8 24.5 %collective-permute-start.3 = (bf16[128,1024]{1,0:T(8,128)(2,1)S(1)}, bf16[128,1024]{1,0:T(8,128)(2,1)S(1)}, u32[]{:S(2)}, u32[]{:S(2)}) collective-permute-start(bf16[128,1024]{1,0:T(8,128)(2,1)S(1)} %get-tuple-element.34), channel_id=1, source_target_pairs={{0,12},{1,13},{2,14},{3,15},{4,0},{5,1},{6,2},{7,3},{8,4},{9,5},{1... | collective-permute-start | bytes 786440 | tf_op jit(solution)/shard_map/ppermute | solution.py:29
  42.7 18.6 %collective-permute-start.2 = (bf16[128,1024]{1,0:T(8,128)(2,1)S(1)}, bf16[128,1024]{1,0:T(8,128)(2,1)S(1)}, u32[]{:S(2)}, u32[]{:S(2)}) collective-permute-start(bf16[128,1024]{1,0:T(8,128)(2,1)S(1)} %get-tuple-element.35), channel_id=1, source_target_pairs={{0,4},{1,5},{2,6},{3,7},{4,8},{5,9},{6,10},{7,11},{8,12},{9,13},{1... | collective-permute-start | bytes 786440 | tf_op jit(solution)/shard_map/ppermute | solution.py:29
  44.6 13.6 %collective-permute-start.4 = (bf16[32,1024]{1,0:T(8,128)(2,1)S(1)}, bf16[32,1024]{1,0:T(8,128)(2,1)S(1)}, u32[]{:S(2)}, u32[]{:S(2)}) collective-permute-start(bf16[32,1024]{1,0:T(8,128)(2,1)S(1)} %slice.6), channel_id=1, source_target_pairs={{0,10},{1,11},{2,12},{3,13},{4,14},{5,15},{6,0},{7,1},{8,2},{9,3},... | collective-permute-start | bytes 196616 | tf_op jit(solution)/shard_map/ppermute | solution.py:29
  49.7 11.6 %collective-permute-start.5 = (bf16[32,1024]{1,0:T(8,128)(2,1)S(1)}, bf16[32,1024]{1,0:T(8,128)(2,1)S(1)}, u32[]{:S(2)}, u32[]{:S(2)}) collective-permute-start(bf16[32,1024]{1,0:T(8,128)(2,1)S(1)} %slice.7), channel_id=1, source_target_pairs={{0,6},{1,7},{2,8},{3,9},{4,10},{5,11},{6,12},{7,13},{8,14},{9,15},... | collective-permute-start | bytes 196616 | tf_op jit(solution)/shard_map/ppermute | solution.py:29
  62.7 7.1 %collective-permute-start.6 = (bf16[512,1024]{1,0:T(8,128)(2,1)S(1)}, bf16[512,1024]{1,0:T(8,128)(2,1)S(1)}, u32[]{:S(2)}, u32[]{:S(2)}) collective-permute-start(bf16[512,1024]{1,0:T(8,128)(2,1)S(1)} %assemble.1), channel_id=1, source_target_pairs={{0,1},{1,0},{2,3},{3,2},{4,5},{5,4},{6,7},{7,6},{8,9},{9,8},{10,11... | collective-permute-start | bytes 3145736 | tf_op jit(solution)/shard_map/ppermute | solution.py:29
  70.6 1.0 copy-start.2
  72.2 1.3 copy-start.3
  146.2 13.0 %all-to-all-start.7 = ((f32[32,8,128]{2,1,0:T(8,128)}), f32[32,8,128]{2,1,0:T(8,128)S(1)}, u32[]{:S(2)}, u32[]{:S(2)}) async-start(f32[32,8,128]{2,1,0:T(8,128)} %get-tuple-element.33), calls=%async_computation.7 | async-start | bytes 262144 | tf_op jit(solution)/shard_map/all_to_all | solution.py:285

commit v11 on v10

--- a/solution.py
+++ b/solution.py
@@ -57,23 +57,27 @@
     along_x = [[x * NZ + z for x in range(NX)] for z in range(NZ)]
     line = spread(target_points, NZ, along_z)
     before, after = ring_step(source_points, source_points)
-    before, after, line, masses = lax.optimization_barrier((before, after, line, masses))
+    before_2, after_2 = move_y(source_points, 2), move_y(source_points, -2)
+    before, after, before_2, after_2, line, masses = lax.optimization_barrier(
+        (before, after, before_2, after_2, line, masses)
+    )
     target = spread(line, NX, along_x)
     half = source_points.shape[0] // 2
-    two_before = move_y(jnp.concatenate([source_points, before], axis=0), 2)
-    two_after = move_y(jnp.concatenate([source_points, after], axis=0), -2)
+    before_3, after_3 = move_y(before, 2), move_y(after, -2)
     far_low, far_high = move_y(after[:half], -3), move_y(before[half:], 3)
-    mine = assemble([source_points, before, after, two_before, two_after, far_low, far_high])
+    near = [source_points, before, after, before_2, after_2, before_3, after_3]
+    mine = assemble(near + [far_low, far_high])
     other = move_col(mine, lambda y, core: (y, 1 - core))
     return mine, other, target, masses
 
 
 def assemble_kernel(*refs):
-    pieces, (out, sems) = refs[:7], refs[7:]
+    pieces, (out, sems) = refs[:9], refs[9:]
     rows = pieces[0].shape[0]
     half = rows // 2
-    moves = [(0, 0, 0, 0), (1, 0, -1, 0), (2, 0, 1, 0), (3, 0, -2, 0), (3, rows, -3, 0)]
-    moves += [(4, 0, 2, 0), (4, rows, 3, 0), (5, 0, 4, 0), (6, 0, 4, half)]
+    places = (0, -1, 1, -2, 2, -3, 3)
+    moves = [(k, 0, place, 0) for k, place in enumerate(places)]
+    moves += [(7, 0, 4, 0), (8, 0, 4, half)]
     y = lax.axis_index("col") // NC
     made = []
     for k, (piece, first, place, offset) in enumerate(moves):

time: 161 us -> 168 us (1.043)
  waiting for transfers between devices: 29.3 us -> 19.6 us
  starting transfers between devices: 45.6 us -> 55.2 us
  blocking collectives: 63 us -> 68.8 us
  local copies, waits for them, and re-layouts: 2.74 us -> 4.55 us
    ppermute x7 -> x9, starting transfers between devices: 26.7 us -> 36.3 us  [move_col(): return lax.ppermute(values, 'col', pairs)]
    all_to_all x2, waiting for transfers between devices: 5.43 us -> 0.14 us  [spread(): out = lax.all_to_all(copies, 'row', 0, 0, axis_index_groups=lines)]
    all_to_all x2, blocking collectives: 25.9 us -> 31.1 us  [local(): parts = lax.all_to_all(part, 'row', 0, 0)]
    ppermute x7 -> x9, waiting for transfers between devices: 15.5 us -> 11.1 us  [move_col(): return lax.ppermute(values, 'col', pairs)]
    unnamed x8 -> x16, local copies, waits for them, and re-layouts: 1.82 us -> 3.63 us
  transfers between devices with their start and end apart: 10 -> 12, of which waited for: 6 -> 6; matrix products, arithmetic and copies ran while one was open for 2% -> 2% of each run, Pallas kernels for 1% -> 1%
where the time goes in v11:
time: 168 us; the launch traced here: 167 us
  blocking collectives  68.8 us (41%)
  starting transfers between devices  55.2 us (33%)
  waiting for transfers between devices  19.6 us (12%)
  Pallas kernels  14.1 us (8%)
  local copies, waits for them, and re-layouts  4.55 us (3%)
  matrix products  2.6 us (2%)
    all_to_all x3, blocking collectives, local(): parts = lax.all_to_all(part, 'col', 0, 0)  37.6 us
    ppermute x9, starting transfers between devices, move_col(): return lax.ppermute(values, 'col', pairs)  36.3 us
    all_to_all x2, blocking collectives, local(): parts = lax.all_to_all(part, 'row', 0, 0)  31.1 us
    all_to_all x2, starting transfers between devices, spread(): out = lax.all_to_all(copies, 'row', 0, 0, axis_index_groups=lines)  15 us
    ppermute x9, waiting for transfers between devices, move_col(): return lax.ppermute(values, 'col', pairs)  11.1 us
    pallas_call x7, Pallas kernels, call(): pl.pallas_call(kernel, out_shape=[jax.ShapeDtypeStruct(shape, F32) for sh...  9.06 us
    all_to_all x1, waiting for transfers between devices, local(): parts = lax.all_to_all(part, 'row', 0, 0)  8.39 us
    all_to_all x1, starting transfers between devices, local(): parts = lax.all_to_all(part, 'row', 0, 0)  3.85 us
  transfers between devices with their start and end apart: 12, of which 6 were waited for; matrix products, arithmetic and copies ran while one was open for 2% of the time, Pallas kernels for 1%

profile of v11, /device:TPU:1, one launch (start us, length us, event | category | flops | bytes accessed | tf_op | source)
XLA Modules:
  0.0 167.4 jit_solution(13613433505450494704)
XLA Ops:
  0.6 0.8 copy-done.5
  1.5 0.9 copies.2
  2.4 10.9 %all-to-all-start = ((bf16[8,32,1024]{2,1,0:T(8,128)(2,1)}), bf16[8,32,1024]{2,1,0:T(8,128)(2,1)S(1)}, u32[]{:S(2)}, u32[]{:S(2)}) async-start(bf16[8,32,1024]{2,1,0:T(8,128)(2,1)} %copies.2), calls=%async_computation | async-start | bytes 1048576 | tf_op jit(solution)/shard_map/all_to_all | solution.py:51
  13.2 4.2 %collective-permute-start.2 = (bf16[64,1024]{1,0:T(8,128)(2,1)}, bf16[64,1024]{1,0:T(8,128)(2,1)S(1)}, u32[]{:S(2)}, u32[]{:S(2)}) collective-permute-start(bf16[64,1024]{1,0:T(8,128)(2,1)} %refs_0_.1), channel_id=1, source_target_pairs={{0,4},{1,5},{2,6},{3,7},{4,8},{5,9},{6,10},{7,11},{8,12},{9,13},{1... | collective-permute-start | bytes 393224 | tf_op jit(solution)/shard_map/ppermute | solution.py:29
  17.4 3.3 %collective-permute-start.1 = (bf16[64,1024]{1,0:T(8,128)(2,1)}, bf16[64,1024]{1,0:T(8,128)(2,1)S(1)}, u32[]{:S(2)}, u32[]{:S(2)}) collective-permute-start(bf16[64,1024]{1,0:T(8,128)(2,1)} %refs_0_.1), channel_id=1, source_target_pairs={{0,14},{1,15},{2,0},{3,1},{4,2},{5,3},{6,4},{7,5},{8,6},{9,7},{10,... | collective-permute-start | bytes 393224 | tf_op jit(solution)/shard_map/ppermute | solution.py:29
  20.7 2.0 %collective-permute-start = (bf16[64,1024]{1,0:T(8,128)(2,1)}, bf16[64,1024]{1,0:T(8,128)(2,1)S(1)}, u32[]{:S(2)}, u32[]{:S(2)}) collective-permute-start(bf16[64,1024]{1,0:T(8,128)(2,1)} %refs_0_.1), channel_id=1, source_target_pairs={{0,2},{1,3},{2,4},{3,5},{4,6},{5,7},{6,8},{7,9},{8,10},{9,11},{10,... | collective-permute-start | bytes 393224 | tf_op jit(solution)/shard_map/ppermute | solution.py:29
  22.7 3.7 %collective-permute-start.3 = (bf16[64,1024]{1,0:T(8,128)(2,1)}, bf16[64,1024]{1,0:T(8,128)(2,1)S(1)}, u32[]{:S(2)}, u32[]{:S(2)}) collective-permute-start(bf16[64,1024]{1,0:T(8,128)(2,1)} %refs_0_.1), channel_id=1, source_target_pairs={{0,12},{1,13},{2,14},{3,15},{4,0},{5,1},{6,2},{7,3},{8,4},{9,5},{1... | collective-permute-start | bytes 393224 | tf_op jit(solution)/shard_map/ppermute | solution.py:29
  26.5 0.7 broadcast_multiply_fusion
  27.1 0.1 reshape.32
  27.2 0.1 reshape.33.mass
  27.3 0.7 multiply_bitcast_fusion.mass
  28.0 3.0 %collective-permute-done.3.refs_4_ = bf16[64,1024]{1,0:T(8,128)(2,1)S(1)} collective-permute-done((bf16[64,1024]{1,0:T(8,128)(2,1)}, bf16[64,1024]{1,0:T(8,128)(2,1)S(1)}, u32[]{:S(2)}, u32[]{:S(2)}) %collective-permute-start.3) | collective-permute-done | bytes 131104 | tf_op jit(solution)/shard_map/ppermute | solution.py:29
  31.0 0.1 all-to-all-done
  31.2 1.4 copies.3
  32.6 4.2 %all-to-all-start.1 = ((bf16[4,256,1024]{2,1,0:T(8,128)(2,1)}), bf16[4,256,1024]{2,1,0:T(8,128)(2,1)S(1)}, u32[]{:S(2)}, u32[]{:S(2)}) async-start(bf16[4,256,1024]{2,1,0:T(8,128)(2,1)} %copies.3), calls=%async_computation.1 | async-start | bytes 4194304 | tf_op jit(solution)/shard_map/all_to_all | solution.py:51
  36.8 5.1 %collective-permute-start.4 = (bf16[64,1024]{1,0:T(8,128)(2,1)S(1)}, bf16[64,1024]{1,0:T(8,128)(2,1)S(1)}, u32[]{:S(2)}, u32[]{:S(2)}) collective-permute-start(bf16[64,1024]{1,0:T(8,128)(2,1)S(1)} %collective-permute-done.refs_1_), channel_id=1, source_target_pairs={{0,4},{1,5},{2,6},{3,7},{4,8},{5,9},{6,10},{7,11},{8,12},{9,13},{1... | collective-permute-start | bytes 393224 | tf_op jit(solution)/shard_map/ppermute | solution.py:29
  41.9 2.7 %collective-permute-start.5 = (bf16[64,1024]{1,0:T(8,128)(2,1)S(1)}, bf16[64,1024]{1,0:T(8,128)(2,1)S(1)}, u32[]{:S(2)}, u32[]{:S(2)}) collective-permute-start(bf16[64,1024]{1,0:T(8,128)(2,1)S(1)} %collective-permute-done.1.refs_2_), channel_id=1, source_target_pairs={{0,12},{1,13},{2,14},{3,15},{4,0},{5,1},{6,2},{7,3},{8,4},{9,5},{1... | collective-permute-start | bytes 393224 | tf_op jit(solution)/shard_map/ppermute | solution.py:29
  44.6 6.9 %collective-permute-start.6 = (bf16[32,1024]{1,0:T(8,128)(2,1)S(1)}, bf16[32,1024]{1,0:T(8,128)(2,1)S(1)}, u32[]{:S(2)}, u32[]{:S(2)}) collective-permute-start(bf16[32,1024]{1,0:T(8,128)(2,1)S(1)} %slice.6), channel_id=1, source_target_pairs={{0,10},{1,11},{2,12},{3,13},{4,14},{5,15},{6,0},{7,1},{8,2},{9,3},... | collective-permute-start | bytes 196616 | tf_op jit(solution)/shard_map/ppermute | solution.py:29
  51.5 1.9 %collective-permute-start.7 = (bf16[32,1024]{1,0:T(8,128)(2,1)S(1)}, bf16[32,1024]{1,0:T(8,128)(2,1)S(1)}, u32[]{:S(2)}, u32[]{:S(2)}) collective-permute-start(bf16[32,1024]{1,0:T(8,128)(2,1)S(1)} %slice.7), channel_id=1, source_target_pairs={{0,6},{1,7},{2,8},{3,9},{4,10},{5,11},{6,12},{7,13},{8,14},{9,15},... | collective-permute-start | bytes 196616 | tf_op jit(solution)/shard_map/ppermute | solution.py:29
  53.4 2.1 %collective-permute-done.6.refs_7_ = bf16[32,1024]{1,0:T(8,128)(2,1)S(1)} collective-permute-done((bf16[32,1024]{1,0:T(8,128)(2,1)S(1)}, bf16[32,1024]{1,0:T(8,128)(2,1)S(1)}, u32[]{:S(2)}, u32[]{:S(2)}) %collective-permute-start.6) | collective-permute-done | bytes 65568 | tf_op jit(solution)/shard_map/ppermute | solution.py:29
  55.5 4.0 %collective-permute-done.7.refs_8_ = bf16[32,1024]{1,0:T(8,128)(2,1)S(1)} collective-permute-done((bf16[32,1024]{1,0:T(8,128)(2,1)S(1)}, bf16[32,1024]{1,0:T(8,128)(2,1)S(1)}, u32[]{:S(2)}, u32[]{:S(2)}) %collective-permute-start.7) | collective-permute-done | bytes 65568 | tf_op jit(solution)/shard_map/ppermute | solution.py:29
  59.5 0.9 copy-done.2
  60.4 0.9 copy-done.4
  61.3 1.4 assemble.1
  62.8 6.5 %collective-permute-start.8 = (bf16[512,1024]{1,0:T(8,128)(2,1)S(1)}, bf16[512,1024]{1,0:T(8,128)(2,1)S(1)}, u32[]{:S(2)}, u32[]{:S(2)}) collective-permute-start(bf16[512,1024]{1,0:T(8,128)(2,1)S(1)} %assemble.1), channel_id=1, source_target_pairs={{0,1},{1,0},{2,3},{3,2},{4,5},{5,4},{6,7},{7,6},{8,9},{9,8},{10,11... | collective-permute-start | bytes 3145736 | tf_op jit(solution)/shard_map/ppermute | solution.py:29
  69.3 0.3 multiply_reduce_fusion
  69.6 2.0 %collective-permute-done.8.points = bf16[512,1024]{1,0:T(8,128)(2,1)S(1)} collective-permute-done((bf16[512,1024]{1,0:T(8,128)(2,1)S(1)}, bf16[512,1024]{1,0:T(8,128)(2,1)S(1)}, u32[]{:S(2)}, u32[]{:S(2)}) %collective-permute-start.8) | collective-permute-done | bytes 1048608 | tf_op jit(solution)/shard_map/ppermute | solution.py:29
  71.6 0.8 place.1
  72.4 1.0 copy-done.6
  73.4 0.6 in_place_squares.1
  73.9 1.3 convolution_multiply_fusion.1.mine
  75.3 1.3 convolution_multiply_fusion.other
  76.6 1.2 first_kernel.1
  77.7 13.0 %all_to_all.40.parts = f32[16,8,128]{2,1,0:T(8,128)S(1)} all-to-all(f32[16,8,128]{2,1,0:T(8,128)S(1)} %first_kernel.1), channel_id=1, replica_groups=mesh['row'=32,'col'=16] {'col'}, dimensions={0} | all-to-all | bytes 131072 | tf_op jit(solution)/shard_map/all_to_all | solution.py:285
  90.7 1.6 target_kernel.3
  92.2 18.7 %all_to_all.41.parts = f32[32,8,128]{2,1,0:T(8,128)S(1)} all-to-all(f32[32,8,128]{2,1,0:T(8,128)S(1)} %get-tuple-element.34), channel_id=1, replica_groups=mesh['row'=32,'col'=16] {'row'}, dimensions={0} | all-to-all | bytes 262144 | tf_op jit(solution)/shard_map/all_to_all | solution.py:289
  111.0 1.2 source_kernel.2
  112.2 12.3 %all_to_all.42.parts = f32[16,8,128]{2,1,0:T(8,128)S(1)} all-to-all(f32[16,8,128]{2,1,0:T(8,128)S(1)} %source_kernel.2), channel_id=1, replica_groups=mesh['row'=32,'col'=16] {'col'}, dimensions={0} | all-to-all | bytes 131072 | tf_op jit(solution)/shard_map/all_to_all | solution.py:285
  124.5 1.6 target_kernel.4
  126.1 12.4 %all_to_all.43.parts = f32[32,8,128]{2,1,0:T(8,128)S(1)} all-to-all(f32[32,8,128]{2,1,0:T(8,128)S(1)} %get-tuple-element.35), channel_id=1, replica_groups=mesh['row'=32,'col'=16] {'row'}, dimensions={0} | all-to-all | bytes 262144 | tf_op jit(solution)/shard_map/all_to_all | solution.py:289
  138.5 1.2 source_kernel.3
  139.7 12.3 %all_to_all.44.parts = f32[16,8,128]{2,1,0:T(8,128)S(1)} all-to-all(f32[16,8,128]{2,1,0:T(8,128)S(1)} %source_kernel.3), channel_id=1, replica_groups=mesh['row'=32,'col'=16] {'col'}, dimensions={0} | all-to-all | bytes 131072 | tf_op jit(solution)/shard_map/all_to_all | solution.py:285
  152.1 1.7 %target_kernel.5 = (f32[32,8,128]{2,1,0:T(8,128)}, f32[8,128]{1,0:T(8,128)S(1)}) custom-call(f32[16,8,128]{2,1,0:T(8,128)S(1)} %all_to_all.44.parts, f32[8,128]{1,0:T(8,128)S(1)} %reshape.33.mass, f32[8,128]{1,0:T(8,128)S(1)} %pad_maximum_fusion.squares, f32[512,1024]{1,0:T(8,128)S(1)} %convolution_multiply_fusion.1.mine, ...), custom_call_target="tpu_custom_call" | custom-call | flops 6291456 | bytes 4194304 | tf_op jit(solution)/shard_map/target_kernel/pallas_call | solution.py:245
  153.8 3.9 %all-to-all-start.7 = ((f32[32,8,128]{2,1,0:T(8,128)}), f32[32,8,128]{2,1,0:T(8,128)S(1)}, u32[]{:S(2)}, u32[]{:S(2)}) async-start(f32[32,8,128]{2,1,0:T(8,128)} %get-tuple-element.37), calls=%async_computation.7 | async-start | bytes 262144 | tf_op jit(solution)/shard_map/all_to_all | solution.py:289
  157.6 0.1 reshape.37
  157.7 0.7 reshape.38
  158.4 8.4 %all-to-all-done.7.parts = f32[32,8,128]{2,1,0:T(8,128)S(1)} async-done(((f32[32,8,128]{2,1,0:T(8,128)}), f32[32,8,128]{2,1,0:T(8,128)S(1)}, u32[]{:S(2)}, u32[]{:S(2)}) %all-to-all-start.7) | async-done | bytes 131104 | tf_op jit(solution)/shard_map/all_to_all | solution.py:289
  166.8 0.7 last_kernel.1
  (23 shorter events, 0.1 us)
Async XLA Ops:
  0.6 0.8 copy-start.5
  2.4 28.8 %all-to-all-start = ((bf16[8,32,1024]{2,1,0:T(8,128)(2,1)}), bf16[8,32,1024]{2,1,0:T(8,128)(2,1)S(1)}, u32[]{:S(2)}, u32[]{:S(2)}) async-start(bf16[8,32,1024]{2,1,0:T(8,128)(2,1)} %copies.2), calls=%async_computation | async-start | bytes 1048576 | tf_op jit(solution)/shard_map/all_to_all | solution.py:51
  13.2 14.8 %collective-permute-start.2 = (bf16[64,1024]{1,0:T(8,128)(2,1)}, bf16[64,1024]{1,0:T(8,128)(2,1)S(1)}, u32[]{:S(2)}, u32[]{:S(2)}) collective-permute-start(bf16[64,1024]{1,0:T(8,128)(2,1)} %refs_0_.1), channel_id=1, source_target_pairs={{0,4},{1,5},{2,6},{3,7},{4,8},{5,9},{6,10},{7,11},{8,12},{9,13},{1... | collective-permute-start | bytes 393224 | tf_op jit(solution)/shard_map/ppermute | solution.py:29
  17.4 10.6 %collective-permute-start.1 = (bf16[64,1024]{1,0:T(8,128)(2,1)}, bf16[64,1024]{1,0:T(8,128)(2,1)S(1)}, u32[]{:S(2)}, u32[]{:S(2)}) collective-permute-start(bf16[64,1024]{1,0:T(8,128)(2,1)} %refs_0_.1), channel_id=1, source_target_pairs={{0,14},{1,15},{2,0},{3,1},{4,2},{5,3},{6,4},{7,5},{8,6},{9,7},{10,... | collective-permute-start | bytes 393224 | tf_op jit(solution)/shard_map/ppermute | solution.py:29
  20.7 7.3 %collective-permute-start = (bf16[64,1024]{1,0:T(8,128)(2,1)}, bf16[64,1024]{1,0:T(8,128)(2,1)S(1)}, u32[]{:S(2)}, u32[]{:S(2)}) collective-permute-start(bf16[64,1024]{1,0:T(8,128)(2,1)} %refs_0_.1), channel_id=1, source_target_pairs={{0,2},{1,3},{2,4},{3,5},{4,6},{5,7},{6,8},{7,9},{8,10},{9,11},{10,... | collective-permute-start | bytes 393224 | tf_op jit(solution)/shard_map/ppermute | solution.py:29
  22.7 8.3 %collective-permute-start.3 = (bf16[64,1024]{1,0:T(8,128)(2,1)}, bf16[64,1024]{1,0:T(8,128)(2,1)S(1)}, u32[]{:S(2)}, u32[]{:S(2)}) collective-permute-start(bf16[64,1024]{1,0:T(8,128)(2,1)} %refs_0_.1), channel_id=1, source_target_pairs={{0,12},{1,13},{2,14},{3,15},{4,0},{5,1},{6,2},{7,3},{8,4},{9,5},{1... | collective-permute-start | bytes 393224 | tf_op jit(solution)/shard_map/ppermute | solution.py:29
  28.0 4.6 %copy-start.1 = (bf16[64,1024]{1,0:T(8,128)(2,1)}, bf16[64,1024]{1,0:T(8,128)(2,1)S(1)}, u32[]{:S(2)}) copy-start(bf16[64,1024]{1,0:T(8,128)(2,1)S(1)} %collective-permute-done.2.refs_3_) | copy-start | bytes 393220
  31.0 1.5 copy-start.3
  32.6 27.0 %copy-start = (bf16[64,1024]{1,0:T(8,128)(2,1)S(1)}, bf16[64,1024]{1,0:T(8,128)(2,1)}, u32[]{:S(2)}) copy-start(bf16[64,1024]{1,0:T(8,128)(2,1)} %refs_0_.1) | copy-start | bytes 393220
  32.6 40.8 %all-to-all-start.1 = ((bf16[4,256,1024]{2,1,0:T(8,128)(2,1)}), bf16[4,256,1024]{2,1,0:T(8,128)(2,1)S(1)}, u32[]{:S(2)}, u32[]{:S(2)}) async-start(bf16[4,256,1024]{2,1,0:T(8,128)(2,1)} %copies.3), calls=%async_computation.1 | async-start | bytes 4194304 | tf_op jit(solution)/shard_map/all_to_all | solution.py:51
  36.8 22.8 %collective-permute-start.4 = (bf16[64,1024]{1,0:T(8,128)(2,1)S(1)}, bf16[64,1024]{1,0:T(8,128)(2,1)S(1)}, u32[]{:S(2)}, u32[]{:S(2)}) collective-permute-start(bf16[64,1024]{1,0:T(8,128)(2,1)S(1)} %collective-permute-done.refs_1_), channel_id=1, source_target_pairs={{0,4},{1,5},{2,6},{3,7},{4,8},{5,9},{6,10},{7,11},{8,12},{9,13},{1... | collective-permute-start | bytes 393224 | tf_op jit(solution)/shard_map/ppermute | solution.py:29
  41.9 17.6 %collective-permute-start.5 = (bf16[64,1024]{1,0:T(8,128)(2,1)S(1)}, bf16[64,1024]{1,0:T(8,128)(2,1)S(1)}, u32[]{:S(2)}, u32[]{:S(2)}) collective-permute-start(bf16[64,1024]{1,0:T(8,128)(2,1)S(1)} %collective-permute-done.1.refs_2_), channel_id=1, source_target_pairs={{0,12},{1,13},{2,14},{3,15},{4,0},{5,1},{6,2},{7,3},{8,4},{9,5},{1... | collective-permute-start | bytes 393224 | tf_op jit(solution)/shard_map/ppermute | solution.py:29
  44.6 10.9 %collective-permute-start.6 = (bf16[32,1024]{1,0:T(8,128)(2,1)S(1)}, bf16[32,1024]{1,0:T(8,128)(2,1)S(1)}, u32[]{:S(2)}, u32[]{:S(2)}) collective-permute-start(bf16[32,1024]{1,0:T(8,128)(2,1)S(1)} %slice.6), channel_id=1, source_target_pairs={{0,10},{1,11},{2,12},{3,13},{4,14},{5,15},{6,0},{7,1},{8,2},{9,3},... | collective-permute-start | bytes 196616 | tf_op jit(solution)/shard_map/ppermute | solution.py:29
  51.5 8.0 %collective-permute-start.7 = (bf16[32,1024]{1,0:T(8,128)(2,1)S(1)}, bf16[32,1024]{1,0:T(8,128)(2,1)S(1)}, u32[]{:S(2)}, u32[]{:S(2)}) collective-permute-start(bf16[32,1024]{1,0:T(8,128)(2,1)S(1)} %slice.7), channel_id=1, source_target_pairs={{0,6},{1,7},{2,8},{3,9},{4,10},{5,11},{6,12},{7,13},{8,14},{9,15},... | collective-permute-start | bytes 196616 | tf_op jit(solution)/shard_map/ppermute | solution.py:29
  59.5 0.9 copy-start.2
  60.4 0.9 copy-start.4
  62.8 8.8 %collective-permute-start.8 = (bf16[512,1024]{1,0:T(8,128)(2,1)S(1)}, bf16[512,1024]{1,0:T(8,128)(2,1)S(1)}, u32[]{:S(2)}, u32[]{:S(2)}) collective-permute-start(bf16[512,1024]{1,0:T(8,128)(2,1)S(1)} %assemble.1), channel_id=1, source_target_pairs={{0,1},{1,0},{2,3},{3,2},{4,5},{5,4},{6,7},{7,6},{8,9},{9,8},{10,11... | collective-permute-start | bytes 3145736 | tf_op jit(solution)/shard_map/ppermute | solution.py:29
  72.4 1.0 copy-start.6
  73.9 1.3 copy-start.7
  153.8 13.0 %all-to-all-start.7 = ((f32[32,8,128]{2,1,0:T(8,128)}), f32[32,8,128]{2,1,0:T(8,128)S(1)}, u32[]{:S(2)}, u32[]{:S(2)}) async-start(f32[32,8,128]{2,1,0:T(8,128)} %get-tuple-element.37), calls=%async_computation.7 | async-start | bytes 262144 | tf_op jit(solution)/shard_map/all_to_all | solution.py:289

commit v12 on v10

--- a/solution.py
+++ b/solution.py
@@ -271,10 +271,11 @@
     masses = core_first(source_logmass * LOG2E), (target_logmass * LOG2E).reshape(SMALL)
     mine, other, target, masses = gather_points(source_points, target_points, masses)
     source_mass, target_mass = masses
+    target, other, mine_sq = lax.optimization_barrier((target, other, squares(mine)))
     other, other_sq = place(other)
-    source_sq = jnp.concatenate([squares(mine), other_sq], axis=0)
+    target, target_sq = in_place_squares(target)
+    source_sq = jnp.concatenate([mine_sq, other_sq], axis=0)
     target, other, source_sq = lax.optimization_barrier((target, other, source_sq))
-    target, target_sq = in_place_squares(target)
     tiles = products(mine, target), products(other, target)
     (part,) = call(first_kernel, [(cols,) + SMALL], [WIDE], target_mass, target_sq, *tiles)
     for step in range(ITERS):

time: 161 us -> 161 us (level)
  no operation moved by 1% of the time
where the time goes in v12:
time: 161 us
  blocking collectives  63 us (39%)
  starting transfers between devices  45.6 us (28%)
  waiting for transfers between devices  29.3 us (18%)
  Pallas kernels  14.1 us (9%)
  local copies, waits for them, and re-layouts  3.4 us (2%)
  matrix products  2.57 us (2%)
  other arithmetic  1.72 us (1%)
    all_to_all x3, blocking collectives, local(): parts = lax.all_to_all(part, 'col', 0, 0)  37.1 us
    ppermute x7, starting transfers between devices, move_col(): return lax.ppermute(values, 'col', pairs)  26.7 us
    all_to_all x2, blocking collectives, local(): parts = lax.all_to_all(part, 'row', 0, 0)  25.9 us
    ppermute x7, waiting for transfers between devices, move_col(): return lax.ppermute(values, 'col', pairs)  15.5 us
    all_to_all x2, starting transfers between devices, spread(): out = lax.all_to_all(copies, 'row', 0, 0, axis_index_groups=lines)  15 us
    pallas_call x7, Pallas kernels, call(): pl.pallas_call(kernel, out_shape=[jax.ShapeDtypeStruct(shape, F32) for sh...  9.06 us
    all_to_all x1, waiting for transfers between devices, local(): parts = lax.all_to_all(part, 'row', 0, 0)  8.39 us
    all_to_all x2, waiting for transfers between devices, spread(): out = lax.all_to_all(copies, 'row', 0, 0, axis_index_groups=lines)  5.43 us
  transfers between devices with their start and end apart: 10, of which 6 were waited for; matrix products, arithmetic and copies ran while one was open for 2% of the time, Pallas kernels for 1%

profile of v12, /device:TPU:1, one launch (start us, length us, event | category | flops | bytes accessed | tf_op | source)
XLA Modules:
  0.0 160.5 jit_solution(9026399252245806528)
XLA Ops:
  0.6 0.8 copy-done.3
  1.5 0.9 copies.2
  2.3 10.9 %all-to-all-start = ((bf16[8,32,1024]{2,1,0:T(8,128)(2,1)}), bf16[8,32,1024]{2,1,0:T(8,128)(2,1)S(1)}, u32[]{:S(2)}, u32[]{:S(2)}) async-start(bf16[8,32,1024]{2,1,0:T(8,128)(2,1)} %copies.2), calls=%async_computation | async-start | bytes 1048576 | tf_op jit(solution)/shard_map/all_to_all | solution.py:51
  13.2 5.1 %collective-permute-start.1 = (bf16[64,1024]{1,0:T(8,128)(2,1)}, bf16[64,1024]{1,0:T(8,128)(2,1)S(1)}, u32[]{:S(2)}, u32[]{:S(2)}) collective-permute-start(bf16[64,1024]{1,0:T(8,128)(2,1)} %refs_0_.1), channel_id=1, source_target_pairs={{0,14},{1,15},{2,0},{3,1},{4,2},{5,3},{6,4},{7,5},{8,6},{9,7},{10,... | collective-permute-start | bytes 393224 | tf_op jit(solution)/shard_map/ppermute | solution.py:29
  18.3 1.9 %collective-permute-start = (bf16[64,1024]{1,0:T(8,128)(2,1)}, bf16[64,1024]{1,0:T(8,128)(2,1)S(1)}, u32[]{:S(2)}, u32[]{:S(2)}) collective-permute-start(bf16[64,1024]{1,0:T(8,128)(2,1)} %refs_0_.1), channel_id=1, source_target_pairs={{0,2},{1,3},{2,4},{3,5},{4,6},{5,7},{6,8},{7,9},{8,10},{9,11},{10,... | collective-permute-start | bytes 393224 | tf_op jit(solution)/shard_map/ppermute | solution.py:29
  20.2 0.7 broadcast_multiply_fusion
  20.9 0.1 reshape.32
  21.0 0.1 reshape.33.mass
  21.1 0.7 multiply_bitcast_fusion.mass
  21.8 4.0 %collective-permute-done.refs_1_ = bf16[64,1024]{1,0:T(8,128)(2,1)S(1)} collective-permute-done((bf16[64,1024]{1,0:T(8,128)(2,1)}, bf16[64,1024]{1,0:T(8,128)(2,1)S(1)}, u32[]{:S(2)}, u32[]{:S(2)}) %collective-permute-start) | collective-permute-done | bytes 131104 | tf_op jit(solution)/shard_map/ppermute | solution.py:29
  25.7 5.4 %all-to-all-done = bf16[8,32,1024]{2,1,0:T(8,128)(2,1)S(1)} async-done(((bf16[8,32,1024]{2,1,0:T(8,128)(2,1)}), bf16[8,32,1024]{2,1,0:T(8,128)(2,1)S(1)}, u32[]{:S(2)}, u32[]{:S(2)}) %all-to-all-start) | async-done | bytes 524320 | tf_op jit(solution)/shard_map/all_to_all | solution.py:51
  31.2 1.4 copies.3
  32.6 0.0 copy-start.2
  32.6 4.2 %all-to-all-start.1 = ((bf16[4,256,1024]{2,1,0:T(8,128)(2,1)}), bf16[4,256,1024]{2,1,0:T(8,128)(2,1)S(1)}, u32[]{:S(2)}, u32[]{:S(2)}) async-start(bf16[4,256,1024]{2,1,0:T(8,128)(2,1)} %copies.3), calls=%async_computation.1 | async-start | bytes 4194304 | tf_op jit(solution)/shard_map/all_to_all | solution.py:51
  36.8 5.9 %collective-permute-start.3 = (bf16[128,1024]{1,0:T(8,128)(2,1)S(1)}, bf16[128,1024]{1,0:T(8,128)(2,1)S(1)}, u32[]{:S(2)}, u32[]{:S(2)}) collective-permute-start(bf16[128,1024]{1,0:T(8,128)(2,1)S(1)} %get-tuple-element.40), channel_id=1, source_target_pairs={{0,12},{1,13},{2,14},{3,15},{4,0},{5,1},{6,2},{7,3},{8,4},{9,5},{1... | collective-permute-start | bytes 786440 | tf_op jit(solution)/shard_map/ppermute | solution.py:29
  42.7 1.9 %collective-permute-start.2 = (bf16[128,1024]{1,0:T(8,128)(2,1)S(1)}, bf16[128,1024]{1,0:T(8,128)(2,1)S(1)}, u32[]{:S(2)}, u32[]{:S(2)}) collective-permute-start(bf16[128,1024]{1,0:T(8,128)(2,1)S(1)} %get-tuple-element.41), channel_id=1, source_target_pairs={{0,4},{1,5},{2,6},{3,7},{4,8},{5,9},{6,10},{7,11},{8,12},{9,13},{1... | collective-permute-start | bytes 786440 | tf_op jit(solution)/shard_map/ppermute | solution.py:29
  44.6 5.0 %collective-permute-start.4 = (bf16[32,1024]{1,0:T(8,128)(2,1)S(1)}, bf16[32,1024]{1,0:T(8,128)(2,1)S(1)}, u32[]{:S(2)}, u32[]{:S(2)}) collective-permute-start(bf16[32,1024]{1,0:T(8,128)(2,1)S(1)} %slice.6), channel_id=1, source_target_pairs={{0,10},{1,11},{2,12},{3,13},{4,14},{5,15},{6,0},{7,1},{8,2},{9,3},... | collective-permute-start | bytes 196616 | tf_op jit(solution)/shard_map/ppermute | solution.py:29
  49.7 2.0 %collective-permute-start.5 = (bf16[32,1024]{1,0:T(8,128)(2,1)S(1)}, bf16[32,1024]{1,0:T(8,128)(2,1)S(1)}, u32[]{:S(2)}, u32[]{:S(2)}) collective-permute-start(bf16[32,1024]{1,0:T(8,128)(2,1)S(1)} %slice.7), channel_id=1, source_target_pairs={{0,6},{1,7},{2,8},{3,9},{4,10},{5,11},{6,12},{7,13},{8,14},{9,15},... | collective-permute-start | bytes 196616 | tf_op jit(solution)/shard_map/ppermute | solution.py:29
  51.7 6.5 %collective-permute-done.4.refs_5_ = bf16[32,1024]{1,0:T(8,128)(2,1)S(1)} collective-permute-done((bf16[32,1024]{1,0:T(8,128)(2,1)S(1)}, bf16[32,1024]{1,0:T(8,128)(2,1)S(1)}, u32[]{:S(2)}, u32[]{:S(2)}) %collective-permute-start.4) | collective-permute-done | bytes 65568 | tf_op jit(solution)/shard_map/ppermute | solution.py:29
  58.2 3.0 %collective-permute-done.5.refs_6_ = bf16[32,1024]{1,0:T(8,128)(2,1)S(1)} collective-permute-done((bf16[32,1024]{1,0:T(8,128)(2,1)S(1)}, bf16[32,1024]{1,0:T(8,128)(2,1)S(1)}, u32[]{:S(2)}, u32[]{:S(2)}) %collective-permute-start.5) | collective-permute-done | bytes 65568 | tf_op jit(solution)/shard_map/ppermute | solution.py:29
  61.2 0.0 collective-permute-done.3.refs_4_
  61.3 1.5 assemble.1
  62.7 4.8 %collective-permute-start.6 = (bf16[512,1024]{1,0:T(8,128)(2,1)S(1)}, bf16[512,1024]{1,0:T(8,128)(2,1)S(1)}, u32[]{:S(2)}, u32[]{:S(2)}) collective-permute-start(bf16[512,1024]{1,0:T(8,128)(2,1)S(1)} %assemble.1), channel_id=1, source_target_pairs={{0,1},{1,0},{2,3},{3,2},{4,5},{5,4},{6,7},{7,6},{8,9},{9,8},{10,11... | collective-permute-start | bytes 3145736 | tf_op jit(solution)/shard_map/ppermute | solution.py:29
  67.6 0.3 multiply_reduce_fusion
  67.8 2.0 %collective-permute-done.6.points = bf16[512,1024]{1,0:T(8,128)(2,1)S(1)} collective-permute-done((bf16[512,1024]{1,0:T(8,128)(2,1)S(1)}, bf16[512,1024]{1,0:T(8,128)(2,1)S(1)}, u32[]{:S(2)}, u32[]{:S(2)}) %collective-permute-start.6) | collective-permute-done | bytes 1048608 | tf_op jit(solution)/shard_map/ppermute | solution.py:29
  69.8 1.0 copy-done
  70.8 0.0 all-to-all-done.1
  70.8 0.6 in_place_squares.1
  71.4 0.7 copy-done.1
  72.0 0.8 place.1
  72.8 1.3 convolution_multiply_fusion.1.mine
  74.1 1.3 convolution_multiply_fusion.other
  75.4 1.2 first_kernel.1
  76.6 12.4 %all_to_all.40.parts = f32[16,8,128]{2,1,0:T(8,128)S(1)} all-to-all(f32[16,8,128]{2,1,0:T(8,128)S(1)} %first_kernel.1), channel_id=1, replica_groups=mesh['row'=32,'col'=16] {'col'}, dimensions={0} | all-to-all | bytes 131072 | tf_op jit(solution)/shard_map/all_to_all | solution.py:282
  89.0 1.6 target_kernel.3
  90.6 13.5 %all_to_all.41.parts = f32[32,8,128]{2,1,0:T(8,128)S(1)} all-to-all(f32[32,8,128]{2,1,0:T(8,128)S(1)} %get-tuple-element.36), channel_id=1, replica_groups=mesh['row'=32,'col'=16] {'row'}, dimensions={0} | all-to-all | bytes 262144 | tf_op jit(solution)/shard_map/all_to_all | solution.py:286
  104.1 1.2 source_kernel.2
  105.3 12.3 %all_to_all.42.parts = f32[16,8,128]{2,1,0:T(8,128)S(1)} all-to-all(f32[16,8,128]{2,1,0:T(8,128)S(1)} %source_kernel.2), channel_id=1, replica_groups=mesh['row'=32,'col'=16] {'col'}, dimensions={0} | all-to-all | bytes 131072 | tf_op jit(solution)/shard_map/all_to_all | solution.py:282
  117.6 1.6 target_kernel.4
  119.2 12.4 %all_to_all.43.parts = f32[32,8,128]{2,1,0:T(8,128)S(1)} all-to-all(f32[32,8,128]{2,1,0:T(8,128)S(1)} %get-tuple-element.37), channel_id=1, replica_groups=mesh['row'=32,'col'=16] {'row'}, dimensions={0} | all-to-all | bytes 262144 | tf_op jit(solution)/shard_map/all_to_all | solution.py:286
  131.6 1.2 source_kernel.3
  132.8 12.3 %all_to_all.44.parts = f32[16,8,128]{2,1,0:T(8,128)S(1)} all-to-all(f32[16,8,128]{2,1,0:T(8,128)S(1)} %source_kernel.3), channel_id=1, replica_groups=mesh['row'=32,'col'=16] {'col'}, dimensions={0} | all-to-all | bytes 131072 | tf_op jit(solution)/shard_map/all_to_all | solution.py:282
  145.2 1.7 %target_kernel.5 = (f32[32,8,128]{2,1,0:T(8,128)}, f32[8,128]{1,0:T(8,128)S(1)}) custom-call(f32[16,8,128]{2,1,0:T(8,128)S(1)} %all_to_all.44.parts, f32[8,128]{1,0:T(8,128)S(1)} %reshape.33.mass, f32[8,128]{1,0:T(8,128)S(1)} %pad_maximum_fusion.2.squares, f32[512,1024]{1,0:T(8,128)S(1)} %convolution_multiply_fusion.1.mine, ...), custom_call_target="tpu_custom_call" | custom-call | flops 6291456 | bytes 4194304 | tf_op jit(solution)/shard_map/target_kernel/pallas_call | solution.py:241
  146.9 3.9 %all-to-all-start.7 = ((f32[32,8,128]{2,1,0:T(8,128)}), f32[32,8,128]{2,1,0:T(8,128)S(1)}, u32[]{:S(2)}, u32[]{:S(2)}) async-start(f32[32,8,128]{2,1,0:T(8,128)} %get-tuple-element.39), calls=%async_computation.7 | async-start | bytes 262144 | tf_op jit(solution)/shard_map/all_to_all | solution.py:286
  150.7 0.1 reshape.37
  150.8 0.7 reshape.38
  151.5 8.4 %all-to-all-done.7.parts = f32[32,8,128]{2,1,0:T(8,128)S(1)} async-done(((f32[32,8,128]{2,1,0:T(8,128)}), f32[32,8,128]{2,1,0:T(8,128)S(1)}, u32[]{:S(2)}, u32[]{:S(2)}) %all-to-all-start.7) | async-done | bytes 131104 | tf_op jit(solution)/shard_map/all_to_all | solution.py:286
  159.9 0.7 last_kernel.1
  (12 shorter events, 0.1 us)
Async XLA Ops:
  0.6 0.8 copy-start.3
  2.3 28.8 %all-to-all-start = ((bf16[8,32,1024]{2,1,0:T(8,128)(2,1)}), bf16[8,32,1024]{2,1,0:T(8,128)(2,1)S(1)}, u32[]{:S(2)}, u32[]{:S(2)}) async-start(bf16[8,32,1024]{2,1,0:T(8,128)(2,1)} %copies.2), calls=%async_computation | async-start | bytes 1048576 | tf_op jit(solution)/shard_map/all_to_all | solution.py:51
  13.2 8.6 %collective-permute-start.1 = (bf16[64,1024]{1,0:T(8,128)(2,1)}, bf16[64,1024]{1,0:T(8,128)(2,1)S(1)}, u32[]{:S(2)}, u32[]{:S(2)}) collective-permute-start(bf16[64,1024]{1,0:T(8,128)(2,1)} %refs_0_.1), channel_id=1, source_target_pairs={{0,14},{1,15},{2,0},{3,1},{4,2},{5,3},{6,4},{7,5},{8,6},{9,7},{10,... | collective-permute-start | bytes 393224 | tf_op jit(solution)/shard_map/ppermute | solution.py:29
  18.3 7.4 %collective-permute-start = (bf16[64,1024]{1,0:T(8,128)(2,1)}, bf16[64,1024]{1,0:T(8,128)(2,1)S(1)}, u32[]{:S(2)}, u32[]{:S(2)}) collective-permute-start(bf16[64,1024]{1,0:T(8,128)(2,1)} %refs_0_.1), channel_id=1, source_target_pairs={{0,2},{1,3},{2,4},{3,5},{4,6},{5,7},{6,8},{7,9},{8,10},{9,11},{10,... | collective-permute-start | bytes 393224 | tf_op jit(solution)/shard_map/ppermute | solution.py:29
  32.6 4.2 %copy-start.2 = (bf16[64,1024]{1,0:T(8,128)(2,1)S(1)}, bf16[64,1024]{1,0:T(8,128)(2,1)}, u32[]{:S(2)}) copy-start(bf16[64,1024]{1,0:T(8,128)(2,1)} %refs_0_.1) | copy-start | bytes 393220
  32.6 38.2 %all-to-all-start.1 = ((bf16[4,256,1024]{2,1,0:T(8,128)(2,1)}), bf16[4,256,1024]{2,1,0:T(8,128)(2,1)S(1)}, u32[]{:S(2)}, u32[]{:S(2)}) async-start(bf16[4,256,1024]{2,1,0:T(8,128)(2,1)} %copies.3), calls=%async_computation.1 | async-start | bytes 4194304 | tf_op jit(solution)/shard_map/all_to_all | solution.py:51
  36.8 24.5 %collective-permute-start.3 = (bf16[128,1024]{1,0:T(8,128)(2,1)S(1)}, bf16[128,1024]{1,0:T(8,128)(2,1)S(1)}, u32[]{:S(2)}, u32[]{:S(2)}) collective-permute-start(bf16[128,1024]{1,0:T(8,128)(2,1)S(1)} %get-tuple-element.40), channel_id=1, source_target_pairs={{0,12},{1,13},{2,14},{3,15},{4,0},{5,1},{6,2},{7,3},{8,4},{9,5},{1... | collective-permute-start | bytes 786440 | tf_op jit(solution)/shard_map/ppermute | solution.py:29
  42.7 18.6 %collective-permute-start.2 = (bf16[128,1024]{1,0:T(8,128)(2,1)S(1)}, bf16[128,1024]{1,0:T(8,128)(2,1)S(1)}, u32[]{:S(2)}, u32[]{:S(2)}) collective-permute-start(bf16[128,1024]{1,0:T(8,128)(2,1)S(1)} %get-tuple-element.41), channel_id=1, source_target_pairs={{0,4},{1,5},{2,6},{3,7},{4,8},{5,9},{6,10},{7,11},{8,12},{9,13},{1... | collective-permute-start | bytes 786440 | tf_op jit(solution)/shard_map/ppermute | solution.py:29
  44.6 13.6 %collective-permute-start.4 = (bf16[32,1024]{1,0:T(8,128)(2,1)S(1)}, bf16[32,1024]{1,0:T(8,128)(2,1)S(1)}, u32[]{:S(2)}, u32[]{:S(2)}) collective-permute-start(bf16[32,1024]{1,0:T(8,128)(2,1)S(1)} %slice.6), channel_id=1, source_target_pairs={{0,10},{1,11},{2,12},{3,13},{4,14},{5,15},{6,0},{7,1},{8,2},{9,3},... | collective-permute-start | bytes 196616 | tf_op jit(solution)/shard_map/ppermute | solution.py:29
  49.7 11.6 %collective-permute-start.5 = (bf16[32,1024]{1,0:T(8,128)(2,1)S(1)}, bf16[32,1024]{1,0:T(8,128)(2,1)S(1)}, u32[]{:S(2)}, u32[]{:S(2)}) collective-permute-start(bf16[32,1024]{1,0:T(8,128)(2,1)S(1)} %slice.7), channel_id=1, source_target_pairs={{0,6},{1,7},{2,8},{3,9},{4,10},{5,11},{6,12},{7,13},{8,14},{9,15},... | collective-permute-start | bytes 196616 | tf_op jit(solution)/shard_map/ppermute | solution.py:29
  62.7 7.1 %collective-permute-start.6 = (bf16[512,1024]{1,0:T(8,128)(2,1)S(1)}, bf16[512,1024]{1,0:T(8,128)(2,1)S(1)}, u32[]{:S(2)}, u32[]{:S(2)}) collective-permute-start(bf16[512,1024]{1,0:T(8,128)(2,1)S(1)} %assemble.1), channel_id=1, source_target_pairs={{0,1},{1,0},{2,3},{3,2},{4,5},{5,4},{6,7},{7,6},{8,9},{9,8},{10,11... | collective-permute-start | bytes 3145736 | tf_op jit(solution)/shard_map/ppermute | solution.py:29
  69.8 1.0 copy-start
  70.8 1.2 copy-start.1
  146.9 13.0 %all-to-all-start.7 = ((f32[32,8,128]{2,1,0:T(8,128)}), f32[32,8,128]{2,1,0:T(8,128)S(1)}, u32[]{:S(2)}, u32[]{:S(2)}) async-start(f32[32,8,128]{2,1,0:T(8,128)} %get-tuple-element.39), calls=%async_computation.7 | async-start | bytes 262144 | tf_op jit(solution)/shard_map/all_to_all | solution.py:286
